TPU v7x, 128 devices: a whole 4x4x4 slice. The times are simulated.
128 devices in a mesh: orb: 64 (over z, y, x), grid: 2 (over core).
Axes of the slice: x: 4, y: 4, z: 4, core: 2. Of those that a mesh axis runs over, the one named last changes fastest.
Arguments:
- coefficients: bfloat16 [192, 128, 128, 128], P('orb', None, 'grid'), may hold values from -8 to 8
- occupations: int32 [192], replicated, may hold values from 0 to 2
- slot_orbital: int32 [192], replicated, may hold values from 0 to 191, each once
Outputs:
- updated: bfloat16 [192, 128, 128, 128], P('orb', None, 'grid')
- orbital_energies: float32 [192], P('orb')
- potential: float32 [128, 128, 128], P('orb', 'grid')
Inputs may be any that keep to these rules, and one draw needn't show every extreme that they name: `slot_orbital`: every orbital number appears once.
All inputs are finite; a program needn't handle non-finite values.
Results may differ from a plain program's by a relative error of at most 0.0008.
The roundings to bfloat16 on the way count: a program that leaves them out, or rounds other values in their place, can miss the bound.
Values may be sent and summed in bfloat16 or wider, within the bound.
No kernel may reach another device: no remote copies, remote signals or barrier semaphores. Data moves between devices by JAX's collectives and lax.ppermute only.
A program may use at most 192 MiB of HBM per device.

v0:
```python
import math

import jax
import jax.numpy as jnp
from jax import lax
from jax.sharding import PartitionSpec as P

MAGIC = (
    8.433424733352934e-07,
    -1.290557201342061e-05,
    8.76298447621056e-05,
    -0.00030158038132690465,
    0.001747237136729939,
    -0.009420470302010804,
    0.023738214637249424,
    0.0612625895831208,
    0.9940415697834004,
    -0.06048952891969835,
    -0.021030251609303816,
    0.013372634148547948,
    -0.0034412814449349387,
    0.0004944322768868992,
    -5.185986881173433e-05,
    2.7273449291197967e-06,
)
STEP_SIZE = 0.1
COULOMB = 4.0 * math.pi


def with_halo(cells, sides, width):
    for axis, dim in sides:
        count = lax.axis_size(axis)
        head = lax.slice_in_dim(cells, 0, width, axis=dim)
        tail = lax.slice_in_dim(cells, cells.shape[dim] - width, cells.shape[dim], axis=dim)
        cells = jnp.concatenate(
            [
                lax.ppermute(tail, axis, [(i, (i + 1) % count) for i in range(count)]),
                cells,
                lax.ppermute(head, axis, [((i + 1) % count, i) for i in range(count)]),
            ],
            axis=dim,
        )
    return cells


def magic_pairs():
    return [(position - 8, MAGIC[position]) for position in range(16)]


def transposed_pairs():
    return [(8 - position, MAGIC[position]) for position in range(16)]


def kinetic_pairs():
    spread = 14
    weights = []
    for distance in range(1, spread + 1):
        numerator = 2.0 * (-1.0) ** (distance + 1) * math.factorial(spread) ** 2
        weights.append(
            numerator
            / (
                distance
                * distance
                * math.factorial(spread - distance)
                * math.factorial(spread + distance)
            )
        )
    result = [(0, -2.0 * sum(weights))]
    for distance in range(1, spread + 1):
        result.append((distance, weights[distance - 1]))
        result.append((-distance, weights[distance - 1]))
    return result


def band_matrix(length_in, length_out, start_row, pairs, periodic):
    rows_in = lax.broadcasted_iota(jnp.int32, (length_in, length_out), 0)
    cols_out = lax.broadcasted_iota(jnp.int32, (length_in, length_out), 1)
    distance = rows_in - cols_out - start_row
    matrix = jnp.zeros((length_in, length_out), jnp.float32)
    for offset_cells, weight in pairs:
        rounded = jnp.asarray(weight, jnp.float32).astype(jnp.bfloat16).astype(jnp.float32)
        if periodic:
            matches = jnp.mod(distance - offset_cells, length_in) == 0
        else:
            matches = distance == offset_cells
        matrix = matrix + jnp.where(matches, rounded, jnp.float32(0.0))
    return matrix.astype(jnp.bfloat16)


def along_last(values, matrix):
    return jnp.dot(values, matrix, preferred_element_type=jnp.float32)


def along_depth(values, matrix):
    return jnp.einsum("ji,ojxy->oixy", matrix, values, preferred_element_type=jnp.float32)


def along_width(values, matrix):
    return jnp.einsum("ji,ozjy->oziy", matrix, values, preferred_element_type=jnp.float32)


def fourier_tables(length):
    first_index = lax.broadcasted_iota(jnp.int32, (length, length), 0)
    second_index = lax.broadcasted_iota(jnp.int32, (length, length), 1)
    angles = jnp.mod(first_index * second_index, length).astype(jnp.float32) * (
        2.0 * math.pi / length
    )
    return (jnp.cos(angles), jnp.sin(angles))


def depth_transform(values, matrix):
    return jnp.einsum("kz,zxy->kxy", matrix, values, precision=lax.Precision.HIGHEST)


def width_transform(values, matrix):
    return jnp.einsum("kx,zxy->zky", matrix, values, precision=lax.Precision.HIGHEST)


def coulomb_kernel(length, columns_dev, block_index):
    shape_all = (length, length, columns_dev)
    depth_wave = lax.broadcasted_iota(jnp.int32, shape_all, 0)
    width_wave = lax.broadcasted_iota(jnp.int32, shape_all, 1)
    column_wave = block_index * columns_dev + lax.broadcasted_iota(jnp.int32, shape_all, 2)

    def curve(waves):
        return 2.0 - 2.0 * jnp.cos(waves.astype(jnp.float32) * (2.0 * math.pi / length))

    summed = curve(depth_wave) + curve(width_wave) + curve(column_wave)
    anchor = (depth_wave == 0) & (width_wave == 0) & (column_wave == 0)
    return jnp.where(
        anchor, jnp.float32(0.0), COULOMB / jnp.where(anchor, jnp.float32(1.0), summed)
    )


def poisson(slab):
    gathered = lax.all_gather(slab, "grid", axis=1, tiled=True)
    length = gathered.shape[2]
    cosine, sine = fourier_tables(length)
    highest = lax.Precision.HIGHEST
    real_y = jnp.dot(gathered, cosine, precision=highest)
    imag_y = -jnp.dot(gathered, sine, precision=highest)
    real_x = width_transform(real_y, cosine) + width_transform(imag_y, sine)
    imag_x = width_transform(imag_y, cosine) - width_transform(real_y, sine)
    columns = lax.all_to_all(
        jnp.stack([real_x, imag_x]), "orb", split_axis=3, concat_axis=1, tiled=True
    )
    real_cols = columns[0]
    imag_cols = columns[1]
    real_z = depth_transform(real_cols, cosine) + depth_transform(imag_cols, sine)
    imag_z = depth_transform(imag_cols, cosine) - depth_transform(real_cols, sine)
    kernel = coulomb_kernel(length, real_z.shape[2], lax.axis_index("orb"))
    real_scaled = real_z * kernel
    imag_scaled = imag_z * kernel
    real_back = (depth_transform(real_scaled, cosine) - depth_transform(imag_scaled, sine)) / length
    imag_back = (depth_transform(imag_scaled, cosine) + depth_transform(real_scaled, sine)) / length
    slab_rows = lax.all_to_all(
        jnp.stack([real_back, imag_back]), "orb", split_axis=1, concat_axis=3, tiled=True
    )
    real_rows = (
        width_transform(slab_rows[0], cosine) - width_transform(slab_rows[1], sine)
    ) / length
    imag_rows = (
        width_transform(slab_rows[1], cosine) + width_transform(slab_rows[0], sine)
    ) / length
    return (
        jnp.dot(real_rows, cosine, precision=highest) - jnp.dot(imag_rows, sine, precision=highest)
    ) / length


def extended(full_slab, corner, ext_width):
    cells_x = full_slab.shape[1]
    tripled = jnp.concatenate([full_slab, full_slab, full_slab], axis=1)
    return lax.dynamic_slice_in_dim(tripled, cells_x + corner - 8, ext_width, 1)


def on_device(coefficients, occupations, slot_orbital):
    local_orbitals, depth_cells, half_width, length = coefficients.shape
    total_slots = slot_orbital.shape[0]
    margin = 22
    ext_width = half_width + 16
    wide_rows = half_width + 2 * margin
    padded = with_halo(coefficients, (("grid", 2),), margin)
    magic_line = band_matrix(length, length, 0, magic_pairs(), True)
    magic_cross = band_matrix(wide_rows, ext_width, margin - 8, magic_pairs(), False)
    mag_y = along_last(padded, magic_line).astype(jnp.bfloat16)
    mag_yx = along_width(mag_y, magic_cross).astype(jnp.bfloat16)
    psi_ext = along_depth(mag_yx, magic_line).astype(jnp.bfloat16)
    kinetic_line = band_matrix(length, length, 0, kinetic_pairs(), True)
    kinetic_cross = band_matrix(wide_rows, half_width, margin, kinetic_pairs(), False)
    second = (
        along_last(coefficients, kinetic_line)
        + along_depth(coefficients, kinetic_line)
        + along_width(padded, kinetic_cross)
    )
    catalog = lax.broadcasted_iota(jnp.int32, (total_slots, total_slots), 1)
    occupancy = jnp.sum(
        jnp.where(slot_orbital[:, None] == catalog, occupations[None, :], 0), axis=1
    )
    all_weights = occupancy.astype(jnp.float32) / total_slots
    corner = lax.axis_index("grid") * half_width
    slabs = lax.all_to_all(psi_ext, "orb", split_axis=1, concat_axis=0, tiled=True)
    own_slabs = slabs[:, :, 8 : 8 + half_width, :].astype(jnp.float32)
    density = jnp.sum(all_weights[:, None, None, None] * own_slabs * own_slabs, axis=0)
    full_slab = poisson(density)
    field_ext = extended(full_slab, corner, ext_width)
    slab_product = (field_ext[None] * slabs.astype(jnp.float32)).astype(jnp.bfloat16)
    product = lax.all_to_all(slab_product, "orb", split_axis=0, concat_axis=1, tiled=True)
    trans_line = band_matrix(length, length, 0, transposed_pairs(), True)
    trans_cross = band_matrix(ext_width, half_width, 8, transposed_pairs(), False)
    back_z = along_depth(product, trans_line).astype(jnp.bfloat16)
    back_zx = along_width(back_z, trans_cross).astype(jnp.bfloat16)
    applied = -0.5 * second + along_last(back_zx, trans_line)
    coeff_wide = coefficients.astype(jnp.float32)
    numerator = jnp.sum(coeff_wide * applied, axis=(1, 2, 3))
    norm_sums = jnp.sum(coeff_wide * coeff_wide, axis=(1, 2, 3))
    numerator, norm_sums = lax.psum((numerator, norm_sums), "grid")
    energies = numerator / norm_sums
    updated = (
        coeff_wide - STEP_SIZE * (applied - energies[:, None, None, None] * coeff_wide)
    ).astype(jnp.bfloat16)
    potential = lax.dynamic_slice_in_dim(full_slab, corner, half_width, 1)
    return (updated, energies, potential)


def solution(mesh):
    return jax.shard_map(
        on_device,
        mesh=mesh,
        in_specs=(P("orb", None, "grid", None), P(), P()),
        out_specs=(P("orb", None, "grid", None), P("orb"), P("orb", "grid", None)),
        check_vma=False,
    )
```

profile of v0, /device:TPU:1, one launch (start us, length us, event | category | flops | bytes accessed | tf_op | source)
XLA Modules:
  0.0 432.3 jit_solution(4209746294255295311)
XLA Ops:
  0.6 3.6 fusion.569
  4.2 0.5 copy.124
  4.7 1.5 collective-permute-start.1
  6.2 0.5 copy.123
  7.1 3.1 collective-permute-done.1
  10.1 1.4 copy.84
  11.6 1.7 collective-permute-done
  13.2 2.9 copy.83
  16.1 11.5 %convert_bitcast_fusion.2 = bf16[3,128,80,128]{3,2,1,0:T(8,128)(2,1)} fusion(bf16[3,128,22,128]{3,2,1,0:T(8,128)(2,1)S(1)} %copy.84, bf16[3,128,64,128]{3,2,1,0:T(8,128)(2,1)} %param.3, bf16[3,128,22,128]{3,2,1,0:T(8,128)(2,1)} %copy.83), kind=kOutput, calls=%fused_computation.26 | convolution fusion | flops 2253756416 | bytes 18481152 | tf_op jit(solution)/shard_map/ji,ozjy->oziy/dot_general | solution.py:99
  27.6 9.0 %convert_bitcast_fusion.1 = bf16[3,128,80,128]{1,3,2,0:T(8,128)(2,1)} fusion(bf16[3,128,80,128]{3,2,1,0:T(8,128)(2,1)} %convert_bitcast_fusion.2), kind=kOutput, calls=%fused_computation.25 | convolution fusion | flops 1014497280 | bytes 15728640 | tf_op jit(solution)/shard_map/ji,ojxy->oixy/dot_general | solution.py:95
  36.6 11.0 %copy.87 = bf16[3,128,80,128]{3,2,0,1:T(8,128)(2,1)} copy(bf16[3,128,80,128]{1,3,2,0:T(8,128)(2,1)} %convert_bitcast_fusion.1) | data formatting | bytes 15728640 | tf_op jit(solution)/shard_map/convert_element_type | solution.py:187
  47.7 12.0 %all-to-all-start = ((bf16[3,128,80,128]{3,2,0,1:T(8,128)(2,1)}), bf16[3,128,80,128]{3,2,0,1:T(8,128)(2,1)}, u32[]{:S(2)}, u32[]{:S(2)}) async-start(bf16[3,128,80,128]{3,2,0,1:T(8,128)(2,1)} %copy.87), calls=%async_computation | async-start | bytes 15728640 | tf_op jit(solution)/shard_map/all_to_all | solution.py:201
  59.9 110.9 %all-to-all-done = bf16[3,128,80,128]{3,2,0,1:T(8,128)(2,1)} async-done(((bf16[3,128,80,128]{3,2,0,1:T(8,128)(2,1)}), bf16[3,128,80,128]{3,2,0,1:T(8,128)(2,1)}, u32[]{:S(2)}, u32[]{:S(2)}) %all-to-all-start) | async-done | bytes 7864352 | tf_op jit(solution)/shard_map/all_to_all | solution.py:201
  170.8 4.6 %copy.89 = bf16[64,3,2,80,128]{4,3,2,1,0:T(8,128)(2,1)S(1)} copy(bf16[64,3,2,80,128]{4,3,1,2,0:T(8,128)(2,1)} %bitcast.16) | data formatting | bytes 15728640 | tf_op jit(solution)/shard_map/all_to_all | solution.py:201
  175.4 3.0 copy-done.1
  178.4 2.2 fusion
  180.6 3.1 all_gather.3
  184.3 0.5 fusion.145
  185.3 0.5 fusion.141
  185.9 0.6 fusion.26
  187.0 0.9 copy.94
  187.9 9.7 %all-to-all-start.1 = ((f32[2,2,128,128]{2,1,0,3:T(2,128)}), f32[2,2,128,128]{2,1,0,3:T(2,128)S(1)}, u32[]{:S(2)}, u32[]{:S(2)}) async-start(f32[2,2,128,128]{2,1,0,3:T(2,128)} %copy.94), calls=%async_computation.1 | async-start | bytes 524288 | tf_op jit(solution)/shard_map/all_to_all | solution.py:144
  197.7 9.9 %all-to-all-done.1 = f32[2,2,128,128]{2,1,0,3:T(2,128)S(1)} async-done(((f32[2,2,128,128]{2,1,0,3:T(2,128)}), f32[2,2,128,128]{2,1,0,3:T(2,128)S(1)}, u32[]{:S(2)}, u32[]{:S(2)}) %all-to-all-start.1) | async-done | bytes 262176 | tf_op jit(solution)/shard_map/all_to_all | solution.py:144
  211.9 0.9 copy.96
  212.8 4.6 %all-to-all-start.2 = ((f32[2,128,128,2]{2,3,0,1:T(2,128)}), f32[2,128,128,2]{2,3,0,1:T(2,128)S(1)}, u32[]{:S(2)}, u32[]{:S(2)}) async-start(f32[2,128,128,2]{2,3,0,1:T(2,128)} %copy.96), calls=%async_computation.2 | async-start | bytes 524288 | tf_op jit(solution)/shard_map/all_to_all | solution.py:156
  217.4 9.5 %all-to-all-done.2 = f32[2,128,128,2]{2,3,0,1:T(2,128)S(1)} async-done(((f32[2,128,128,2]{2,3,0,1:T(2,128)}), f32[2,128,128,2]{2,3,0,1:T(2,128)S(1)}, u32[]{:S(2)}, u32[]{:S(2)}) %all-to-all-start.2) | async-done | bytes 262176 | tf_op jit(solution)/shard_map/all_to_all | solution.py:156
  228.1 0.5 fusion.34
  228.6 0.5 fusion.36
  229.1 0.6 fusion.129
  229.7 0.6 fusion.37
  230.3 7.8 %multiply_convert_fusion = bf16[192,2,80,128]{3,2,1,0:T(8,128)(2,1)} fusion(f32[2,80,128]{2,1,0:T(8,128)S(1)} %fusion.39, bf16[64,3,2,80,128]{4,3,2,1,0:T(8,128)(2,1)} %copy-done.1), kind=kLoop, calls=%fused_computation.5 | loop fusion | flops 11796480 | bytes 15810560 | tf_op jit(solution)/shard_map/convert_element_type | solution.py:206
  238.1 5.9 %all-to-all-start.3 = ((bf16[192,2,80,128]{3,2,1,0:T(8,128)(2,1)}), bf16[192,2,80,128]{3,2,1,0:T(8,128)(2,1)}, u32[]{:S(2)}, u32[]{:S(2)}) async-start(bf16[192,2,80,128]{3,2,1,0:T(8,128)(2,1)} %multiply_convert_fusion), calls=%async_computation.3 | async-start | bytes 15728640 | tf_op jit(solution)/shard_map/all_to_all | solution.py:207
  244.0 9.3 %copy.75 = bf16[3,128,64,128]{1,3,2,0:T(8,128)(2,1)} copy(bf16[3,128,64,128]{3,2,1,0:T(8,128)(2,1)} %param.3) | data formatting | bytes 12582912 | tf_op args[0]
  253.3 10.1 %fusion.174 = f32[128,3,64,128]{0,3,2,1:T(8,128)} fusion(bf16[3,128,64,128]{1,3,2,0:T(8,128)(2,1)} %copy.75), kind=kOutput, calls=%fused_computation.295 | convolution fusion | flops 812433408 | bytes 18874368 | tf_op jit(solution)/shard_map/ji,ojxy->oixy/dot_general | solution.py:95
  263.4 7.2 %fusion.176 = f32[128,3,128,64]{2,0,3,1:T(8,128)} fusion(bf16[3,128,64,128]{1,3,2,0:T(8,128)(2,1)S(1)} %copy-done), kind=kOutput, calls=%fused_computation.297 | convolution fusion | flops 812433408 | bytes 18874368 | tf_op jit(solution)/shard_map/dot_general | solution.py:91
  270.6 7.1 %fusion.24 = f32[3,128,128,64]{2,3,1,0:T(8,128)} fusion(bf16[3,128,22,128]{3,2,1,0:T(8,128)(2,1)S(1)} %copy-done.3, bf16[3,128,64,128]{3,2,1,0:T(8,128)(2,1)S(1)} %bitcast.165, bf16[3,128,22,128]{3,2,1,0:T(8,128)(2,1)S(1)} %copy-done.4), kind=kOutput, calls=%fused_computation.30 | convolution fusion | flops 711942912 | bytes 23199744 | tf_op jit(solution)/shard_map/ji,ozjy->oziy/dot_general | solution.py:99
  277.7 12.6 %copy.85 = f32[3,128,128,64]{1,2,3,0:T(8,128)} copy(f32[3,128,128,64]{2,3,1,0:T(8,128)} %fusion.24) | data formatting | bytes 25165824 | tf_op jit(solution)/shard_map/ji,ozjy->oziy/dot_general | solution.py:99
  290.3 0.6 constant_dynamic-slice_fusion
  291.0 50.5 %all-to-all-done.3 = bf16[192,2,80,128]{3,2,1,0:T(8,128)(2,1)} async-done(((bf16[192,2,80,128]{3,2,1,0:T(8,128)(2,1)}), bf16[192,2,80,128]{3,2,1,0:T(8,128)(2,1)}, u32[]{:S(2)}, u32[]{:S(2)}) %all-to-all-start.3) | async-done | bytes 7864352 | tf_op jit(solution)/shard_map/all_to_all | solution.py:207
  341.5 4.6 %copy.100 = bf16[64,3,2,80,128]{4,3,2,0,1:T(8,128)(2,1)S(1)} copy(bf16[64,3,2,80,128]{4,3,2,1,0:T(8,128)(2,1)} %bitcast.35) | data formatting | bytes 15728640 | tf_op jit(solution)/shard_map/all_to_all | solution.py:207
  346.1 7.9 %convert_bitcast_fusion = bf16[3,128,80,128]{1,3,2,0:T(8,128)(2,1)} fusion(bf16[3,128,80,128]{3,2,1,0:T(8,128)(2,1)S(1)} %bitcast.166), kind=kOutput, calls=%fused_computation.24 | convolution fusion | flops 1014497280 | bytes 15728640 | tf_op jit(solution)/shard_map/ji,ojxy->oixy/dot_general | solution.py:95
  354.0 11.1 %copy.102 = bf16[3,128,80,128]{3,2,1,0:T(8,128)(2,1)} copy(bf16[3,128,80,128]{1,3,2,0:T(8,128)(2,1)} %convert_bitcast_fusion) | data formatting | bytes 15728640 | tf_op jit(solution)/shard_map/convert_element_type | solution.py:210
  365.1 5.2 %convert_bitcast_fusion.3 = bf16[3,128,64,128]{3,2,1,0:T(8,128)(2,1)S(1)} fusion(bf16[3,128,80,128]{3,2,1,0:T(8,128)(2,1)} %copy.102), kind=kOutput, calls=%fused_computation.29 | convolution fusion | flops 506718208 | bytes 14155776 | tf_op jit(solution)/shard_map/ji,ozjy->oziy/dot_general | solution.py:99
  370.4 9.7 %fusion.16 = f32[3,128,64,128]{1,3,2,0:T(8,128)} fusion(bf16[3,128,64,128]{3,2,1,0:T(8,128)(2,1)S(1)} %convert_bitcast_fusion.3), kind=kOutput, calls=%fused_computation.27 | convolution fusion | flops 809238528 | bytes 18874368 | tf_op jit(solution)/shard_map/dot_general | solution.py:91
  380.0 23.5 %fusion.2 = (f32[3]{0:T(128)S(1)}, f32[3]{0:T(128)S(1)}, f32[3,128,64,128]{1,3,2,0:T(8,128)}) fusion(bf16[3,128,64,128]{1,3,2,0:T(8,128)(2,1)S(1)} %bitcast.162, f32[3,128,64,128]{1,3,2,0:T(8,128)} %fusion.16, f32[3,128,128,64]{1,2,3,0:T(8,128)} %copy.85, f32[128,3,64,128]{0,3,2,1:T(8,128)} %fusion.174, f32[128,3,128,64]{2,0,3,1:T(8,128)} %fusion.176), kind=kLoop, calls=%fused_computation.8 | loop fusion | flops 28311544 | bytes 69206040 | tf_op jit(solution)/shard_map/reduce_sum | solution.py:215
  403.5 7.2 %all-reduce = (f32[3]{0:T(128)S(1)}, f32[3]{0:T(128)S(1)}) all-reduce(f32[3]{0:T(128)S(1)} %get-tuple-element.16, f32[3]{0:T(128)S(1)} %get-tuple-element.15), channel_id=1, replica_groups=mesh['orb'=64,'grid'=2] {'grid'}, use_global_device_ids=true, to_apply=%region_3.4 | all-reduce | flops 6 | bytes 48 | tf_op jit(solution)/shard_map/psum | solution.py:216
  410.7 12.3 %fusion.5 = bf16[3,128,64,128]{1,3,2,0:T(8,128)(2,1)} fusion(f32[3,128,64,128]{1,3,2,0:T(8,128)} %get-tuple-element.19, bf16[3,128,64,128]{1,3,2,0:T(8,128)(2,1)} %copy.75, f32[3]{0:T(128)S(1)} %div.45), kind=kLoop, calls=%fused_computation.11 | loop fusion | flops 18874368 | bytes 25165836 | tf_op jit(solution)/shard_map/convert_element_type | solution.py:220
  423.1 9.0 %copy.105 = bf16[3,128,64,128]{3,2,1,0:T(8,128)(2,1)} copy(bf16[3,128,64,128]{1,3,2,0:T(8,128)(2,1)} %fusion.5) | data formatting | bytes 12582912
  (53 shorter events, 7.6 us)
Async XLA Ops:
  4.7 5.4 %collective-permute-start.1 = (bf16[3,128,22,128]{3,1,2,0:T(8,128)(2,1)S(1)}, bf16[3,128,22,128]{3,1,2,0:T(8,128)(2,1)S(1)}, u32[]{:S(2)}, u32[]{:S(2)}) collective-permute-start(bf16[3,128,22,128]{3,1,2,0:T(8,128)(2,1)S(1)} %copy.124), channel_id=1, source_target_pairs={{1,0},{0,1},{3,2},{2,3},{5,4},{4,5},{7,6},{6,7},{9,8},{8,9},{11,10... | collective-permute-start | bytes 6488072 | tf_op jit(solution)/shard_map/ppermute | solution.py:39
  6.8 6.4 %collective-permute-start = (bf16[3,128,22,128]{3,1,2,0:T(8,128)(2,1)S(1)}, bf16[3,128,22,128]{3,1,2,0:T(8,128)(2,1)S(1)}, u32[]{:S(2)}, u32[]{:S(2)}) collective-permute-start(bf16[3,128,22,128]{3,1,2,0:T(8,128)(2,1)S(1)} %copy.123), channel_id=1, source_target_pairs={{0,1},{1,0},{2,3},{3,2},{4,5},{5,4},{6,7},{7,6},{8,9},{9,8},{10,11... | collective-permute-start | bytes 6488072 | tf_op jit(solution)/shard_map/ppermute | solution.py:37
  11.5 16.0 %copy-start.2 = (bf16[3,128,22,128]{3,2,1,0:T(8,128)(2,1)}, bf16[3,128,22,128]{3,2,1,0:T(8,128)(2,1)S(1)}, u32[]{:S(2)}) copy-start(bf16[3,128,22,128]{3,2,1,0:T(8,128)(2,1)S(1)} %copy.84) | copy-start | bytes 6488068
  47.6 12.0 %copy-start.5 = (s32[192]{0:T(256)S(1)}, s32[192]{0:T(256)}, u32[]{:S(2)}) copy-start(s32[192]{0:T(256)} %param.4) | copy-start | bytes 2308
  47.6 12.1 %copy-start.6 = (s32[192]{0:T(256)S(1)}, s32[192]{0:T(256)}, u32[]{:S(2)}) copy-start(s32[192]{0:T(256)} %param.5) | copy-start | bytes 2308
  47.7 123.1 %all-to-all-start = ((bf16[3,128,80,128]{3,2,0,1:T(8,128)(2,1)}), bf16[3,128,80,128]{3,2,0,1:T(8,128)(2,1)}, u32[]{:S(2)}, u32[]{:S(2)}) async-start(bf16[3,128,80,128]{3,2,0,1:T(8,128)(2,1)} %copy.87), calls=%async_computation | async-start | bytes 15728640 | tf_op jit(solution)/shard_map/all_to_all | solution.py:201
  175.4 3.1 copy-start.1
  187.9 19.7 %all-to-all-start.1 = ((f32[2,2,128,128]{2,1,0,3:T(2,128)}), f32[2,2,128,128]{2,1,0,3:T(2,128)S(1)}, u32[]{:S(2)}, u32[]{:S(2)}) async-start(f32[2,2,128,128]{2,1,0,3:T(2,128)} %copy.94), calls=%async_computation.1 | async-start | bytes 524288 | tf_op jit(solution)/shard_map/all_to_all | solution.py:144
  212.8 14.1 %all-to-all-start.2 = ((f32[2,128,128,2]{2,3,0,1:T(2,128)}), f32[2,128,128,2]{2,3,0,1:T(2,128)S(1)}, u32[]{:S(2)}, u32[]{:S(2)}) async-start(f32[2,128,128,2]{2,3,0,1:T(2,128)} %copy.96), calls=%async_computation.2 | async-start | bytes 524288 | tf_op jit(solution)/shard_map/all_to_all | solution.py:156
  238.1 103.4 %all-to-all-start.3 = ((bf16[192,2,80,128]{3,2,1,0:T(8,128)(2,1)}), bf16[192,2,80,128]{3,2,1,0:T(8,128)(2,1)}, u32[]{:S(2)}, u32[]{:S(2)}) async-start(bf16[192,2,80,128]{3,2,1,0:T(8,128)(2,1)} %multiply_convert_fusion), calls=%async_computation.3 | async-start | bytes 15728640 | tf_op jit(solution)/shard_map/all_to_all | solution.py:207
  244.0 26.6 %slice-start.2 = ((s8[6291456]{0:T(1024)(128)(4,1)}), s8[2097152]{0:T(1024)(128)(4,1)S(1)}, s32[]{:S(2)}) async-start(s8[6291456]{0:T(1024)(128)(4,1)} %bitcast.164), calls=%async_computation.6 | async-start | bytes 4194304
  253.3 10.1 %copy-start = (bf16[3,128,64,128]{1,3,2,0:T(8,128)(2,1)S(1)}, bf16[3,128,64,128]{1,3,2,0:T(8,128)(2,1)}, u32[]{:S(2)}) copy-start(bf16[3,128,64,128]{1,3,2,0:T(8,128)(2,1)} %copy.75) | copy-start | bytes 18874372
  253.3 17.4 %slice-start.3 = ((s8[6291456]{0:T(1024)(128)(4,1)}), s8[4194304]{0:T(1024)(128)(4,1)S(1)}, s32[]{:S(2)}) async-start(s8[6291456]{0:T(1024)(128)(4,1)} %bitcast.164), calls=%async_computation.7 | async-start | bytes 8388608
  263.4 7.2 %copy-start.3 = (bf16[3,128,22,128]{3,2,1,0:T(8,128)(2,1)S(1)}, bf16[3,128,22,128]{3,2,1,0:T(8,128)(2,1)}, u32[]{:S(2)}) copy-start(bf16[3,128,22,128]{3,2,1,0:T(8,128)(2,1)} %copy-done.2) | copy-start | bytes 6488068
  263.4 7.2 %copy-start.4 = (bf16[3,128,22,128]{3,2,1,0:T(8,128)(2,1)S(1)}, bf16[3,128,22,128]{3,2,1,0:T(8,128)(2,1)}, u32[]{:S(2)}) copy-start(bf16[3,128,22,128]{3,2,1,0:T(8,128)(2,1)} %copy.83) | copy-start | bytes 6488068
  365.1 14.9 %slice-start = ((s8[6291456]{0:T(1024)(128)(4,1)}), s8[4194304]{0:T(1024)(128)(4,1)S(1)}, s32[]{:S(2)}) async-start(s8[6291456]{0:T(1024)(128)(4,1)} %bitcast.161), calls=%async_computation.4 | async-start | bytes 8388608
  370.3 9.7 %slice-start.1 = ((s8[6291456]{0:T(1024)(128)(4,1)}), s8[2097152]{0:T(1024)(128)(4,1)S(1)}, s32[]{:S(2)}) async-start(s8[6291456]{0:T(1024)(128)(4,1)} %bitcast.161), calls=%async_computation.5 | async-start | bytes 4194304
  410.7 12.3 %copy-start.7 = (f32[3]{0:T(128)}, f32[3]{0:T(128)S(1)}, u32[]{:S(2)}) copy-start(f32[3]{0:T(128)S(1)} %div.45) | copy-start | bytes 40
where the time goes:
time: 439 us; the launch traced here: 432 us
  waiting for transfers between devices  186 us (42%)
  matrix products  78.1 us (18%)
  local copies, waits for them, and re-layouts  76.8 us (17%)
  other arithmetic  46.2 us (11%)
  starting transfers between devices  34 us (8%)
  blocking collectives  10.3 us (2%)
    all_to_all x1, waiting for transfers between devices, on_device(): lax.all_to_all(psi_ext, 'orb', split_axis=1, concat_axis=0, tiled=True)  111 us
    all_to_all x1, waiting for transfers between devices, on_device(): lax.all_to_all(slab_product, 'orb', split_axis=0, concat_axis=1, tiled=True)  50.5 us
    dot_general x3, matrix products, along_depth(): jnp.einsum('ji,ojxy->oixy', matrix, values, preferred_element_type=jnp.fl...  27.1 us
    dot_general x3, matrix products, along_width(): jnp.einsum('ji,ozjy->oziy', matrix, values, preferred_element_type=jnp.fl...  23.7 us
    reduce_sum x1, other arithmetic, on_device(): norm_sums = jnp.sum(coeff_wide * coeff_wide, axis=(1, 2, 3))  23.5 us
    unnamed x28, local copies, waits for them, and re-layouts  22.4 us
    dot_general x2, matrix products, along_last(): return jnp.dot(values, matrix, preferred_element_type=jnp.float32)  16.9 us
    dot_general x1, local copies, waits for them, and re-layouts, along_width(): jnp.einsum('ji,ozjy->oziy', matrix, values, preferred_element_type=jnp.fl...  12.6 us
  transfers between devices with their start and end apart: 6, of which 6 were waited for; matrix products, arithmetic and copies ran while one was open for 11% of the time, Pallas kernels for 0%

commit v1 on v0

v1 whole, which is shorter than its diff:
```python
import functools
import math

import jax
import jax.numpy as jnp
import ml_dtypes
import numpy as np
from jax import lax
from jax.experimental import pallas as pl
from jax.experimental.pallas import tpu as pltpu
from jax.sharding import PartitionSpec as P

MAGIC = (
    8.433424733352934e-07,
    -1.290557201342061e-05,
    8.76298447621056e-05,
    -0.00030158038132690465,
    0.001747237136729939,
    -0.009420470302010804,
    0.023738214637249424,
    0.0612625895831208,
    0.9940415697834004,
    -0.06048952891969835,
    -0.021030251609303816,
    0.013372634148547948,
    -0.0034412814449349387,
    0.0004944322768868992,
    -5.185986881173433e-05,
    2.7273449291197967e-06,
)
STEP_SIZE = 0.1
COULOMB = 4.0 * math.pi
LEVELS = 32000.0
FINE = 16384.0
F32 = jnp.float32
BF16 = jnp.bfloat16
HIGHEST = lax.Precision.HIGHEST
VMEM_LIMIT = 56 * 1024 * 1024


def magic_pairs():
    return [(position - 8, MAGIC[position]) for position in range(16)]


def transposed_pairs():
    return [(8 - position, MAGIC[position]) for position in range(16)]


def kinetic_pairs():
    spread = 14
    weights = []
    for distance in range(1, spread + 1):
        numerator = 2.0 * (-1.0) ** (distance + 1) * math.factorial(spread) ** 2
        weights.append(
            numerator
            / (
                distance
                * distance
                * math.factorial(spread - distance)
                * math.factorial(spread + distance)
            )
        )
    result = [(0, -2.0 * sum(weights))]
    for distance in range(1, spread + 1):
        result.append((distance, weights[distance - 1]))
        result.append((-distance, weights[distance - 1]))
    return result


def rounded(weight):
    return np.float32(np.float32(weight).astype(ml_dtypes.bfloat16))


def band_periodic(length, pairs, scale=1.0):
    matrix = np.zeros((length, length), np.float32)
    for offset, weight in pairs:
        for i in range(length):
            matrix[i, (i + offset) % length] += scale * rounded(weight)
    return matrix.astype(ml_dtypes.bfloat16)


def band_open(length, margin, pairs, scale=1.0):
    matrix = np.zeros((length, length + 2 * margin), np.float32)
    for offset, weight in pairs:
        for i in range(length):
            matrix[i, i + offset + margin] += scale * rounded(weight)
    return matrix.astype(ml_dtypes.bfloat16)


def hartley(length):
    index = np.arange(length)
    angle = 2.0 * np.pi * ((index[:, None] * index[None, :]) % length) / length
    return ((np.cos(angle) + np.sin(angle)) / math.sqrt(length)).astype(np.float32)


def curve(length):
    return 2.0 - 2.0 * np.cos(2.0 * np.pi * np.arange(length) / length)


def dot(a, b):
    return jnp.dot(a, b, preferred_element_type=F32)


def dot_exact(a, b):
    return jnp.dot(a, b, preferred_element_type=F32, precision=HIGHEST)


def params(count):
    return pltpu.CompilerParams(
        dimension_semantics=("arbitrary",) * count, vmem_limit_bytes=VMEM_LIMIT
    )


def whole(array):
    zeros = (0,) * array.ndim
    return pl.BlockSpec(array.shape, lambda *_: zeros)


def scale_of(largest):
    largest = jnp.maximum(largest, 1e-30)
    code = jnp.ceil(jnp.log2(largest))
    power = jnp.exp2(code)
    units = jnp.ceil(largest / power * FINE) + 1.0
    return code, units, units * (1.0 / FINE) * power


def coded_rows(cells_y, codes):
    row = lax.broadcasted_iota(jnp.int32, (16, cells_y), 0)
    values = jnp.zeros((16, cells_y), F32)
    for k, code in enumerate(codes):
        values = jnp.where(row == k, code, values)
    return values.astype(jnp.int32).astype(jnp.int16)


def density_kernel(
    occ_ref, slot_ref, c_ref, h_ref, my_ref, ax_ref, mz_ref, dht_ref, psi_ref, q_ref, mid, dens
):
    orbital = pl.program_id(0)
    chunk = pl.program_id(1)
    orbitals = pl.num_programs(0)
    chunks = pl.num_programs(1)
    cells_z, cells_x, cells_y = c_ref.shape[1], c_ref.shape[2], c_ref.shape[3]
    length = cells_z * chunks
    block = 8
    first = lax.axis_index("orb") * orbitals
    weight = occ_ref[slot_ref[first + orbital]].astype(F32) / slot_ref.shape[0]
    my = my_ref[...]
    ax = ax_ref[...]
    mz = mz_ref[...]

    def planes(i, carry):
        z0 = i * block
        ext = jnp.concatenate(
            [
                h_ref[0, pl.ds(z0, block), 0:16, :],
                c_ref[0, pl.ds(z0, block)],
                h_ref[0, pl.ds(z0, block), 16:32, :],
            ],
            axis=1,
        )
        wide = ext.shape[1]
        mag_y = dot(ext.reshape(block * wide, cells_y), my).astype(BF16)
        mag_y = mag_y.reshape(block, wide, cells_y)
        for p in range(0, block, 2):
            both = dot(ax, jnp.concatenate([mag_y[p], mag_y[p + 1]], axis=1))
            row = (chunk * cells_z + z0 + p) * cells_x
            mid[pl.ds(pl.multiple_of(row, cells_x), cells_x), :] = both[:, :cells_y]
            mid[pl.ds(pl.multiple_of(row + cells_x, cells_x), cells_x), :] = both[:, cells_y:]
        return carry

    lax.fori_loop(0, cells_z // block, planes, 0)

    @pl.when((orbital == 0) & (chunk == 0))
    def _():
        dens[...] = jnp.zeros_like(dens)

    @pl.when(chunk == chunks - 1)
    def _():
        def columns(i, carry):
            x = 2 * i
            pair = jnp.concatenate(
                [
                    mid[pl.ds(x, length, stride=cells_x), :].astype(BF16),
                    mid[pl.ds(x + 1, length, stride=cells_x), :].astype(BF16),
                ],
                axis=1,
            )
            values = dot(mz, pair).astype(BF16)
            for k in range(2):
                psi = values[:, k * cells_y : (k + 1) * cells_y]
                psi_ref[0, x + k] = psi
                psi = psi.astype(F32)
                dens[x + k] = dens[x + k] + weight * (psi * psi)
            return carry

        lax.fori_loop(0, cells_x // 2, columns, 0, unroll=2)

    @pl.when((orbital == orbitals - 1) & (chunk == chunks - 1))
    def _():
        dht = dht_ref[...]

        def total(x, acc):
            return acc + dens[x]

        summed = lax.fori_loop(0, cells_x, total, jnp.zeros((length, cells_y), F32), unroll=4)
        mean = jnp.sum(summed) / (length * cells_x * cells_y)
        mean_code, mean_fine, mean_step = scale_of(mean)
        mean_units = jnp.round(mean * (LEVELS / mean_step))
        mean = mean_units * (mean_step * (1.0 / LEVELS))

        def transform(i, largest):
            x = 2 * i
            pair = jnp.concatenate([dens[x] - mean, dens[x + 1] - mean], axis=1)
            waves = dot_exact(dht, pair)
            for k in range(2):
                part = waves[:, k * cells_y : (k + 1) * cells_y]
                mid[pl.ds(x + k, length, stride=cells_x), :] = part
                largest = jnp.maximum(largest, jnp.abs(part))
            return largest

        largest = lax.fori_loop(
            0, cells_x // 2, transform, jnp.zeros((length, cells_y), F32), unroll=2
        )
        code, fine, top = scale_of(jnp.max(largest))
        factor = LEVELS / top
        code_rows = coded_rows(cells_y, (code, fine, mean_code, mean_fine, mean_units))
        per = length // q_ref.shape[0]

        def quantise(i, carry):
            rows = per * cells_x
            values = mid[pl.ds(pl.multiple_of(i * rows, rows), rows), :] * factor
            q_ref[i, 0:rows, :] = jnp.round(values).astype(jnp.int32).astype(jnp.int16)
            q_ref[i, rows : rows + 16, :] = code_rows
            return carry

        lax.fori_loop(0, q_ref.shape[0], quantise, 0, unroll=2)


def density(occupations, slot_orbital, c, halo, my, ax, mz, dht, owners):
    orbitals, length, cells_x, cells_y = c.shape
    chunks = 4
    part = length // chunks
    smem = pl.BlockSpec(memory_space=pltpu.SMEM)
    rows = (length // owners) * cells_x + 16
    return pl.pallas_call(
        density_kernel,
        grid=(orbitals, chunks),
        in_specs=[
            smem,
            smem,
            pl.BlockSpec((1, part, cells_x, cells_y), lambda o, j: (o, j, 0, 0)),
            pl.BlockSpec((1, part, halo.shape[2], cells_y), lambda o, j: (o, j, 0, 0)),
            whole(my),
            whole(ax),
            whole(mz),
            whole(dht),
        ],
        out_specs=[
            pl.BlockSpec((1, cells_x, length, cells_y), lambda o, j: (o, 0, 0, 0)),
            pl.BlockSpec((owners, rows, cells_y), lambda o, j: (0, 0, 0)),
        ],
        out_shape=[
            jax.ShapeDtypeStruct((orbitals, cells_x, length, cells_y), BF16),
            jax.ShapeDtypeStruct((owners, rows, cells_y), jnp.int16),
        ],
        scratch_shapes=[
            pltpu.VMEM((length * cells_x, cells_y), F32),
            pltpu.VMEM((cells_x, length, cells_y), F32),
        ],
        compiler_params=params(2),
        name="density",
    )(occupations, slot_orbital, c, halo, my, ax, mz, dht)


def kinetic_kernel(c_ref, h_ref, dy_ref, dx_ref, dz_ref, kin_ref, sums_ref, wide_c, acc):
    length, cells_x, cells_y = c_ref.shape[1], c_ref.shape[2], c_ref.shape[3]
    block = 8
    dy = dy_ref[...]
    dx = dx_ref[...]
    dz = dz_ref[...]

    def widen(i, carry):
        rows = block * cells_x
        values = c_ref[0, pl.ds(i * block, block)].reshape(rows, cells_y)
        wide_c[pl.ds(pl.multiple_of(i * rows, rows), rows), :] = values.astype(F32)
        return carry

    lax.fori_loop(0, length // block, widen, 0)

    def columns(i, carry):
        x = 2 * i
        pair = jnp.concatenate(
            [
                wide_c[pl.ds(x, length, stride=cells_x), :].astype(BF16),
                wide_c[pl.ds(x + 1, length, stride=cells_x), :].astype(BF16),
            ],
            axis=1,
        )
        values = dot(dz, pair)
        acc[pl.ds(x, length, stride=cells_x), :] = values[:, :cells_y]
        acc[pl.ds(x + 1, length, stride=cells_x), :] = values[:, cells_y:]
        return carry

    lax.fori_loop(0, cells_x // 2, columns, 0, unroll=2)

    def planes(i, carry):
        energy, norm = carry
        z0 = i * block
        own = c_ref[0, pl.ds(z0, block)]
        ext = jnp.concatenate(
            [h_ref[0, pl.ds(z0, block), 0:16, :], own, h_ref[0, pl.ds(z0, block), 16:32, :]],
            axis=1,
        )
        rows = block * cells_x
        along_y = dot(own.reshape(rows, cells_y), dy)
        for p in range(0, block, 2):
            along_x = dot(dx, jnp.concatenate([ext[p], ext[p + 1]], axis=1))
            for k in range(2):
                z = z0 + p + k
                at = pl.ds(pl.multiple_of(z * cells_x, cells_x), cells_x)
                value = (
                    acc[at, :]
                    + along_x[:, k * cells_y : (k + 1) * cells_y]
                    + along_y[(p + k) * cells_x : (p + k + 1) * cells_x]
                )
                kin_ref[0, z] = value
                coeff = own[p + k].astype(F32)
                energy = energy + coeff * value
                norm = norm + coeff * coeff
        return energy, norm

    zeros = jnp.zeros((cells_x, cells_y), F32)
    energy, norm = lax.fori_loop(0, length // block, planes, (zeros, zeros))
    sums_ref[0, 0] = jnp.sum(energy.reshape(cells_x // 8, 8, cells_y), axis=0)
    sums_ref[0, 1] = jnp.sum(norm.reshape(cells_x // 8, 8, cells_y), axis=0)


def kinetic(c, halo, dy, dx, dz):
    orbitals, length, cells_x, cells_y = c.shape
    cells = orbitals * length * cells_x * cells_y
    return pl.pallas_call(
        kinetic_kernel,
        grid=(orbitals,),
        in_specs=[
            pl.BlockSpec((1, length, cells_x, cells_y), lambda o: (o, 0, 0, 0)),
            pl.BlockSpec((1, length, halo.shape[2], cells_y), lambda o: (o, 0, 0, 0)),
            whole(dy),
            whole(dx),
            whole(dz),
        ],
        out_specs=[
            pl.BlockSpec((1, length, cells_x, cells_y), lambda o: (o, 0, 0, 0)),
            pl.BlockSpec((1, 2, 8, cells_y), lambda o: (o, 0, 0, 0)),
        ],
        out_shape=[
            jax.ShapeDtypeStruct((orbitals, length, cells_x, cells_y), F32),
            jax.ShapeDtypeStruct((orbitals, 2, 8, cells_y), F32),
        ],
        scratch_shapes=[
            pltpu.VMEM((length * cells_x, cells_y), F32),
            pltpu.VMEM((length * cells_x, cells_y), F32),
        ],
        compiler_params=params(1),
        cost_estimate=pl.CostEstimate(
            flops=cells * 768 * 4, bytes_accessed=cells * 7, transcendentals=0
        ),
        name="kinetic",
    )(c, halo, dy, dx, dz)


def unpacked(ref, source, rows):
    codes = ref[source, rows : rows + 16, :].astype(jnp.int32).astype(F32)
    powers = jnp.exp2(codes) * (1.0 / (LEVELS * FINE))
    step = codes[1:2] * powers[0:1]
    mean = codes[4:5] * (codes[3:4] * powers[2:3])
    return ref[source, 0:rows, :].astype(jnp.int32).astype(F32) * step, mean


def sum_kernel(per, got_ref, out_ref):
    rows = out_ref.shape[0]
    cells_y = out_ref.shape[1]

    def body(source, carry):
        total, means = carry
        values, mean = unpacked(got_ref, source, rows)
        return total + values, means + mean

    total, means = lax.fori_loop(
        0,
        got_ref.shape[0],
        body,
        (jnp.zeros((rows, cells_y), F32), jnp.zeros((1, cells_y), F32)),
        unroll=2,
    )
    length = got_ref.shape[0] * per
    row = lax.broadcasted_iota(jnp.int32, (rows, cells_y), 0)
    flat = (lax.axis_index("orb") == 0) & (row < rows // per)
    out_ref[...] = total + jnp.where(flat, means * math.sqrt(length), 0.0)


def slab_sum(got, rows, per):
    return pl.pallas_call(
        functools.partial(sum_kernel, per),
        out_shape=jax.ShapeDtypeStruct((rows, got.shape[2]), F32),
        compiler_params=pltpu.CompilerParams(vmem_limit_bytes=VMEM_LIMIT),
        name="slab_sum",
    )(got)


def solve_kernel(curve_z_ref, slab_ref, dht_ref, curve_x_ref, curve_y_ref, q_ref):
    per, length, cells_y = slab_ref.shape
    cells_x = length // 2
    orb = lax.axis_index("orb")
    corner = pl.multiple_of(lax.axis_index("grid") * cells_x, cells_x)
    dht = dht_ref[...]
    own = dht_ref[pl.ds(corner, cells_x), :]
    row = lax.broadcasted_iota(jnp.int32, (length, cells_y), 0)
    col = lax.broadcasted_iota(jnp.int32, (length, cells_y), 1)
    plane_curve = curve_x_ref[...] + curve_y_ref[...]
    parts = []
    for k in range(per):
        wave = orb * per + k
        anchor = (row == 0) & (col == 0) & (wave == 0)
        bent = plane_curve + curve_z_ref[wave]
        factor = jnp.where(anchor, 0.0, COULOMB / jnp.where(anchor, 1.0, bent))
        spectrum = dot_exact(dot_exact(dht, slab_ref[k]), dht) * factor
        parts.append(dot_exact(dot_exact(own, spectrum), dht))
    field = jnp.concatenate(parts, axis=0)
    code, fine, top = scale_of(jnp.max(jnp.abs(field)))
    coded = jnp.round(field * (LEVELS / top)).astype(jnp.int32).astype(jnp.int16)
    code_rows = coded_rows(cells_y, (code, fine))
    rows = per * cells_x

    def spread(i, carry):
        q_ref[i, 0:rows, :] = coded
        q_ref[i, rows : rows + 16, :] = code_rows
        return carry

    lax.fori_loop(0, q_ref.shape[0], spread, 0)


def solve(curve_z, slab, dht, curve_x, curve_y, owners):
    per, length, cells_y = slab.shape
    vmem = pl.BlockSpec(memory_space=pltpu.VMEM)
    return pl.pallas_call(
        solve_kernel,
        in_specs=[pl.BlockSpec(memory_space=pltpu.SMEM), vmem, vmem, vmem, vmem],
        out_shape=jax.ShapeDtypeStruct((owners, per * (length // 2) + 16, cells_y), jnp.int16),
        compiler_params=pltpu.CompilerParams(vmem_limit_bytes=VMEM_LIMIT),
        name="solve",
    )(curve_z, slab, dht, curve_x, curve_y)


def field_kernel(got_ref, psi_ref, dht_ref, tz_ref, back_ref, slab_ref, sums_ref, waves):
    step = pl.program_id(0)
    orbitals, some_x, length, cells_y = psi_ref.shape
    owners = got_ref.shape[0]
    cells_x = waves.shape[0] // length
    per = length // owners
    rows = per * cells_x
    dht = dht_ref[...]
    tz = tz_ref[...]
    first = lax.axis_index("orb") * per

    @pl.when(step == 0)
    def _():
        def unpack(source, carry):
            at = pl.ds(pl.multiple_of(source * rows, rows), rows)
            waves[at, :] = unpacked(got_ref, source, rows)[0]
            return carry

        lax.fori_loop(0, owners, unpack, 0, unroll=2)
        sums_ref[...] = jnp.zeros_like(sums_ref)

    def columns(i, carry):
        local = 2 * i
        x = step * some_x + local
        pair = jnp.concatenate(
            [
                waves[pl.ds(x, length, stride=cells_x), :],
                waves[pl.ds(x + 1, length, stride=cells_x), :],
            ],
            axis=1,
        )
        field = dot_exact(dht, pair)
        slab_ref[local] = field[:, :cells_y]
        slab_ref[local + 1] = field[:, cells_y:]
        new = []
        for o in range(orbitals):
            psi = jnp.concatenate([psi_ref[o, local], psi_ref[o, local + 1]], axis=1).astype(F32)
            product = field * psi
            squares = product * psi
            squares = squares[:, :cells_y] + squares[:, cells_y:]
            new.append(carry[o] + jnp.sum(squares.reshape(length // 8, 8, cells_y), axis=0))
            back = dot(tz, product.astype(BF16)).astype(BF16)
            back_ref[o, local] = back[:, :cells_y]
            back_ref[o, local + 1] = back[:, cells_y:]
        return tuple(new)

    zeros = jnp.zeros((8, cells_y), F32)
    energy = lax.fori_loop(0, some_x // 2, columns, (zeros,) * orbitals, unroll=2)
    for o in range(orbitals):
        sums_ref[o] = sums_ref[o] + energy[o]


def field(got, psi, dht, tz):
    orbitals, cells_x, length, cells_y = psi.shape
    chunks = 8
    part = cells_x // chunks
    return pl.pallas_call(
        field_kernel,
        grid=(chunks,),
        in_specs=[
            whole(got),
            pl.BlockSpec((orbitals, part, length, cells_y), lambda i: (0, i, 0, 0)),
            whole(dht),
            whole(tz),
        ],
        out_specs=[
            pl.BlockSpec((orbitals, part, length, cells_y), lambda i: (0, i, 0, 0)),
            pl.BlockSpec((part, length, cells_y), lambda i: (i, 0, 0)),
            pl.BlockSpec((orbitals, 8, cells_y), lambda i: (0, 0, 0)),
        ],
        out_shape=[
            jax.ShapeDtypeStruct((orbitals, cells_x, length, cells_y), BF16),
            jax.ShapeDtypeStruct((cells_x, length, cells_y), F32),
            jax.ShapeDtypeStruct((orbitals, 8, cells_y), F32),
        ],
        scratch_shapes=[pltpu.VMEM((length * cells_x, cells_y), F32)],
        compiler_params=params(1),
        name="field",
    )(got, psi, dht, tz)


def update_kernel(
    energy_ref, back_ref, low_ref, high_ref, c_ref, kin_ref, tx_ref, ty_ref, out_ref, wide
):
    orbital = pl.program_id(0)
    cells_x, some_z, cells_y = back_ref.shape[1], back_ref.shape[2], back_ref.shape[3]
    margin = low_ref.shape[1]
    energy = energy_ref[orbital]
    tx = tx_ref[...]
    ty = ty_ref[...]

    def put(row, values):
        count = values.shape[0] * some_z
        wide[pl.ds(pl.multiple_of(row, some_z), count), :] = values.reshape(count, cells_y).astype(
            F32
        )

    put(0, low_ref[0])
    put((margin + cells_x) * some_z, high_ref[0])

    def widen(i, carry):
        put((margin + 8 * i) * some_z, back_ref[0, pl.ds(8 * i, 8)])
        return carry

    lax.fori_loop(0, cells_x // 8, widen, 0)
    total = cells_x + 2 * margin
    block = 4

    def planes(i, carry):
        z0 = i * block
        crossed = []
        for p in range(0, block, 2):
            pair = jnp.concatenate(
                [
                    wide[pl.ds(z0 + p, total, stride=some_z), :].astype(BF16),
                    wide[pl.ds(z0 + p + 1, total, stride=some_z), :].astype(BF16),
                ],
                axis=1,
            )
            both = dot(tx, pair).astype(BF16)
            crossed += [both[:, :cells_y], both[:, cells_y:]]
        potential = dot(jnp.concatenate(crossed, axis=0), ty)
        for p in range(block):
            z = z0 + p
            applied = potential[p * cells_x : (p + 1) * cells_x] + kin_ref[0, z]
            coeff = c_ref[0, z].astype(F32)
            out_ref[0, z] = (coeff - STEP_SIZE * (applied - energy * coeff)).astype(BF16)
        return carry

    lax.fori_loop(0, some_z // block, planes, 0, unroll=2)


def update(energies, back, low, high, c, kin, tx, ty):
    orbitals, length, cells_x, cells_y = c.shape
    chunks = 4
    part = length // chunks
    margin = low.shape[1]

    def x_major(count):
        return pl.BlockSpec((1, count, part, cells_y), lambda o, j: (o, 0, j, 0))

    z_major = pl.BlockSpec((1, part, cells_x, cells_y), lambda o, j: (o, j, 0, 0))
    return pl.pallas_call(
        update_kernel,
        grid=(orbitals, chunks),
        in_specs=[
            pl.BlockSpec(memory_space=pltpu.SMEM),
            x_major(cells_x),
            x_major(margin),
            x_major(margin),
            z_major,
            z_major,
            whole(tx),
            whole(ty),
        ],
        out_specs=z_major,
        out_shape=jax.ShapeDtypeStruct(c.shape, BF16),
        scratch_shapes=[pltpu.VMEM(((cells_x + 2 * margin) * part, cells_y), F32)],
        compiler_params=params(2),
        name="update",
    )(energies, back, low, high, c, kin, tx, ty)


def to_other(array):
    return lax.ppermute(array, "grid", [(0, 1), (1, 0)])


def to_all(blocks):
    return lax.all_to_all(blocks, "orb", split_axis=0, concat_axis=0, tiled=True)


def on_device(coefficients, occupations, slot_orbital):
    orbitals, length, cells_x, cells_y = coefficients.shape
    owners = slot_orbital.shape[0] // orbitals
    per = length // owners
    magic, trans, kin_taps = magic_pairs(), transposed_pairs(), kinetic_pairs()
    magic_line = band_periodic(length, magic)
    trans_line = band_periodic(length, trans)
    kin_line = band_periodic(length, kin_taps, -0.5)
    dht = hartley(length)
    waves = curve(length).astype(np.float32)

    rims = jnp.concatenate(
        [coefficients[:, :, cells_x - 16 :], coefficients[:, :, :16]], axis=2
    )
    halo = to_other(rims)
    psi, coded = density(
        occupations,
        slot_orbital,
        coefficients,
        halo,
        jnp.asarray(magic_line.T),
        jnp.asarray(band_open(cells_x, 16, magic)),
        jnp.asarray(magic_line),
        jnp.asarray(dht),
        owners,
    )
    got = to_all(coded)
    kin, kin_sums = kinetic(
        coefficients,
        halo,
        jnp.asarray(kin_line.T),
        jnp.asarray(band_open(cells_x, 16, kin_taps, -0.5)),
        jnp.asarray(kin_line),
    )
    half = slab_sum(got, per * cells_x, per).reshape(per, cells_x, cells_y)
    slab = lax.all_gather(half, "grid", axis=1, tiled=True)
    spread = solve(
        jnp.asarray(waves),
        slab,
        jnp.asarray(dht),
        jnp.asarray(np.broadcast_to(waves[:, None], (length, cells_y))),
        jnp.asarray(np.broadcast_to(waves[None, :], (length, cells_y))),
        owners,
    )
    back, full_field, field_sums = field(
        to_all(spread), psi, jnp.asarray(dht), jnp.asarray(trans_line)
    )
    low = to_other(back[:, cells_x - 8 :])
    high = to_other(back[:, :8])
    sums = jnp.stack(
        [
            jnp.sum(kin_sums[:, 0], axis=(1, 2)) + jnp.sum(field_sums, axis=(1, 2)),
            jnp.sum(kin_sums[:, 1], axis=(1, 2)),
        ]
    )
    sums = sums + to_other(sums)
    energies = sums[0] / sums[1]
    updated = update(
        energies,
        back,
        low,
        high,
        coefficients,
        kin,
        jnp.asarray(band_open(cells_x, 8, trans)),
        jnp.asarray(trans_line.T),
    )
    first = lax.axis_index("orb") * per
    potential = lax.dynamic_slice_in_dim(full_field, first, per, 1).transpose(1, 0, 2)
    return (updated, energies, potential)


def solution(mesh):
    return jax.shard_map(
        on_device,
        mesh=mesh,
        in_specs=(P("orb", None, "grid", None), P(), P()),
        out_specs=(P("orb", None, "grid", None), P("orb"), P("orb", "grid", None)),
        check_vma=False,
    )
```

time: 439 us -> 217 us (0.49); the launches traced: 432 us -> 217 us
  waiting for transfers between devices: 186 us -> 6.11 us
  Pallas kernels: 0 us -> 140 us
  matrix products: 78.1 us -> 0 us
  local copies, waits for them, and re-layouts: 76.8 us -> 11.1 us
  other arithmetic: 46.2 us -> 2.02 us
  blocking collectives: 10.3 us -> 48.7 us
  starting transfers between devices: 34 us -> 7.72 us
    all_to_all x4 -> x1, waiting for transfers between devices: 181 us -> 0.01 us  [to_all(): lax.all_to_all(blocks, 'orb', split_axis=0, concat_axis=0, tiled=True)]
    pallas_call x0 -> x6, Pallas kernels: none -> 140 us  [the longest x1 46.6 us: density(): pl.pallas_call(density_kernel, grid=(orbitals, chunks), in_specs=[smem, s...]
    dot_general x28 -> x0, matrix products: 78.1 us -> none  [the longest x3 27.1 us: along_depth(): jnp.einsum('ji,ojxy->oixy', matrix, values, preferred_element_type=jnp.fl...]
    all_to_all x0 -> x1, blocking collectives: none -> 43.8 us  [to_all(): lax.all_to_all(blocks, 'orb', split_axis=0, concat_axis=0, tiled=True)]
    all_to_all x4 -> x1, starting transfers between devices: 32.2 us -> 5.1 us  [to_all(): lax.all_to_all(blocks, 'orb', split_axis=0, concat_axis=0, tiled=True)]
    reduce_sum x3 -> x2, other arithmetic: 25.8 us -> 0.93 us  [the longest x1 0.83 us: on_device(): jnp.sum(kin_sums[:, 0], axis=(1, 2)) + jnp.sum(field_sums, axis=(1, 2))]
    convert_element_type x2 -> x0, local copies, waits for them, and re-layouts: 22.2 us -> none  [the longest x1 11.1 us: on_device(): back_z = along_depth(product, trans_line).astype(jnp.bfloat16)]
    convert_element_type x2 -> x0, other arithmetic: 20.1 us -> none  [the longest x1 12.3 us: on_device(): updated = (coeff_wide - STEP_SIZE * (applied - energies[:, None, None, No...]
  transfers between devices with their start and end apart: 6 -> 5, of which waited for: 6 -> 2; matrix products, arithmetic and copies ran while one was open for 11% -> 1% of each run, Pallas kernels for 0% -> 17%
where the time goes in v1:
time: 217 us
  Pallas kernels  140 us (65%)
  blocking collectives  48.7 us (22%)
  local copies, waits for them, and re-layouts  11.1 us (5%)
  starting transfers between devices  7.72 us (4%)
  waiting for transfers between devices  6.11 us (3%)
    pallas_call x1, Pallas kernels, density(): pl.pallas_call(density_kernel, grid=(orbitals, chunks), in_specs=[smem, s...  46.6 us
    all_to_all x1, blocking collectives, to_all(): lax.all_to_all(blocks, 'orb', split_axis=0, concat_axis=0, tiled=True)  43.8 us
    pallas_call x1, Pallas kernels, kinetic(): pl.pallas_call(kinetic_kernel, grid=(orbitals,), in_specs=[pl.BlockSpec((...  36.5 us
    pallas_call x1, Pallas kernels, update(): pl.pallas_call(update_kernel, grid=(orbitals, chunks), in_specs=[pl.Block...  27.6 us
    pallas_call x1, Pallas kernels, field(): pl.pallas_call(field_kernel, grid=(chunks,), in_specs=[whole(got), pl.Blo...  21.9 us
    ppermute x4, waiting for transfers between devices, to_other(): return lax.ppermute(array, 'grid', [(0, 1), (1, 0)])  6.11 us
    all_to_all x1, starting transfers between devices, to_all(): lax.all_to_all(blocks, 'orb', split_axis=0, concat_axis=0, tiled=True)  5.1 us
    all_gather x1, blocking collectives, on_device(): slab = lax.all_gather(half, 'grid', axis=1, tiled=True)  4.9 us
  transfers between devices with their start and end apart: 5, of which 2 were waited for; matrix products, arithmetic and copies ran while one was open for 1% of the time, Pallas kernels for 17%

profile of v1, /device:TPU:1, one launch (start us, length us, event | category | flops | bytes accessed | tf_op | source)
XLA Modules:
  0.0 216.8 jit_solution(16329201568419909541)
XLA Ops:
  0.6 2.5 %fusion.3 = (bf16[3,128,16,128]{3,2,1,0:T(8,128)(2,1)S(1)}, bf16[3,128,16,128]{3,2,1,0:T(8,128)(2,1)S(1)}) fusion(bf16[3,128,64,128]{3,2,1,0:T(8,128)(2,1)} %c_ref.5), kind=kLoop, calls=%fused_computation.10 | loop fusion | bytes 6291456 | tf_op jit(solution)/shard_map/slice | solution.py:637
  3.1 0.5 pad_maximum_fusion
  3.7 1.5 collective-permute-start
  5.2 5.3 %collective-permute-done.h_ref = bf16[3,128,32,128]{3,2,1,0:T(8,128)(2,1)S(1)} collective-permute-done((bf16[3,128,32,128]{3,2,1,0:T(8,128)(2,1)S(1)}, bf16[3,128,32,128]{3,2,1,0:T(8,128)(2,1)S(1)}, u32[]{:S(2)}, u32[]{:S(2)}) %collective-permute-start) | collective-permute-done | bytes 3145760 | tf_op jit(solution)/shard_map/ppermute | solution.py:618
  10.4 0.0 copy-start.1
  10.5 1.6 copy-done.1
  12.1 46.6 %density.1 = (bf16[3,64,128,128]{3,2,1,0:T(8,128)(2,1)}, s16[64,144,128]{2,1,0:T(8,128)(2,1)}) custom-call(s32[192]{0:T(256)} %occ_ref.1, s32[192]{0:T(256)} %slot_ref.1, bf16[3,128,64,128]{3,2,1,0:T(8,128)(2,1)} %c_ref.5, bf16[3,128,32,128]{3,2,1,0:T(8,128)(2,1)} %copy-done.1, bf16[128,128]{1,0:T(8,128)(2,1)} %constant.30.clone.my_ref.tz_ref, ...), custom_call_target="tpu_custom_call" | custom-call | tf_op jit(solution)/shard_map/density/pallas_call | solution.py:245
  58.7 0.0 copy-start.5
  58.7 43.8 %all_to_all.10.got_ref = s16[64,144,128]{2,1,0:T(8,128)(2,1)} all-to-all(s16[64,144,128]{2,1,0:T(8,128)(2,1)} %get-tuple-element.11), channel_id=1, replica_groups=mesh['orb'=64,'grid'=2] {'orb'}, dimensions={0} | all-to-all | bytes 4718592 | tf_op jit(solution)/shard_map/all_to_all | solution.py:622
  102.5 3.2 %slab_sum.1 = f32[128,128]{1,0:T(8,128)} custom-call(s16[64,144,128]{2,1,0:T(8,128)(2,1)} %all_to_all.10.got_ref), custom_call_target="tpu_custom_call" | custom-call | tf_op jit(solution)/shard_map/slab_sum/pallas_call | solution.py:402
  105.6 4.9 %all_gather.3.slab_ref = f32[2,128,128]{2,1,0:T(8,128)} all-gather(f32[2,64,128]{2,1,0:T(8,128)} %bitcast.8), channel_id=1, replica_groups=mesh['orb'=64,'grid'=2] {'grid'}, dimensions={1}, use_global_device_ids=true | all-gather | bytes 196608 | tf_op jit(solution)/shard_map/all_gather | solution.py:660
  110.5 0.0 copy-done.5
  110.5 0.6 jit_solution_.7.curve_y_ref
  111.2 0.7 jit_solution_.6.curve_x_ref
  111.9 4.6 %solve.1 = s16[64,144,128]{2,1,0:T(8,128)(2,1)} custom-call(f32[128]{0:T(128)} %constant.36.clone.curve_z_ref, f32[2,128,128]{2,1,0:T(8,128)} %all_gather.3.slab_ref, f32[128,128]{1,0:T(8,128)} %constant.33.clone.dht_ref, f32[128,128]{1,0:T(8,128)} %jit_solution_.6.curve_x_ref, f32[128,128]{1,0:T(8,128)} %jit_solution_.7.curve_y_ref), custom_call_target="tpu_custom_call" | custom-call | tf_op jit(solution)/shard_map/solve/pallas_call | solution.py:445
  116.5 5.1 %all-to-all-start.1 = ((s16[64,144,128]{2,1,0:T(8,128)(2,1)}), s16[64,144,128]{2,1,0:T(8,128)(2,1)S(1)}, u32[]{:S(2)}, u32[]{:S(2)}) async-start(s16[64,144,128]{2,1,0:T(8,128)(2,1)} %solve.1), calls=%async_computation.1 | async-start | bytes 4718592 | tf_op jit(solution)/shard_map/all_to_all | solution.py:622
  121.6 36.5 %kinetic.1 = (f32[3,128,64,128]{3,2,1,0:T(8,128)}, f32[3,2,8,128]{3,2,1,0:T(8,128)}) custom-call(bf16[3,128,64,128]{3,2,1,0:T(8,128)(2,1)} %c_ref.5, bf16[3,128,32,128]{3,2,1,0:T(8,128)(2,1)} %copy-done.1, bf16[128,128]{1,0:T(8,128)(2,1)} %constant.34.clone.dy_ref.dz_ref, bf16[64,96]{1,0:T(8,128)(2,1)} %constant.35.clone.dx_ref, ...), custom_call_target="tpu_custom_call" | custom-call | flops 9663676416 | bytes 22020096 | tf_op jit(solution)/shard_map/kinetic/pallas_call | solution.py:341
  158.1 0.8 slice_reduce_fusion.1
  158.9 0.0 all-to-all-done.1.got_ref
  158.9 0.0 copy-start
  158.9 1.5 copy-done
  160.4 21.9 %field.1 = (bf16[3,64,128,128]{3,2,1,0:T(8,128)(2,1)}, f32[64,128,128]{2,1,0:T(8,128)}, f32[3,8,128]{2,1,0:T(8,128)}) custom-call(s16[64,144,128]{2,1,0:T(8,128)(2,1)} %copy-done, bf16[3,64,128,128]{3,2,1,0:T(8,128)(2,1)} %get-tuple-element.12.psi_ref, f32[128,128]{1,0:T(8,128)} %constant.33.clone.dht_ref, bf16[128,128]{1,0:T(8,128)(2,1)} %constant.30.clone.my_ref.tz_ref), custom_call_target="tpu_custom_call" | custom-call | tf_op jit(solution)/shard_map/field/pallas_call | solution.py:510
  182.3 0.0 copy-start.4
  182.3 1.5 fusion.2
  183.8 0.5 collective-permute-start.3
  184.3 0.1 collective-permute-start.2
  184.4 1.0 dynamic-slice_bitcast_fusion
  185.4 0.6 copy.19
  186.0 0.0 copy-done.4
  186.0 0.1 reduce_sum.28
  186.2 0.5 collective-permute-start.1
  186.7 0.8 collective-permute-done.1
  187.5 0.5 fusion.energy_ref
  188.0 0.0 collective-permute-done.3.high_ref
  188.0 0.0 copy-start.2
  188.0 0.0 collective-permute-done.2.low_ref
  188.0 0.0 copy-start.3
  188.0 0.9 copy-done.2
  188.9 0.3 copy-done.3
  189.2 27.6 %update.1 = bf16[3,128,64,128]{3,2,1,0:T(8,128)(2,1)} custom-call(f32[3]{0:T(128)} %fusion.energy_ref, bf16[3,64,128,128]{3,2,1,0:T(8,128)(2,1)} %get-tuple-element.14.back_ref, bf16[3,8,128,128]{3,2,1,0:T(8,128)(2,1)} %copy-done.3, bf16[3,8,128,128]{3,2,1,0:T(8,128)(2,1)} %copy-done.2, bf16[3,128,64,128]{3,2,1,0:T(8,128)(2,1)} %c_ref.5, ...), custom_call_target="tpu_custom_call" | custom-call | tf_op jit(solution)/shard_map/update/pallas_call | solution.py:596
  (3 shorter events, 0.0 us)
Async XLA Ops:
  3.7 6.8 %collective-permute-start = (bf16[3,128,32,128]{3,2,1,0:T(8,128)(2,1)S(1)}, bf16[3,128,32,128]{3,2,1,0:T(8,128)(2,1)S(1)}, u32[]{:S(2)}, u32[]{:S(2)}) collective-permute-start(bf16[3,128,32,128]{3,2,1,0:T(8,128)(2,1)S(1)} %pad_maximum_fusion), channel_id=1, source_target_pairs={{0,1},{1,0},{2,3},{3,2},{4,5},{5,4},{6,7},{7,6},{8,9},{9,8},{10,11... | collective-permute-start | bytes 9437192 | tf_op jit(solution)/shard_map/ppermute | solution.py:618
  10.4 1.6 copy-start.1
  58.7 51.9 %copy-start.5 = (f32[128]{0:T(128)S(1)}, f32[128]{0:T(128)}, u32[]{:S(2)}) copy-start(f32[128]{0:T(128)} %constant.36.clone.curve_z_ref) | copy-start | bytes 1540
  116.5 42.4 %all-to-all-start.1 = ((s16[64,144,128]{2,1,0:T(8,128)(2,1)}), s16[64,144,128]{2,1,0:T(8,128)(2,1)S(1)}, u32[]{:S(2)}, u32[]{:S(2)}) async-start(s16[64,144,128]{2,1,0:T(8,128)(2,1)} %solve.1), calls=%async_computation.1 | async-start | bytes 4718592 | tf_op jit(solution)/shard_map/all_to_all | solution.py:622
  158.9 1.5 copy-start
  182.3 3.7 %copy-start.4 = (f32[3,8,128]{2,1,0:T(8,128)S(1)}, f32[3,8,128]{2,1,0:T(8,128)}, u32[]{:S(2)}) copy-start(f32[3,8,128]{2,1,0:T(8,128)} %get-tuple-element.13) | copy-start | bytes 36868
  183.8 4.2 %collective-permute-start.3 = (bf16[3,8,128,128]{3,2,1,0:T(8,128)(2,1)S(1)}, bf16[3,8,128,128]{3,2,1,0:T(8,128)(2,1)S(1)}, u32[]{:S(2)}, u32[]{:S(2)}) collective-permute-start(bf16[3,8,128,128]{3,2,1,0:T(8,128)(2,1)S(1)} %get-tuple-element.22), channel_id=1, source_target_pairs={{0,1},{1,0},{2,3},{3,2},{4,5},{5,4},{6,7},{7,6},{8,9},{9,8},{10,11... | collective-permute-start | bytes 2359304 | tf_op jit(solution)/shard_map/ppermute | solution.py:618
  184.3 3.7 %collective-permute-start.2 = (bf16[3,8,128,128]{3,2,1,0:T(8,128)(2,1)S(1)}, bf16[3,8,128,128]{3,2,1,0:T(8,128)(2,1)S(1)}, u32[]{:S(2)}, u32[]{:S(2)}) collective-permute-start(bf16[3,8,128,128]{3,2,1,0:T(8,128)(2,1)S(1)} %get-tuple-element.23), channel_id=1, source_target_pairs={{0,1},{1,0},{2,3},{3,2},{4,5},{5,4},{6,7},{7,6},{8,9},{9,8},{10,11... | collective-permute-start | bytes 2359304 | tf_op jit(solution)/shard_map/ppermute | solution.py:618
  186.2 1.3 collective-permute-start.1
  188.0 0.9 copy-start.2
  188.0 1.1 copy-start.3

commit v2 on v1

v2 whole, which is shorter than its diff:
```python
import functools
import math

import jax
import jax.numpy as jnp
import ml_dtypes
import numpy as np
from jax import lax
from jax.experimental import pallas as pl
from jax.experimental.pallas import tpu as pltpu
from jax.sharding import PartitionSpec as P

MAGIC = (
    8.433424733352934e-07,
    -1.290557201342061e-05,
    8.76298447621056e-05,
    -0.00030158038132690465,
    0.001747237136729939,
    -0.009420470302010804,
    0.023738214637249424,
    0.0612625895831208,
    0.9940415697834004,
    -0.06048952891969835,
    -0.021030251609303816,
    0.013372634148547948,
    -0.0034412814449349387,
    0.0004944322768868992,
    -5.185986881173433e-05,
    2.7273449291197967e-06,
)
STEP_SIZE = 0.1
COULOMB = 4.0 * math.pi
LEVELS = 32000.0
FINE = 16384.0
F32 = jnp.float32
BF16 = jnp.bfloat16
HIGHEST = lax.Precision.HIGHEST
MIB = 1024 * 1024


def magic_pairs():
    return [(position - 8, MAGIC[position]) for position in range(16)]


def transposed_pairs():
    return [(8 - position, MAGIC[position]) for position in range(16)]


def kinetic_pairs():
    spread = 14
    weights = []
    for distance in range(1, spread + 1):
        numerator = 2.0 * (-1.0) ** (distance + 1) * math.factorial(spread) ** 2
        weights.append(
            numerator
            / (
                distance
                * distance
                * math.factorial(spread - distance)
                * math.factorial(spread + distance)
            )
        )
    result = [(0, -2.0 * sum(weights))]
    for distance in range(1, spread + 1):
        result.append((distance, weights[distance - 1]))
        result.append((-distance, weights[distance - 1]))
    return result


def rounded(weight):
    return np.float32(np.float32(weight).astype(ml_dtypes.bfloat16))


def band_periodic(length, pairs, scale=1.0):
    matrix = np.zeros((length, length), np.float32)
    for offset, weight in pairs:
        for i in range(length):
            matrix[i, (i + offset) % length] += scale * rounded(weight)
    return matrix.astype(ml_dtypes.bfloat16)


def band_columns(length, columns, pairs, scale=1.0):
    matrix = np.zeros((length, len(columns)), np.float32)
    place = {cell: k for k, cell in enumerate(columns)}
    for offset, weight in pairs:
        for i in range(length):
            matrix[i, place[i + offset]] += scale * rounded(weight)
    return matrix.astype(ml_dtypes.bfloat16)


def with_rims(length, inner, outer):
    return [*range(-outer, -inner), *range(length + inner, length + outer)]


def hartley(length):
    index = np.arange(length)
    angle = 2.0 * np.pi * ((index[:, None] * index[None, :]) % length) / length
    return ((np.cos(angle) + np.sin(angle)) / math.sqrt(length)).astype(np.float32)


def split_table(table):
    high = table.astype(ml_dtypes.bfloat16)
    low = (table - high.astype(np.float32)).astype(ml_dtypes.bfloat16)
    return np.concatenate([high, low], axis=1)


def curve(length):
    return 2.0 - 2.0 * np.cos(2.0 * np.pi * np.arange(length) / length)


def dot(a, b):
    return jnp.dot(a, b, preferred_element_type=F32)


def dot_exact(a, b):
    return jnp.dot(a, b, preferred_element_type=F32, precision=HIGHEST)


def params(count, mebibytes):
    return pltpu.CompilerParams(
        dimension_semantics=("arbitrary",) * count, vmem_limit_bytes=mebibytes * MIB
    )


def whole(array):
    zeros = (0,) * array.ndim
    return pl.BlockSpec(array.shape, lambda *_: zeros)


def scale_of(largest):
    largest = jnp.maximum(largest, 1e-30)
    code = jnp.ceil(jnp.log2(largest))
    power = jnp.exp2(code)
    units = jnp.ceil(largest / power * FINE) + 1.0
    return code, units, units * (1.0 / FINE) * power


def coded_rows(cells_y, codes):
    row = lax.broadcasted_iota(jnp.int32, (16, cells_y), 0)
    values = jnp.zeros((16, cells_y), F32)
    for k, code in enumerate(codes):
        values = jnp.where(row == k, code, values)
    return values.astype(jnp.int32).astype(jnp.int16)


def side_by_side(first, second):
    return jnp.concatenate([first, second], axis=1)


def hartley_pair(table, pair):
    high = pair.astype(BF16)
    low = (pair - high.astype(F32)).astype(BF16)
    return dot(table, jnp.concatenate([high, high], axis=0)) + dot(
        table, jnp.concatenate([low, low], axis=0)
    )


def rims_kernel(inner, outer, low_ref, high_ref, after_ref, out_ref):
    tile = low_ref.shape[2]
    low = low_ref[0].astype(F32)[:, tile - outer : tile - inner]
    high = high_ref[0].astype(F32)[:, inner:outer]
    out_ref[0] = jnp.concatenate([low, high], axis=1).astype(BF16)


def own_rims(c, inner, outer, after):
    orbitals, length, cells_x, cells_y = c.shape
    tile = 16
    chunks = 2
    part = length // chunks

    def at(k):
        return pl.BlockSpec((1, part, tile, cells_y), lambda o, j: (o, j, k, 0))

    return pl.pallas_call(
        functools.partial(rims_kernel, inner, outer),
        grid=(orbitals, chunks),
        in_specs=[at(cells_x // tile - 1), at(0), pl.BlockSpec(memory_space=pl.ANY)],
        out_specs=at(0),
        out_shape=jax.ShapeDtypeStruct((orbitals, length, 2 * (outer - inner), cells_y), BF16),
        compiler_params=params(2, 8),
        name="own_rims",
    )(c, c, after)


def density_kernel(
    first_steps,
    pitch,
    occ_ref,
    slot_ref,
    c_ref,
    h_ref,
    my_ref,
    ax_ref,
    mz_ref,
    dht_ref,
    psi_ref,
    q_ref,
    mid,
    waves,
    peak,
    level,
):
    step = pl.program_id(0)
    cells_z, cells_x, cells_y = c_ref.shape[1], c_ref.shape[2], c_ref.shape[3]
    rim = h_ref.shape[2]
    orbitals, some_x, length = psi_ref.shape[0], psi_ref.shape[1], psi_ref.shape[2]
    block = 8

    @pl.when(step < first_steps)
    def _():
        my = my_ref[...]
        ax = ax_ref[...]

        def planes(i, carry):
            z0 = i * block
            own = dot(c_ref[0, pl.ds(z0, block)].reshape(block * cells_x, cells_y), my)
            own = own.astype(BF16).reshape(block, cells_x, cells_y)
            far = dot(h_ref[0, pl.ds(z0, block)].reshape(block * rim, cells_y), my)
            far = far.astype(BF16).reshape(block, rim, cells_y)
            for p in range(0, block, 2):
                pair = jnp.concatenate(
                    [side_by_side(own[p], own[p + 1]), side_by_side(far[p], far[p + 1])], axis=0
                )
                both = dot(ax, pair)
                row = pl.multiple_of((step * cells_z + z0 + p) * pitch, 8)
                mid[pl.ds(row, cells_x), :] = both[:, :cells_y]
                mid[pl.ds(row + pitch, cells_x), :] = both[:, cells_y:]
            return carry

        lax.fori_loop(0, cells_z // block, planes, 0, unroll=4)

    def grid_values(x):
        first = lax.axis_index("orb") * orbitals
        total = jnp.zeros((length, 2 * cells_y), F32)
        kept = []
        for o in range(orbitals):
            weight = occ_ref[slot_ref[first + o]].astype(F32) / slot_ref.shape[0]
            row = o * length * pitch + x
            pair = side_by_side(
                mid[pl.ds(row, length, stride=pitch), :].astype(BF16),
                mid[pl.ds(row + 1, length, stride=pitch), :].astype(BF16),
            )
            values = dot(mz_ref[...], pair).astype(BF16)
            kept.append(values)
            wide = values.astype(F32)
            total = total + weight * (wide * wide)
        return kept, total

    @pl.when(step == first_steps)
    def _():
        _, total = grid_values(0)
        code, fine, top = scale_of(jnp.sum(total) / total.size)
        level[0] = code
        level[1] = fine
        level[2] = top
        peak[...] = jnp.zeros_like(peak)

    @pl.when(step >= first_steps)
    def _():
        x0 = (step - first_steps) * some_x
        mean = level[2]
        table = dht_ref[...]
        largest = peak[...]
        for local in range(0, some_x, 2):
            kept, total = grid_values(x0 + local)
            for o in range(orbitals):
                psi_ref[o, local] = kept[o][:, :cells_y]
                psi_ref[o, local + 1] = kept[o][:, cells_y:]
            result = hartley_pair(table, total - mean)
            waves[pl.ds(x0 + local, length, stride=pitch), :] = result[:, :cells_y]
            waves[pl.ds(x0 + local + 1, length, stride=pitch), :] = result[:, cells_y:]
            size = jnp.abs(result)
            size = jnp.maximum(size[:, :cells_y], size[:, cells_y:])
            largest = jnp.maximum(largest, jnp.max(size.reshape(length // 8, 8, cells_y), axis=0))
        peak[...] = largest

    @pl.when(step == pl.num_programs(0) - 1)
    def _():
        code, fine, top = scale_of(jnp.max(peak[...]))
        factor = LEVELS / top
        code_rows = coded_rows(cells_y, (code, fine, level[0], level[1], LEVELS))
        per = length // q_ref.shape[0]
        rows = per * cells_x

        def quantise(i, carry):
            for k in range(per):
                row = pl.multiple_of((i * per + k) * pitch, 8)
                values = jnp.round(waves[pl.ds(row, cells_x), :] * factor)
                at = pl.ds(k * cells_x, cells_x)
                q_ref[i, at, :] = values.astype(jnp.int32).astype(jnp.int16)
            q_ref[i, rows : rows + 16, :] = code_rows
            return carry

        lax.fori_loop(0, q_ref.shape[0], quantise, 0, unroll=4)


def density(occupations, slot_orbital, c, halo, my, ax, mz, dht, owners):
    orbitals, length, cells_x, cells_y = c.shape
    chunks = 4
    part = length // chunks
    first_steps = orbitals * chunks
    some_x = 8
    pitch = cells_x + 8
    smem = pl.BlockSpec(memory_space=pltpu.SMEM)
    rows = (length // owners) * cells_x + 16

    def at_first(s):
        s = jnp.minimum(s, first_steps - 1)
        return (s // chunks, s % chunks, 0, 0)

    return pl.pallas_call(
        functools.partial(density_kernel, first_steps, pitch),
        grid=(first_steps + cells_x // some_x,),
        in_specs=[
            smem,
            smem,
            pl.BlockSpec((1, part, cells_x, cells_y), at_first),
            pl.BlockSpec((1, part, halo.shape[2], cells_y), at_first),
            whole(my),
            whole(ax),
            whole(mz),
            whole(dht),
        ],
        out_specs=[
            pl.BlockSpec(
                (orbitals, some_x, length, cells_y),
                lambda s: (0, jnp.maximum(s - first_steps, 0), 0, 0),
            ),
            pl.BlockSpec((owners, rows, cells_y), lambda s: (0, 0, 0)),
        ],
        out_shape=[
            jax.ShapeDtypeStruct((orbitals, cells_x, length, cells_y), BF16),
            jax.ShapeDtypeStruct((owners, rows, cells_y), jnp.int16),
        ],
        scratch_shapes=[
            pltpu.VMEM((orbitals * length * pitch, cells_y), F32),
            pltpu.VMEM((length * pitch, cells_y), F32),
            pltpu.VMEM((8, cells_y), F32),
            pltpu.SMEM((3,), F32),
        ],
        compiler_params=params(1, 34),
        name="density",
    )(occupations, slot_orbital, c, halo, my, ax, mz, dht)


def kinetic_kernel(
    pitch, c_ref, near_ref, far_ref, dy_ref, dx_ref, dz_ref, after_ref, kin_ref, sums_ref, wide, acc
):
    length, cells_x, cells_y = c_ref.shape[1], c_ref.shape[2], c_ref.shape[3]
    block = 8

    def widen(z, carry):
        row = pl.multiple_of(z * pitch, 8)
        wide[pl.ds(row, cells_x), :] = c_ref[0, z].astype(F32)
        return carry

    lax.fori_loop(0, length, widen, 0, unroll=8)

    def columns(i, carry):
        x = 2 * i
        pair = side_by_side(
            wide[pl.ds(x, length, stride=pitch), :].astype(BF16),
            wide[pl.ds(x + 1, length, stride=pitch), :].astype(BF16),
        )
        values = dot(dz_ref[...], pair)
        acc[pl.ds(x, length, stride=pitch), :] = values[:, :cells_y]
        acc[pl.ds(x + 1, length, stride=pitch), :] = values[:, cells_y:]
        return carry

    lax.fori_loop(0, cells_x // 2, columns, 0, unroll=4)

    def planes(i, carry):
        energy, norm = carry
        z0 = i * block
        own = c_ref[0, pl.ds(z0, block)]
        along_y = dot(own.reshape(block * cells_x, cells_y), dy_ref[...])
        for p in range(0, block, 2):
            z = z0 + p
            pair = jnp.concatenate(
                [
                    side_by_side(c_ref[0, z], c_ref[0, z + 1]),
                    side_by_side(near_ref[0, z], near_ref[0, z + 1]),
                    side_by_side(far_ref[0, z], far_ref[0, z + 1]),
                ],
                axis=0,
            )
            along_x = dot(dx_ref[...], pair)
            for k in range(2):
                at = pl.ds(pl.multiple_of((z + k) * pitch, 8), cells_x)
                value = (
                    acc[at, :]
                    + along_x[:, k * cells_y : (k + 1) * cells_y]
                    + along_y[(p + k) * cells_x : (p + k + 1) * cells_x]
                )
                kin_ref[0, z + k] = value
                coeff = own[p + k].astype(F32)
                tiles = (cells_x // 8, 8, cells_y)
                energy = energy + jnp.sum((coeff * value).reshape(tiles), axis=0)
                norm = norm + jnp.sum((coeff * coeff).reshape(tiles), axis=0)
        return energy, norm

    zeros = jnp.zeros((8, cells_y), F32)
    energy, norm = lax.fori_loop(0, length // block, planes, (zeros, zeros), unroll=2)
    sums_ref[0, 0:8] = energy
    sums_ref[0, 8:16] = norm


def kinetic(c, near, far, dy, dx, dz, after):
    orbitals, length, cells_x, cells_y = c.shape
    cells = orbitals * length * cells_x * cells_y
    pitch = cells_x + 8

    def block(array):
        return pl.BlockSpec((1, *array.shape[1:]), lambda o: (o, 0, 0, 0))

    return pl.pallas_call(
        functools.partial(kinetic_kernel, pitch),
        grid=(orbitals,),
        in_specs=[
            block(c),
            block(near),
            block(far),
            whole(dy),
            whole(dx),
            whole(dz),
            pl.BlockSpec(memory_space=pl.ANY),
        ],
        out_specs=[block(c), pl.BlockSpec((1, 16, cells_y), lambda o: (o, 0, 0))],
        out_shape=[
            jax.ShapeDtypeStruct(c.shape, F32),
            jax.ShapeDtypeStruct((orbitals, 16, cells_y), F32),
        ],
        scratch_shapes=[
            pltpu.VMEM((length * pitch, cells_y), F32),
            pltpu.VMEM((length * pitch, cells_y), F32),
        ],
        compiler_params=params(1, 30),
        cost_estimate=pl.CostEstimate(
            flops=cells * 768 * 4, bytes_accessed=cells * 7, transcendentals=0
        ),
        name="kinetic",
    )(c, near, far, dy, dx, dz, after)


def unpacked(ref, source, rows):
    codes = ref[source, rows : rows + 16, :].astype(jnp.int32).astype(F32)
    powers = jnp.exp2(codes) * (1.0 / (LEVELS * FINE))
    step = codes[1:2] * powers[0:1]
    mean = codes[4:5] * (codes[3:4] * powers[2:3])
    return ref[source, 0:rows, :].astype(jnp.int32).astype(F32) * step, mean


def sum_kernel(per, got_ref, after_ref, out_ref):
    rows = out_ref.shape[0]
    cells_y = out_ref.shape[1]

    def body(source, carry):
        total, means = carry
        values, mean = unpacked(got_ref, source, rows)
        return total + values, means + mean

    total, means = lax.fori_loop(
        0,
        got_ref.shape[0],
        body,
        (jnp.zeros((rows, cells_y), F32), jnp.zeros((1, cells_y), F32)),
        unroll=2,
    )
    length = got_ref.shape[0] * per
    row = lax.broadcasted_iota(jnp.int32, (rows, cells_y), 0)
    flat = (lax.axis_index("orb") == 0) & (row < rows // per)
    out_ref[...] = total + jnp.where(flat, means * math.sqrt(length), 0.0)


def slab_sum(got, rows, per, after):
    return pl.pallas_call(
        functools.partial(sum_kernel, per),
        in_specs=[pl.BlockSpec(memory_space=pltpu.VMEM), pl.BlockSpec(memory_space=pl.ANY)],
        out_shape=jax.ShapeDtypeStruct((rows, got.shape[2]), F32),
        compiler_params=params(0, 12),
        name="slab_sum",
    )(got, after)


def solve_kernel(curve_z_ref, slab_ref, dht_ref, curve_ref, q_ref):
    per, length, cells_y = slab_ref.shape
    cells_x = length // 2
    orb = lax.axis_index("orb")
    corner = pl.multiple_of(lax.axis_index("grid") * cells_x, cells_x)
    dht = dht_ref[...]
    own = dht_ref[pl.ds(corner, cells_x), :]
    row = lax.broadcasted_iota(jnp.int32, (length, cells_y), 0)
    col = lax.broadcasted_iota(jnp.int32, (length, cells_y), 1)
    waves = dot_exact(jnp.concatenate([slab_ref[k] for k in range(per)], axis=0), dht)
    waves = jnp.concatenate(
        [waves[k * length : (k + 1) * length] for k in range(per)], axis=1
    )
    waves = dot_exact(dht, waves)
    parts = []
    for k in range(per):
        wave = orb * per + k
        anchor = (row == 0) & (col == 0) & (wave == 0)
        bent = curve_ref[...] + curve_z_ref[wave]
        factor = jnp.where(anchor, 0.0, COULOMB / jnp.where(anchor, 1.0, bent))
        parts.append(waves[:, k * cells_y : (k + 1) * cells_y] * factor)
    field = dot_exact(own, jnp.concatenate(parts, axis=1))
    field = jnp.concatenate(
        [field[:, k * cells_y : (k + 1) * cells_y] for k in range(per)], axis=0
    )
    field = dot_exact(field, dht)
    code, fine, top = scale_of(jnp.max(jnp.abs(field)))
    coded = jnp.round(field * (LEVELS / top)).astype(jnp.int32).astype(jnp.int16)
    code_rows = coded_rows(cells_y, (code, fine))
    rows = per * cells_x

    def spread(i, carry):
        q_ref[i, 0:rows, :] = coded
        q_ref[i, rows : rows + 16, :] = code_rows
        return carry

    lax.fori_loop(0, q_ref.shape[0], spread, 0, unroll=4)


def solve(curve_z, slab, dht, plane_curve, owners):
    per, length, cells_y = slab.shape
    vmem = pl.BlockSpec(memory_space=pltpu.VMEM)
    return pl.pallas_call(
        solve_kernel,
        in_specs=[pl.BlockSpec(memory_space=pltpu.SMEM), vmem, vmem, vmem],
        out_shape=jax.ShapeDtypeStruct((owners, per * (length // 2) + 16, cells_y), jnp.int16),
        compiler_params=params(0, 12),
        name="solve",
    )(curve_z, slab, dht, plane_curve)


def field_kernel(
    pitch,
    turn_pitch,
    got_ref,
    psi_ref,
    kin_ref,
    dht_ref,
    tz_ref,
    back_ref,
    rim_ref,
    slab_ref,
    sums_ref,
    waves,
    turn,
    head,
    values,
):
    step = pl.program_id(0)
    orbitals, some_x, length, cells_y = psi_ref.shape
    owners = got_ref.shape[0]
    per = length // owners
    cells_x = some_x * pl.num_programs(0)
    rim = rim_ref.shape[2] // 2
    first = pl.multiple_of((lax.axis_index("orb") * per) // 8 * 8, 8)

    @pl.when(step == 0)
    def _():
        def unpack(source, carry):
            found, _ = unpacked(got_ref, source, per * cells_x)
            for k in range(per):
                at = pl.ds(pl.multiple_of((source * per + k) * pitch, 8), cells_x)
                waves[at, :] = found[k * cells_x : (k + 1) * cells_x]
            return carry

        lax.fori_loop(0, owners, unpack, 0, unroll=4)
        sums_ref[...] = kin_ref[...]

    def columns(i, carry):
        new = list(carry)
        for pair in range(2):
            local = 4 * i + 2 * pair
            x = step * some_x + local
            field = hartley_pair(
                dht_ref[...],
                side_by_side(
                    waves[pl.ds(x, length, stride=pitch), :],
                    waves[pl.ds(x + 1, length, stride=pitch), :],
                ),
            )
            values[pair] = field
            own = values[pair, pl.ds(first, 8), :]
            slab_ref[local] = own[:, :cells_y]
            slab_ref[local + 1] = own[:, cells_y:]
            for o in range(orbitals):
                psi = side_by_side(psi_ref[o, local], psi_ref[o, local + 1]).astype(F32)
                product = field * psi
                squares = product * psi
                squares = squares[:, :cells_y] + squares[:, cells_y:]
                new[o] = new[o] + jnp.sum(squares.reshape(length // 8, 8, cells_y), axis=0)
                back = dot(tz_ref[...], product.astype(BF16))
                row = o * length * turn_pitch + local
                turn[pl.ds(row, length, stride=turn_pitch), :] = back[:, :cells_y]
                turn[pl.ds(row + 1, length, stride=turn_pitch), :] = back[:, cells_y:]
        return tuple(new)

    zeros = jnp.zeros((8, cells_y), F32)
    energy = lax.fori_loop(0, some_x // 4, columns, (zeros,) * orbitals, unroll=2)
    for o in range(orbitals):
        sums_ref[o, 0:8] = sums_ref[o, 0:8] + energy[o]

    def turned(o, z, start, count):
        row = pl.multiple_of((o * length + z) * turn_pitch, 8) + start
        return turn[pl.ds(row, count), :]

    def rows(z, carry):
        for o in range(orbitals):
            back_ref[o, z] = turned(o, z, 0, some_x).astype(BF16)
        return carry

    lax.fori_loop(0, length, rows, 0, unroll=8)

    @pl.when(step == 0)
    def _():
        def keep(z, carry):
            for o in range(orbitals):
                head[o, z] = turned(o, z, 0, rim)
            return carry

        lax.fori_loop(0, length, keep, 0, unroll=8)

    @pl.when(step == pl.num_programs(0) - 1)
    def _():
        def send(z, carry):
            for o in range(orbitals):
                both = jnp.concatenate([turned(o, z, some_x - rim, rim), head[o, z]], axis=0)
                rim_ref[o, z] = both.astype(BF16)
            return carry

        lax.fori_loop(0, length, send, 0, unroll=8)


def field(got, psi, kin_sums, dht, tz):
    orbitals, cells_x, length, cells_y = psi.shape
    some_x = 16
    pitch = cells_x + 8
    turn_pitch = some_x + 8
    rim = 8
    return pl.pallas_call(
        functools.partial(field_kernel, pitch, turn_pitch),
        grid=(cells_x // some_x,),
        in_specs=[
            whole(got),
            pl.BlockSpec((orbitals, some_x, length, cells_y), lambda i: (0, i, 0, 0)),
            whole(kin_sums),
            whole(dht),
            whole(tz),
        ],
        out_specs=[
            pl.BlockSpec((orbitals, length, some_x, cells_y), lambda i: (0, 0, i, 0)),
            pl.BlockSpec((orbitals, length, 2 * rim, cells_y), lambda i: (0, 0, 0, 0)),
            pl.BlockSpec((some_x, 8, cells_y), lambda i: (i, 0, 0)),
            whole(kin_sums),
        ],
        out_shape=[
            jax.ShapeDtypeStruct((orbitals, length, cells_x, cells_y), BF16),
            jax.ShapeDtypeStruct((orbitals, length, 2 * rim, cells_y), BF16),
            jax.ShapeDtypeStruct((cells_x, 8, cells_y), F32),
            jax.ShapeDtypeStruct(kin_sums.shape, F32),
        ],
        scratch_shapes=[
            pltpu.VMEM((length * pitch, cells_y), F32),
            pltpu.VMEM((orbitals * length * turn_pitch, cells_y), F32),
            pltpu.VMEM((orbitals, length, rim, cells_y), F32),
            pltpu.VMEM((2, length, 2 * cells_y), F32),
        ],
        compiler_params=params(1, 30),
        name="field",
    )(got, psi, kin_sums, dht, tz)


def update_kernel(
    sums_ref, other_ref, back_ref, rim_ref, c_ref, kin_ref, tx_ref, ty_ref, out_ref, energy_ref
):
    orbital = pl.program_id(0)

    @pl.when(pl.program_id(1) == 0)
    def _():
        both = sums_ref[orbital] + other_ref[orbital]
        energy_ref[orbital] = jnp.sum(both[0:8]) / jnp.sum(both[8:16])

    energy = energy_ref[orbital]
    some_z, cells_x, cells_y = back_ref.shape[1], back_ref.shape[2], back_ref.shape[3]
    tx = tx_ref[...]
    ty = ty_ref[...]
    block = 8

    def planes(i, carry):
        z0 = i * block
        crossed = []
        for p in range(0, block, 2):
            z = z0 + p
            pair = jnp.concatenate(
                [
                    side_by_side(back_ref[0, z], back_ref[0, z + 1]),
                    side_by_side(rim_ref[0, z], rim_ref[0, z + 1]),
                ],
                axis=0,
            )
            both = dot(tx, pair).astype(BF16)
            crossed += [both[:, :cells_y], both[:, cells_y:]]
        potential = dot(jnp.concatenate(crossed, axis=0), ty)
        for p in range(block):
            z = z0 + p
            applied = potential[p * cells_x : (p + 1) * cells_x] + kin_ref[0, z]
            coeff = c_ref[0, z].astype(F32)
            out_ref[0, z] = (coeff - STEP_SIZE * (applied - energy * coeff)).astype(BF16)
        return carry

    lax.fori_loop(0, some_z // block, planes, 0, unroll=4)


def update(sums, other_sums, back, rim, c, kin, tx, ty):
    orbitals, length, cells_x, cells_y = c.shape
    chunks = 4
    part = length // chunks
    block = pl.BlockSpec((1, part, cells_x, cells_y), lambda o, j: (o, j, 0, 0))
    return pl.pallas_call(
        update_kernel,
        grid=(orbitals, chunks),
        in_specs=[
            whole(sums),
            whole(other_sums),
            block,
            pl.BlockSpec((1, part, rim.shape[2], cells_y), lambda o, j: (o, j, 0, 0)),
            block,
            block,
            whole(tx),
            whole(ty),
        ],
        out_specs=[block, pl.BlockSpec(memory_space=pltpu.SMEM)],
        out_shape=[
            jax.ShapeDtypeStruct(c.shape, BF16),
            jax.ShapeDtypeStruct((orbitals,), F32),
        ],
        compiler_params=params(2, 12),
        name="update",
    )(sums, other_sums, back, rim, c, kin, tx, ty)


def to_other(array):
    return lax.ppermute(array, "grid", [(0, 1), (1, 0)])


def to_all(blocks):
    return lax.all_to_all(blocks, "orb", split_axis=0, concat_axis=0, tiled=True)


def on_device(coefficients, occupations, slot_orbital):
    orbitals, length, cells_x, cells_y = coefficients.shape
    owners = slot_orbital.shape[0] // orbitals
    per = length // owners
    magic, trans, kin_taps = magic_pairs(), transposed_pairs(), kinetic_pairs()
    magic_line = band_periodic(length, magic)
    trans_line = band_periodic(length, trans)
    kin_line = band_periodic(length, kin_taps, -0.5)
    inside = list(range(cells_x))
    near_cells = inside + with_rims(cells_x, 0, 8)
    all_cells = near_cells + with_rims(cells_x, 8, 16)
    dht = hartley(length)
    table = jnp.asarray(split_table(dht))
    waves = curve(length)

    near = to_other(own_rims(coefficients, 0, 8, occupations))
    psi, coded = density(
        occupations,
        slot_orbital,
        coefficients,
        near,
        jnp.asarray(magic_line.T),
        jnp.asarray(band_columns(cells_x, near_cells, magic)),
        jnp.asarray(magic_line),
        table,
        owners,
    )
    got = to_all(coded)
    far = to_other(own_rims(coefficients, 8, 16, psi))
    kin, kin_sums = kinetic(
        coefficients,
        near,
        far,
        jnp.asarray(kin_line.T),
        jnp.asarray(band_columns(cells_x, all_cells, kin_taps, -0.5)),
        jnp.asarray(kin_line),
        psi,
    )
    half = slab_sum(got, per * cells_x, per, kin_sums).reshape(per, cells_x, cells_y)
    slab = lax.all_gather(half, "grid", axis=1, tiled=True)
    spread = solve(
        jnp.asarray(waves.astype(np.float32)),
        slab,
        jnp.asarray(dht),
        jnp.asarray((waves[:, None] + waves[None, :]).astype(np.float32)),
        owners,
    )
    back, back_rims, slab_field, sums = field(
        to_all(spread), psi, kin_sums, table, jnp.asarray(trans_line)
    )
    updated, energies = update(
        sums,
        to_other(sums),
        back,
        to_other(back_rims),
        coefficients,
        kin,
        jnp.asarray(band_columns(cells_x, near_cells, trans)),
        jnp.asarray(trans_line.T),
    )
    first = lax.rem(lax.axis_index("orb") * per, 8)
    potential = lax.dynamic_slice_in_dim(slab_field, first, per, 1).transpose(1, 0, 2)
    return (updated, energies, potential)


def solution(mesh):
    return jax.shard_map(
        on_device,
        mesh=mesh,
        in_specs=(P("orb", None, "grid", None), P(), P()),
        out_specs=(P("orb", None, "grid", None), P("orb"), P("orb", "grid", None)),
        check_vma=False,
    )
```

time: 217 us -> 167 us (0.77)
  Pallas kernels: 140 us -> 72.4 us
  local copies, waits for them, and re-layouts: 11.1 us -> 24 us
  blocking collectives: 48.7 us -> 40.8 us
  waiting for transfers between devices: 6.11 us -> 13.8 us
  starting transfers between devices: 7.72 us -> 14.8 us
    pallas_call x5 -> x7, Pallas kernels: 136 us -> 70.1 us  [the longest x1 24 us: density(): pl.pallas_call(functools.partial(density_kernel, first_steps, pitch), gri...]
    unnamed x13 -> x53, local copies, waits for them, and re-layouts: 4.86 us -> 24 us
    all_to_all x1, waiting for transfers between devices: 0.01 us -> 8.15 us  [to_all(): lax.all_to_all(blocks, 'orb', split_axis=0, concat_axis=0, tiled=True)]
    all_to_all x1, blocking collectives: 43.8 us -> 37.5 us  [to_all(): lax.all_to_all(blocks, 'orb', split_axis=0, concat_axis=0, tiled=True)]
    all_to_all x1, starting transfers between devices: 5.1 us -> 11.3 us  [to_all(): lax.all_to_all(blocks, 'orb', split_axis=0, concat_axis=0, tiled=True)]
    slice x2 -> x0, local copies, waits for them, and re-layouts: 3.96 us -> none  [the longest x1 2.48 us: on_device(): coefficients[:, :, cells_x - 16:]]
    pallas_call x1, Pallas kernels: 4.58 us -> 2.25 us  [solve(): pl.pallas_call(solve_kernel, in_specs=[pl.BlockSpec(memory_space=pltpu.SM...]
  transfers between devices with their start and end apart: 5 -> 5, of which waited for: 2 -> 4; matrix products, arithmetic and copies ran while one was open for 1% -> 0% of each run, Pallas kernels for 17% -> 10%
where the time goes in v2:
time: 167 us
  Pallas kernels  72.4 us (43%)
  blocking collectives  40.8 us (24%)
  local copies, waits for them, and re-layouts  24 us (14%)
  starting transfers between devices  14.8 us (9%)
  waiting for transfers between devices  13.8 us (8%)
    all_to_all x1, blocking collectives, to_all(): lax.all_to_all(blocks, 'orb', split_axis=0, concat_axis=0, tiled=True)  37.5 us
    pallas_call x1, Pallas kernels, density(): pl.pallas_call(functools.partial(density_kernel, first_steps, pitch), gri...  24 us
    unnamed x53, local copies, waits for them, and re-layouts  24 us
    pallas_call x1, Pallas kernels, kinetic(): pl.pallas_call(functools.partial(kinetic_kernel, pitch), grid=(orbitals,)...  17.3 us
    pallas_call x1, Pallas kernels, field(): pl.pallas_call(functools.partial(field_kernel, pitch, turn_pitch), grid=(...  13.5 us
    all_to_all x1, starting transfers between devices, to_all(): lax.all_to_all(blocks, 'orb', split_axis=0, concat_axis=0, tiled=True)  11.3 us
    pallas_call x1, Pallas kernels, update(): pl.pallas_call(update_kernel, grid=(orbitals, chunks), in_specs=[whole(su...  9.82 us
    all_to_all x1, waiting for transfers between devices, to_all(): lax.all_to_all(blocks, 'orb', split_axis=0, concat_axis=0, tiled=True)  8.15 us
  transfers between devices with their start and end apart: 5, of which 4 were waited for; matrix products, arithmetic and copies ran while one was open for 0% of the time, Pallas kernels for 10%

profile of v2, /device:TPU:1, one launch (start us, length us, event | category | flops | bytes accessed | tf_op | source)
XLA Modules:
  0.0 166.6 jit_solution(788652453701724918)
XLA Ops:
  0.6 0.0 copy-start
  0.6 2.8 %copy-done = bf16[3,128,64,128]{3,2,1,0:T(8,128)(2,1)S(1)} copy-done((bf16[3,128,64,128]{3,2,1,0:T(8,128)(2,1)S(1)}, bf16[3,128,64,128]{3,2,1,0:T(8,128)(2,1)}, u32[]{:S(2)}) %copy-start) | copy-done | bytes 6291480
  3.4 0.7 copy-done.20
  4.1 0.0 copy-start.19
  4.1 0.0 copy-start.21
  4.1 0.0 copy-start.22
  4.1 0.9 own_rims.2
  5.0 1.5 collective-permute-start
  6.5 3.0 %collective-permute-done.h_ref.near_ref = bf16[3,128,16,128]{3,2,1,0:T(8,128)(2,1)S(1)} collective-permute-done((bf16[3,128,16,128]{3,2,1,0:T(8,128)(2,1)S(1)}, bf16[3,128,16,128]{3,2,1,0:T(8,128)(2,1)S(1)}, u32[]{:S(2)}, u32[]{:S(2)}) %collective-permute-start) | collective-permute-done | bytes 1572896 | tf_op jit(solution)/shard_map/ppermute | solution.py:746
  9.6 0.0 copy-done.1
  9.6 0.0 copy-done.13
  9.6 0.0 copy-done.14
  9.6 0.0 copy-done.15
  9.6 0.0 copy-done.19
  9.6 0.0 copy-done.21
  9.6 0.0 copy-done.22
  9.6 0.0 copy-start.11
  9.6 24.0 %density.1 = (bf16[3,64,128,128]{3,2,1,0:T(8,128)(2,1)S(1)}, s16[64,144,128]{2,1,0:T(8,128)(2,1)S(1)}) custom-call(s32[192]{0:T(256)S(1)} %copy-done.21, s32[192]{0:T(256)S(1)} %copy-done.22, bf16[3,128,64,128]{3,2,1,0:T(8,128)(2,1)S(1)} %copy-done.1, bf16[3,128,16,128]{3,2,1,0:T(8,128)(2,1)S(1)} %collective-permute-done.h_ref.near_ref, ...), custom_call_target="tpu_custom_call" | custom-call | tf_op jit(solution)/shard_map/density/pallas_call | solution.py:311
  33.6 0.0 copy-done.11
  33.6 0.0 copy-start.4
  33.6 3.9 %own_rims.3 = bf16[3,128,16,128]{3,2,1,0:T(8,128)(2,1)} custom-call(bf16[3,128,64,128]{3,2,1,0:T(8,128)(2,1)S(1)} %copy-done.1, bf16[3,128,64,128]{3,2,1,0:T(8,128)(2,1)S(1)} %copy-done.1, bf16[3,64,128,128]{3,2,1,0:T(8,128)(2,1)S(1)} %get-tuple-element.14.after_ref.psi_ref), custom_call_target="tpu_custom_call" | custom-call | tf_op jit(solution)/shard_map/own_rims/pallas_call | solution.py:174
  37.5 0.4 collective-permute-start.1
  37.9 11.3 %all-to-all-start = ((s16[64,144,128]{2,1,0:T(8,128)(2,1)}), s16[64,144,128]{2,1,0:T(8,128)(2,1)S(1)}, u32[]{:S(2)}, u32[]{:S(2)}) async-start(s16[64,144,128]{2,1,0:T(8,128)(2,1)} %copy-done.10), calls=%async_computation | async-start | bytes 4718592 | tf_op jit(solution)/shard_map/all_to_all | solution.py:750
  49.2 0.0 collective-permute-done.1.far_ref
  49.3 0.0 copy-start.2
  49.3 2.8 %copy-done.2 = bf16[3,128,64,128]{3,2,1,0:T(8,128)(2,1)S(1)} copy-done((bf16[3,128,64,128]{3,2,1,0:T(8,128)(2,1)S(1)}, bf16[3,128,64,128]{3,2,1,0:T(8,128)(2,1)}, u32[]{:S(2)}) %copy-start.2) | copy-done | bytes 6291480
  52.1 2.8 %copy-done.5 = bf16[3,64,128,128]{3,2,1,0:T(8,128)(2,1)S(1)} copy-done((bf16[3,64,128,128]{3,2,1,0:T(8,128)(2,1)S(1)}, bf16[3,64,128,128]{3,2,1,0:T(8,128)(2,1)}, u32[]{:S(2)}) %copy-start.5) | copy-done | bytes 6291480
  54.8 1.4 copy-done.12
  56.2 17.3 %kinetic.1 = (f32[3,128,64,128]{3,2,1,0:T(8,128)}, f32[3,16,128]{2,1,0:T(8,128)S(1)}) custom-call(bf16[3,128,64,128]{3,2,1,0:T(8,128)(2,1)S(1)} %copy-done.2, bf16[3,128,16,128]{3,2,1,0:T(8,128)(2,1)S(1)} %copy-done.12, bf16[3,128,16,128]{3,2,1,0:T(8,128)(2,1)} %collective-permute-done.1.far_ref, bf16[128,128]{1,0:T(8,128)(2,1)S(1)} %copy-done.24, ...), custom_call_target="tpu_custom_call" | custom-call | flops 9663676416 | bytes 22020096 | tf_op jit(solution)/shard_map/kinetic/pallas_call | solution.py:416
  73.5 8.1 %all-to-all-done.got_ref = s16[64,144,128]{2,1,0:T(8,128)(2,1)S(1)} async-done(((s16[64,144,128]{2,1,0:T(8,128)(2,1)}), s16[64,144,128]{2,1,0:T(8,128)(2,1)S(1)}, u32[]{:S(2)}, u32[]{:S(2)}) %all-to-all-start) | async-done | bytes 2359328 | tf_op jit(solution)/shard_map/all_to_all | solution.py:750
  81.7 0.9 slab_sum.1
  82.5 3.3 %all_gather.3.slab_ref = f32[2,128,128]{2,1,0:T(8,128)S(1)} all-gather(f32[2,64,128]{2,1,0:T(8,128)S(1)} %bitcast.3), channel_id=1, replica_groups=mesh['orb'=64,'grid'=2] {'grid'}, dimensions={1}, use_global_device_ids=true | all-gather | bytes 196608 | tf_op jit(solution)/shard_map/all_gather | solution.py:792
  85.8 0.0 copy-done.16
  85.8 0.0 copy-done.23
  85.8 2.2 %solve.1 = s16[64,144,128]{2,1,0:T(8,128)(2,1)S(1)} custom-call(f32[128]{0:T(128)S(1)} %copy-done.23, f32[2,128,128]{2,1,0:T(8,128)S(1)} %all_gather.3.slab_ref, f32[128,128]{1,0:T(8,128)S(1)} %copy-done.16, f32[128,128]{1,0:T(8,128)S(1)} %copy-done.17), custom_call_target="tpu_custom_call" | custom-call | tf_op jit(solution)/shard_map/solve/pallas_call | solution.py:527
  88.1 37.5 %all_to_all.10.got_ref = s16[64,144,128]{2,1,0:T(8,128)(2,1)S(1)} all-to-all(s16[64,144,128]{2,1,0:T(8,128)(2,1)S(1)} %solve.1), channel_id=1, replica_groups=mesh['orb'=64,'grid'=2] {'orb'}, dimensions={0} | all-to-all | bytes 4718592 | tf_op jit(solution)/shard_map/all_to_all | solution.py:750
  125.6 13.5 %field.1 = (bf16[3,128,64,128]{3,2,1,0:T(8,128)(2,1)S(1)}, bf16[3,128,16,128]{3,2,1,0:T(8,128)(2,1)}, f32[64,8,128]{2,1,0:T(8,128)S(1)}, f32[3,16,128]{2,1,0:T(8,128)S(1)}) custom-call(s16[64,144,128]{2,1,0:T(8,128)(2,1)S(1)} %all_to_all.10.got_ref, bf16[3,64,128,128]{3,2,1,0:T(8,128)(2,1)S(1)} %copy-done.6, ...), custom_call_target="tpu_custom_call" | custom-call | tf_op jit(solution)/shard_map/field/pallas_call | solution.py:643
  139.1 2.7 %copy-done.8 = bf16[3,128,64,128]{3,2,1,0:T(8,128)(2,1)} copy-done((bf16[3,128,64,128]{3,2,1,0:T(8,128)(2,1)}, bf16[3,128,64,128]{3,2,1,0:T(8,128)(2,1)S(1)}, u32[]{:S(2)}) %copy-start.8) | copy-done | bytes 6291480
  141.8 1.6 collective-permute-start.3
  143.3 0.0 collective-permute-start.2
  143.3 0.6 copy.19
  144.0 2.3 %collective-permute-done.2.other_ref = f32[3,16,128]{2,1,0:T(8,128)S(1)} collective-permute-done((f32[3,16,128]{2,1,0:T(8,128)S(1)}, f32[3,16,128]{2,1,0:T(8,128)S(1)}, u32[]{:S(2)}, u32[]{:S(2)}) %collective-permute-start.2) | collective-permute-done | bytes 24608 | tf_op jit(solution)/shard_map/ppermute | solution.py:746
  146.3 0.3 collective-permute-done.3.rim_ref
  146.6 0.0 copy-done.18
  146.6 2.8 %copy-done.3 = bf16[3,128,64,128]{3,2,1,0:T(8,128)(2,1)S(1)} copy-done((bf16[3,128,64,128]{3,2,1,0:T(8,128)(2,1)S(1)}, bf16[3,128,64,128]{3,2,1,0:T(8,128)(2,1)}, u32[]{:S(2)}) %copy-start.3) | copy-done | bytes 6291480
  149.4 4.6 %copy-done.7 = f32[3,128,64,128]{3,2,1,0:T(8,128)S(1)} copy-done((f32[3,128,64,128]{3,2,1,0:T(8,128)S(1)}, f32[3,128,64,128]{3,2,1,0:T(8,128)}, u32[]{:S(2)}) %copy-start.7) | copy-done | bytes 12582936
  154.0 2.8 %copy-done.9 = bf16[3,128,64,128]{3,2,1,0:T(8,128)(2,1)S(1)} copy-done((bf16[3,128,64,128]{3,2,1,0:T(8,128)(2,1)S(1)}, bf16[3,128,64,128]{3,2,1,0:T(8,128)(2,1)}, u32[]{:S(2)}) %copy-start.9) | copy-done | bytes 6291480
  156.7 9.8 %update.1 = (bf16[3,128,64,128]{3,2,1,0:T(8,128)(2,1)}, f32[3]{0:T(128)}) custom-call(f32[3,16,128]{2,1,0:T(8,128)S(1)} %get-tuple-element.16.sums_ref, f32[3,16,128]{2,1,0:T(8,128)S(1)} %collective-permute-done.2.other_ref, bf16[3,128,64,128]{3,2,1,0:T(8,128)(2,1)S(1)} %copy-done.9, bf16[3,128,16,128]{3,2,1,0:T(8,128)(2,1)S(1)} %collective-permute-done.3.rim_ref, ...), custom_call_target="tpu_custom_call" | custom-call | tf_op jit(solution)/shard_map/update/pallas_call | solution.py:722
  (26 shorter events, 0.1 us)
Async XLA Ops:
  0.6 2.8 %copy-start = (bf16[3,128,64,128]{3,2,1,0:T(8,128)(2,1)S(1)}, bf16[3,128,64,128]{3,2,1,0:T(8,128)(2,1)}, u32[]{:S(2)}) copy-start(bf16[3,128,64,128]{3,2,1,0:T(8,128)(2,1)} %c_ref.5) | copy-start | bytes 18874372
  3.4 0.7 copy-start.20
  4.1 5.5 %copy-start.1 = (bf16[3,128,64,128]{3,2,1,0:T(8,128)(2,1)S(1)}, bf16[3,128,64,128]{3,2,1,0:T(8,128)(2,1)}, u32[]{:S(2)}) copy-start(bf16[3,128,64,128]{3,2,1,0:T(8,128)(2,1)} %c_ref.5) | copy-start | bytes 18874372
  4.1 5.5 %copy-start.13 = (bf16[128,256]{1,0:T(8,128)(2,1)S(1)}, bf16[128,256]{1,0:T(8,128)(2,1)}, u32[]{:S(2)}) copy-start(bf16[128,256]{1,0:T(8,128)(2,1)} %constant.35.clone.dht_ref) | copy-start | bytes 196612
  4.1 5.5 %copy-start.14 = (bf16[128,128]{1,0:T(8,128)(2,1)S(1)}, bf16[128,128]{1,0:T(8,128)(2,1)}, u32[]{:S(2)}) copy-start(bf16[128,128]{1,0:T(8,128)(2,1)} %constant.38.clone.mz_ref.ty_ref) | copy-start | bytes 98308
  4.1 5.5 %copy-start.15 = (bf16[128,128]{1,0:T(8,128)(2,1)S(1)}, bf16[128,128]{1,0:T(8,128)(2,1)}, u32[]{:S(2)}) copy-start(bf16[128,128]{1,0:T(8,128)(2,1)} %constant.36.clone.my_ref.tz_ref) | copy-start | bytes 98308
  4.1 5.5 %copy-start.19 = (bf16[64,80]{1,0:T(8,128)(2,1)S(1)}, bf16[64,80]{1,0:T(8,128)(2,1)}, u32[]{:S(2)}) copy-start(bf16[64,80]{1,0:T(8,128)(2,1)} %constant.37.clone.ax_ref) | copy-start | bytes 30724
  4.1 5.5 %copy-start.21 = (s32[192]{0:T(256)S(1)}, s32[192]{0:T(256)}, u32[]{:S(2)}) copy-start(s32[192]{0:T(256)} %occ_ref.1) | copy-start | bytes 2308
  4.1 5.5 %copy-start.22 = (s32[192]{0:T(256)S(1)}, s32[192]{0:T(256)}, u32[]{:S(2)}) copy-start(s32[192]{0:T(256)} %slot_ref.1) | copy-start | bytes 2308
  5.0 4.5 %collective-permute-start = (bf16[3,128,16,128]{3,2,1,0:T(8,128)(2,1)S(1)}, bf16[3,128,16,128]{3,2,1,0:T(8,128)(2,1)S(1)}, u32[]{:S(2)}, u32[]{:S(2)}) collective-permute-start(bf16[3,128,16,128]{3,2,1,0:T(8,128)(2,1)S(1)} %own_rims.2), channel_id=1, source_target_pairs={{0,1},{1,0},{2,3},{3,2},{4,5},{5,4},{6,7},{7,6},{8,9},{9,8},{10,11... | collective-permute-start | bytes 4718600 | tf_op jit(solution)/shard_map/ppermute | solution.py:746
  9.6 24.0 %copy-start.11 = (bf16[3,128,16,128]{3,2,1,0:T(8,128)(2,1)}, bf16[3,128,16,128]{3,2,1,0:T(8,128)(2,1)S(1)}, u32[]{:S(2)}) copy-start(bf16[3,128,16,128]{3,2,1,0:T(8,128)(2,1)S(1)} %collective-permute-done.h_ref.near_ref) | copy-start | bytes 4718596
  33.6 3.9 %copy-start.4 = (bf16[3,64,128,128]{3,2,1,0:T(8,128)(2,1)}, bf16[3,64,128,128]{3,2,1,0:T(8,128)(2,1)S(1)}, u32[]{:S(2)}) copy-start(bf16[3,64,128,128]{3,2,1,0:T(8,128)(2,1)S(1)} %get-tuple-element.14.after_ref.psi_ref) | copy-start | bytes 18874372
  33.6 3.9 %copy-start.10 = (s16[64,144,128]{2,1,0:T(8,128)(2,1)}, s16[64,144,128]{2,1,0:T(8,128)(2,1)S(1)}, u32[]{:S(2)}) copy-start(s16[64,144,128]{2,1,0:T(8,128)(2,1)S(1)} %get-tuple-element.13) | copy-start | bytes 7077892
  37.5 11.7 %collective-permute-start.1 = (bf16[3,128,16,128]{3,2,1,0:T(8,128)(2,1)}, bf16[3,128,16,128]{3,2,1,0:T(8,128)(2,1)}, u32[]{:S(2)}, u32[]{:S(2)}) collective-permute-start(bf16[3,128,16,128]{3,2,1,0:T(8,128)(2,1)} %own_rims.3), channel_id=1, source_target_pairs={{0,1},{1,0},{2,3},{3,2},{4,5},{5,4},{6,7},{7,6},{8,9},{9,8},{10,11... | collective-permute-start | bytes 4718600 | tf_op jit(solution)/shard_map/ppermute | solution.py:746
  37.9 11.4 %copy-start.24 = (bf16[128,128]{1,0:T(8,128)(2,1)S(1)}, bf16[128,128]{1,0:T(8,128)(2,1)}, u32[]{:S(2)}) copy-start(bf16[128,128]{1,0:T(8,128)(2,1)} %constant.39.clone.dy_ref.dz_ref) | copy-start | bytes 98308
  37.9 11.4 %copy-start.25 = (bf16[64,96]{1,0:T(8,128)(2,1)S(1)}, bf16[64,96]{1,0:T(8,128)(2,1)}, u32[]{:S(2)}) copy-start(bf16[64,96]{1,0:T(8,128)(2,1)} %constant.40.clone.dx_ref) | copy-start | bytes 36868
  37.9 43.8 %all-to-all-start = ((s16[64,144,128]{2,1,0:T(8,128)(2,1)}), s16[64,144,128]{2,1,0:T(8,128)(2,1)S(1)}, u32[]{:S(2)}, u32[]{:S(2)}) async-start(s16[64,144,128]{2,1,0:T(8,128)(2,1)} %copy-done.10), calls=%async_computation | async-start | bytes 4718592 | tf_op jit(solution)/shard_map/all_to_all | solution.py:750
  49.3 2.8 %copy-start.2 = (bf16[3,128,64,128]{3,2,1,0:T(8,128)(2,1)S(1)}, bf16[3,128,64,128]{3,2,1,0:T(8,128)(2,1)}, u32[]{:S(2)}) copy-start(bf16[3,128,64,128]{3,2,1,0:T(8,128)(2,1)} %c_ref.5) | copy-start | bytes 18874372
  52.1 2.8 %copy-start.5 = (bf16[3,64,128,128]{3,2,1,0:T(8,128)(2,1)S(1)}, bf16[3,64,128,128]{3,2,1,0:T(8,128)(2,1)}, u32[]{:S(2)}) copy-start(bf16[3,64,128,128]{3,2,1,0:T(8,128)(2,1)} %copy-done.4) | copy-start | bytes 18874372
  54.8 1.4 copy-start.12
  73.5 12.3 %copy-start.16 = (f32[128,128]{1,0:T(8,128)S(1)}, f32[128,128]{1,0:T(8,128)}, u32[]{:S(2)}) copy-start(f32[128,128]{1,0:T(8,128)} %constant.42.clone.dht_ref) | copy-start | bytes 196612
  73.5 12.3 %copy-start.17 = (f32[128,128]{1,0:T(8,128)S(1)}, f32[128,128]{1,0:T(8,128)}, u32[]{:S(2)}) copy-start(f32[128,128]{1,0:T(8,128)} %constant.43.clone.curve_ref) | copy-start | bytes 196612
  73.5 12.3 %copy-start.23 = (f32[128]{0:T(128)S(1)}, f32[128]{0:T(128)}, u32[]{:S(2)}) copy-start(f32[128]{0:T(128)} %constant.41.clone.curve_z_ref) | copy-start | bytes 1540
  85.8 39.8 %copy-start.6 = (bf16[3,64,128,128]{3,2,1,0:T(8,128)(2,1)S(1)}, bf16[3,64,128,128]{3,2,1,0:T(8,128)(2,1)}, u32[]{:S(2)}) copy-start(bf16[3,64,128,128]{3,2,1,0:T(8,128)(2,1)} %copy-done.4) | copy-start | bytes 18874372
  125.6 21.0 %copy-start.18 = (bf16[64,80]{1,0:T(8,128)(2,1)S(1)}, bf16[64,80]{1,0:T(8,128)(2,1)}, u32[]{:S(2)}) copy-start(bf16[64,80]{1,0:T(8,128)(2,1)} %constant.44.clone.tx_ref) | copy-start | bytes 30724
  139.1 2.7 %copy-start.8 = (bf16[3,128,64,128]{3,2,1,0:T(8,128)(2,1)}, bf16[3,128,64,128]{3,2,1,0:T(8,128)(2,1)S(1)}, u32[]{:S(2)}) copy-start(bf16[3,128,64,128]{3,2,1,0:T(8,128)(2,1)S(1)} %get-tuple-element.17.back_ref) | copy-start | bytes 18874372
  141.8 4.8 %collective-permute-start.3 = (bf16[3,128,16,128]{3,2,1,0:T(8,128)(2,1)}, bf16[3,128,16,128]{3,2,1,0:T(8,128)(2,1)S(1)}, u32[]{:S(2)}, u32[]{:S(2)}) collective-permute-start(bf16[3,128,16,128]{3,2,1,0:T(8,128)(2,1)} %get-tuple-element.18), channel_id=1, source_target_pairs={{0,1},{1,0},{2,3},{3,2},{4,5},{5,4},{6,7},{7,6},{8,9},{9,8},{10,11... | collective-permute-start | bytes 4718600 | tf_op jit(solution)/shard_map/ppermute | solution.py:746
  143.3 2.9 %collective-permute-start.2 = (f32[3,16,128]{2,1,0:T(8,128)S(1)}, f32[3,16,128]{2,1,0:T(8,128)S(1)}, u32[]{:S(2)}, u32[]{:S(2)}) collective-permute-start(f32[3,16,128]{2,1,0:T(8,128)S(1)} %get-tuple-element.16.sums_ref), channel_id=1, source_target_pairs={{0,1},{1,0},{2,3},{3,2},{4,5},{5,4},{6,7},{7,6},{8,9},{9,8},{10,11... | collective-permute-start | bytes 73736 | tf_op jit(solution)/shard_map/ppermute | solution.py:746
  146.6 2.8 %copy-start.3 = (bf16[3,128,64,128]{3,2,1,0:T(8,128)(2,1)S(1)}, bf16[3,128,64,128]{3,2,1,0:T(8,128)(2,1)}, u32[]{:S(2)}) copy-start(bf16[3,128,64,128]{3,2,1,0:T(8,128)(2,1)} %c_ref.5) | copy-start | bytes 18874372
  149.4 4.6 %copy-start.7 = (f32[3,128,64,128]{3,2,1,0:T(8,128)S(1)}, f32[3,128,64,128]{3,2,1,0:T(8,128)}, u32[]{:S(2)}) copy-start(f32[3,128,64,128]{3,2,1,0:T(8,128)} %get-tuple-element.19.kin_ref) | copy-start | bytes 37748740
  154.0 2.8 %copy-start.9 = (bf16[3,128,64,128]{3,2,1,0:T(8,128)(2,1)S(1)}, bf16[3,128,64,128]{3,2,1,0:T(8,128)(2,1)}, u32[]{:S(2)}) copy-start(bf16[3,128,64,128]{3,2,1,0:T(8,128)(2,1)} %copy-done.8) | copy-start | bytes 18874372

commit v3 on v2

--- a/solution.py
+++ b/solution.py
@@ -195,16 +195,18 @@
     dht_ref,
     psi_ref,
     q_ref,
+    peak,
     mid,
     waves,
-    peak,
     level,
 ):
     step = pl.program_id(0)
     cells_z, cells_x, cells_y = c_ref.shape[1], c_ref.shape[2], c_ref.shape[3]
     rim = h_ref.shape[2]
     orbitals, some_x, length = psi_ref.shape[0], psi_ref.shape[1], psi_ref.shape[2]
-    block = 8
+    block = 64
+    many = 8
+    group = 8
 
     @pl.when(step < first_steps)
     def _():
@@ -217,38 +219,42 @@
             own = own.astype(BF16).reshape(block, cells_x, cells_y)
             far = dot(h_ref[0, pl.ds(z0, block)].reshape(block * rim, cells_y), my)
             far = far.astype(BF16).reshape(block, rim, cells_y)
-            for p in range(0, block, 2):
-                pair = jnp.concatenate(
-                    [side_by_side(own[p], own[p + 1]), side_by_side(far[p], far[p + 1])], axis=0
+            for p in range(0, block, many):
+                some = range(p, p + many)
+                flat = jnp.concatenate(
+                    [
+                        jnp.concatenate([own[z] for z in some], axis=1),
+                        jnp.concatenate([far[z] for z in some], axis=1),
+                    ],
+                    axis=0,
                 )
-                both = dot(ax, pair)
-                row = pl.multiple_of((step * cells_z + z0 + p) * pitch, 8)
-                mid[pl.ds(row, cells_x), :] = both[:, :cells_y]
-                mid[pl.ds(row + pitch, cells_x), :] = both[:, cells_y:]
+                crossed = dot(ax, flat)
+                for k in range(many):
+                    row = pl.multiple_of((step * cells_z + z0 + p + k) * pitch, 8)
+                    mid[pl.ds(row, cells_x), :] = crossed[:, k * cells_y : (k + 1) * cells_y]
             return carry
 
-        lax.fori_loop(0, cells_z // block, planes, 0, unroll=4)
-
-    def grid_values(x):
+        lax.fori_loop(0, cells_z // block, planes, 0)
+
+    def grid_values(x, count):
         first = lax.axis_index("orb") * orbitals
-        total = jnp.zeros((length, 2 * cells_y), F32)
-        kept = []
+        columns = [
+            mid[pl.ds(o * length * pitch + x + k, length, stride=pitch), :].astype(BF16)
+            for o in range(orbitals)
+            for k in range(count)
+        ]
+        values = dot(mz_ref[...], jnp.concatenate(columns, axis=1)).astype(BF16)
+        total = None
         for o in range(orbitals):
             weight = occ_ref[slot_ref[first + o]].astype(F32) / slot_ref.shape[0]
-            row = o * length * pitch + x
-            pair = side_by_side(
-                mid[pl.ds(row, length, stride=pitch), :].astype(BF16),
-                mid[pl.ds(row + 1, length, stride=pitch), :].astype(BF16),
-            )
-            values = dot(mz_ref[...], pair).astype(BF16)
-            kept.append(values)
-            wide = values.astype(F32)
-            total = total + weight * (wide * wide)
-        return kept, total
+            wide = values[:, o * count * cells_y : (o + 1) * count * cells_y].astype(F32)
+            part = weight * (wide * wide)
+            total = part if total is None else total + part
+        return values, total
 
     @pl.when(step == first_steps)
     def _():
-        _, total = grid_values(0)
+        _, total = grid_values(0, 2)
         code, fine, top = scale_of(jnp.sum(total) / total.size)
         level[0] = code
         level[1] = fine
@@ -261,17 +267,18 @@
         mean = level[2]
         table = dht_ref[...]
         largest = peak[...]
-        for local in range(0, some_x, 2):
-            kept, total = grid_values(x0 + local)
+        for local in range(0, some_x, group):
+            values, total = grid_values(x0 + local, group)
             for o in range(orbitals):
-                psi_ref[o, local] = kept[o][:, :cells_y]
-                psi_ref[o, local + 1] = kept[o][:, cells_y:]
+                for k in range(group):
+                    at = (o * group + k) * cells_y
+                    psi_ref[o, local + k] = values[:, at : at + cells_y]
             result = hartley_pair(table, total - mean)
-            waves[pl.ds(x0 + local, length, stride=pitch), :] = result[:, :cells_y]
-            waves[pl.ds(x0 + local + 1, length, stride=pitch), :] = result[:, cells_y:]
-            size = jnp.abs(result)
-            size = jnp.maximum(size[:, :cells_y], size[:, cells_y:])
-            largest = jnp.maximum(largest, jnp.max(size.reshape(length // 8, 8, cells_y), axis=0))
+            for k in range(group):
+                part = result[:, k * cells_y : (k + 1) * cells_y]
+                waves[pl.ds(x0 + local + k, length, stride=pitch), :] = part
+                size = jnp.abs(part).reshape(length // 8, 8, cells_y)
+                largest = jnp.maximum(largest, jnp.max(size, axis=0))
         peak[...] = largest
 
     @pl.when(step == pl.num_programs(0) - 1)
@@ -296,7 +303,7 @@
 
 def density(occupations, slot_orbital, c, halo, my, ax, mz, dht, owners):
     orbitals, length, cells_x, cells_y = c.shape
-    chunks = 4
+    chunks = 2
     part = length // chunks
     first_steps = orbitals * chunks
     some_x = 8
@@ -327,18 +334,19 @@
                 lambda s: (0, jnp.maximum(s - first_steps, 0), 0, 0),
             ),
             pl.BlockSpec((owners, rows, cells_y), lambda s: (0, 0, 0)),
+            pl.BlockSpec((8, cells_y), lambda s: (0, 0)),
         ],
         out_shape=[
-            jax.ShapeDtypeStruct((orbitals, cells_x, length, cells_y), BF16),
-            jax.ShapeDtypeStruct((owners, rows, cells_y), jnp.int16),
+            pltpu.HBM((orbitals, cells_x, length, cells_y), BF16),
+            pltpu.HBM((owners, rows, cells_y), jnp.int16),
+            jax.ShapeDtypeStruct((8, cells_y), F32),
         ],
         scratch_shapes=[
             pltpu.VMEM((orbitals * length * pitch, cells_y), F32),
             pltpu.VMEM((length * pitch, cells_y), F32),
-            pltpu.VMEM((8, cells_y), F32),
             pltpu.SMEM((3,), F32),
         ],
-        compiler_params=params(1, 34),
+        compiler_params=params(1, 30),
         name="density",
     )(occupations, slot_orbital, c, halo, my, ax, mz, dht)
 
@@ -427,14 +435,14 @@
         ],
         out_specs=[block(c), pl.BlockSpec((1, 16, cells_y), lambda o: (o, 0, 0))],
         out_shape=[
-            jax.ShapeDtypeStruct(c.shape, F32),
+            pltpu.HBM(c.shape, F32),
             jax.ShapeDtypeStruct((orbitals, 16, cells_y), F32),
         ],
         scratch_shapes=[
             pltpu.VMEM((length * pitch, cells_y), F32),
             pltpu.VMEM((length * pitch, cells_y), F32),
         ],
-        compiler_params=params(1, 30),
+        compiler_params=params(1, 26),
         cost_estimate=pl.CostEstimate(
             flops=cells * 768 * 4, bytes_accessed=cells * 7, transcendentals=0
         ),
@@ -570,36 +578,38 @@
         lax.fori_loop(0, owners, unpack, 0, unroll=4)
         sums_ref[...] = kin_ref[...]
 
-    def columns(i, carry):
-        new = list(carry)
-        for pair in range(2):
-            local = 4 * i + 2 * pair
-            x = step * some_x + local
-            field = hartley_pair(
-                dht_ref[...],
-                side_by_side(
-                    waves[pl.ds(x, length, stride=pitch), :],
-                    waves[pl.ds(x + 1, length, stride=pitch), :],
-                ),
-            )
-            values[pair] = field
-            own = values[pair, pl.ds(first, 8), :]
-            slab_ref[local] = own[:, :cells_y]
-            slab_ref[local + 1] = own[:, cells_y:]
-            for o in range(orbitals):
-                psi = side_by_side(psi_ref[o, local], psi_ref[o, local + 1]).astype(F32)
-                product = field * psi
-                squares = product * psi
-                squares = squares[:, :cells_y] + squares[:, cells_y:]
-                new[o] = new[o] + jnp.sum(squares.reshape(length // 8, 8, cells_y), axis=0)
-                back = dot(tz_ref[...], product.astype(BF16))
-                row = o * length * turn_pitch + local
-                turn[pl.ds(row, length, stride=turn_pitch), :] = back[:, :cells_y]
-                turn[pl.ds(row + 1, length, stride=turn_pitch), :] = back[:, cells_y:]
-        return tuple(new)
-
-    zeros = jnp.zeros((8, cells_y), F32)
-    energy = lax.fori_loop(0, some_x // 4, columns, (zeros,) * orbitals, unroll=2)
+    group = 8
+    energy = [jnp.zeros((8, cells_y), F32) for _ in range(orbitals)]
+    for local in range(0, some_x, group):
+        x = step * some_x + local
+        field = hartley_pair(
+            dht_ref[...],
+            jnp.concatenate(
+                [waves[pl.ds(x + k, length, stride=pitch), :] for k in range(group)], axis=1
+            ),
+        )
+        values[local // group] = field
+        own = values[local // group, pl.ds(first, 8), :]
+        for k in range(group):
+            slab_ref[local + k] = own[:, k * cells_y : (k + 1) * cells_y]
+        products = []
+        for o in range(orbitals):
+            psi = jnp.concatenate([psi_ref[o, local + k] for k in range(group)], axis=1)
+            psi = psi.astype(F32)
+            product = field * psi
+            products.append(product.astype(BF16))
+            squares = product * psi
+            for k in range(group):
+                part = squares[:, k * cells_y : (k + 1) * cells_y]
+                part = part.reshape(length // 8, 8, cells_y)
+                energy[o] = energy[o] + jnp.sum(part, axis=0)
+        back = dot(tz_ref[...], jnp.concatenate(products, axis=1))
+        for o in range(orbitals):
+            for k in range(group):
+                at = (o * group + k) * cells_y
+                row = o * length * turn_pitch + local + k
+                turn[pl.ds(row, length, stride=turn_pitch), :] = back[:, at : at + cells_y]
+
     for o in range(orbitals):
         sums_ref[o, 0:8] = sums_ref[o, 0:8] + energy[o]
 
@@ -644,7 +654,7 @@
         functools.partial(field_kernel, pitch, turn_pitch),
         grid=(cells_x // some_x,),
         in_specs=[
-            whole(got),
+            pl.BlockSpec(memory_space=pltpu.VMEM),
             pl.BlockSpec((orbitals, some_x, length, cells_y), lambda i: (0, i, 0, 0)),
             whole(kin_sums),
             whole(dht),
@@ -657,7 +667,7 @@
             whole(kin_sums),
         ],
         out_shape=[
-            jax.ShapeDtypeStruct((orbitals, length, cells_x, cells_y), BF16),
+            pltpu.HBM((orbitals, length, cells_x, cells_y), BF16),
             jax.ShapeDtypeStruct((orbitals, length, 2 * rim, cells_y), BF16),
             jax.ShapeDtypeStruct((cells_x, 8, cells_y), F32),
             jax.ShapeDtypeStruct(kin_sums.shape, F32),
@@ -666,9 +676,9 @@
             pltpu.VMEM((length * pitch, cells_y), F32),
             pltpu.VMEM((orbitals * length * turn_pitch, cells_y), F32),
             pltpu.VMEM((orbitals, length, rim, cells_y), F32),
-            pltpu.VMEM((2, length, 2 * cells_y), F32),
-        ],
-        compiler_params=params(1, 30),
+            pltpu.VMEM((2, length, 8 * cells_y), F32),
+        ],
+        compiler_params=params(1, 26),
         name="field",
     )(got, psi, kin_sums, dht, tz)
 
@@ -687,22 +697,23 @@
     some_z, cells_x, cells_y = back_ref.shape[1], back_ref.shape[2], back_ref.shape[3]
     tx = tx_ref[...]
     ty = ty_ref[...]
-    block = 8
+    block = 16
+    many = 8
 
     def planes(i, carry):
         z0 = i * block
         crossed = []
-        for p in range(0, block, 2):
-            z = z0 + p
-            pair = jnp.concatenate(
+        for p in range(0, block, many):
+            some = range(p, p + many)
+            flat = jnp.concatenate(
                 [
-                    side_by_side(back_ref[0, z], back_ref[0, z + 1]),
-                    side_by_side(rim_ref[0, z], rim_ref[0, z + 1]),
+                    jnp.concatenate([back_ref[0, z0 + k] for k in some], axis=1),
+                    jnp.concatenate([rim_ref[0, z0 + k] for k in some], axis=1),
                 ],
                 axis=0,
             )
-            both = dot(tx, pair).astype(BF16)
-            crossed += [both[:, :cells_y], both[:, cells_y:]]
+            both = dot(tx, flat).astype(BF16)
+            crossed += [both[:, k * cells_y : (k + 1) * cells_y] for k in range(many)]
         potential = dot(jnp.concatenate(crossed, axis=0), ty)
         for p in range(block):
             z = z0 + p
@@ -716,7 +727,7 @@
 
 def update(sums, other_sums, back, rim, c, kin, tx, ty):
     orbitals, length, cells_x, cells_y = c.shape
-    chunks = 4
+    chunks = 2
     part = length // chunks
     block = pl.BlockSpec((1, part, cells_x, cells_y), lambda o, j: (o, j, 0, 0))
     return pl.pallas_call(
@@ -746,6 +757,10 @@
     return lax.ppermute(array, "grid", [(0, 1), (1, 0)])
 
 
+def in_hbm(array):
+    return pltpu.with_memory_space_constraint(array, pltpu.HBM)
+
+
 def to_all(blocks):
     return lax.all_to_all(blocks, "orb", split_axis=0, concat_axis=0, tiled=True)
 
@@ -765,8 +780,10 @@
     table = jnp.asarray(split_table(dht))
     waves = curve(length)
 
-    near = to_other(own_rims(coefficients, 0, 8, occupations))
-    psi, coded = density(
+    own_near = own_rims(coefficients, 0, 8, occupations)
+    near = to_other(own_near)
+    far = to_other(own_rims(coefficients, 8, 16, own_near))
+    psi, coded, peak = density(
         occupations,
         slot_orbital,
         coefficients,
@@ -778,15 +795,14 @@
         owners,
     )
     got = to_all(coded)
-    far = to_other(own_rims(coefficients, 8, 16, psi))
     kin, kin_sums = kinetic(
-        coefficients,
+        in_hbm(coefficients),
         near,
         far,
         jnp.asarray(kin_line.T),
         jnp.asarray(band_columns(cells_x, all_cells, kin_taps, -0.5)),
         jnp.asarray(kin_line),
-        psi,
+        peak,
     )
     half = slab_sum(got, per * cells_x, per, kin_sums).reshape(per, cells_x, cells_y)
     slab = lax.all_gather(half, "grid", axis=1, tiled=True)
@@ -803,10 +819,10 @@
     updated, energies = update(
         sums,
         to_other(sums),
-        back,
+        in_hbm(back),
         to_other(back_rims),
-        coefficients,
-        kin,
+        in_hbm(coefficients),
+        in_hbm(kin),
         jnp.asarray(band_columns(cells_x, near_cells, trans)),
         jnp.asarray(trans_line.T),
     )

time: 167 us -> 142 us (0.85)
  local copies, waits for them, and re-layouts: 24 us -> 5.61 us
  Pallas kernels: 72.4 us -> 64.1 us
    unnamed x53 -> x39, local copies, waits for them, and re-layouts: 24 us -> 5.58 us
    pallas_call x1, Pallas kernels: 24 us -> 15.7 us  [density(): pl.pallas_call(functools.partial(density_kernel, first_steps, pitch), gri...]
    all_to_all x1, waiting for transfers between devices: 8.15 us -> 12.5 us  [to_all(): lax.all_to_all(blocks, 'orb', split_axis=0, concat_axis=0, tiled=True)]
    pallas_call x1, Pallas kernels: 9.82 us -> 13.7 us  [update(): pl.pallas_call(update_kernel, grid=(orbitals, chunks), in_specs=[whole(su...]
    pallas_call x1, Pallas kernels: 13.5 us -> 10.1 us  [field(): pl.pallas_call(functools.partial(field_kernel, pitch, turn_pitch), grid=(...]
    ppermute x4, waiting for transfers between devices: 5.65 us -> 2.93 us  [to_other(): return lax.ppermute(array, 'grid', [(0, 1), (1, 0)])]
  transfers between devices with their start and end apart: 5 -> 5, of which waited for: 4 -> 4; matrix products, arithmetic and copies ran while one was open for 0% -> 0% of each run, Pallas kernels for 10% -> 26%
where the time goes in v3:
time: 142 us
  Pallas kernels  64.1 us (45%)
  blocking collectives  41.5 us (29%)
  waiting for transfers between devices  15.4 us (11%)
  starting transfers between devices  14.4 us (10%)
  local copies, waits for them, and re-layouts  5.61 us (4%)
    all_to_all x1, blocking collectives, to_all(): lax.all_to_all(blocks, 'orb', split_axis=0, concat_axis=0, tiled=True)  37.9 us
    pallas_call x1, Pallas kernels, kinetic(): pl.pallas_call(functools.partial(kinetic_kernel, pitch), grid=(orbitals,)...  17.9 us
    pallas_call x1, Pallas kernels, density(): pl.pallas_call(functools.partial(density_kernel, first_steps, pitch), gri...  15.7 us
    pallas_call x1, Pallas kernels, update(): pl.pallas_call(update_kernel, grid=(orbitals, chunks), in_specs=[whole(su...  13.7 us
    all_to_all x1, waiting for transfers between devices, to_all(): lax.all_to_all(blocks, 'orb', split_axis=0, concat_axis=0, tiled=True)  12.5 us
    all_to_all x1, starting transfers between devices, to_all(): lax.all_to_all(blocks, 'orb', split_axis=0, concat_axis=0, tiled=True)  11.3 us
    pallas_call x1, Pallas kernels, field(): pl.pallas_call(functools.partial(field_kernel, pitch, turn_pitch), grid=(...  10.1 us
    unnamed x39, local copies, waits for them, and re-layouts  5.58 us
  transfers between devices with their start and end apart: 5, of which 4 were waited for; matrix products, arithmetic and copies ran while one was open for 0% of the time, Pallas kernels for 26%

profile of v3, /device:TPU:1, one launch (start us, length us, event | category | flops | bytes accessed | tf_op | source)
XLA Modules:
  0.0 142.0 jit_solution(8662333196106137272)
XLA Ops:
  0.6 0.0 copy-start
  0.6 2.8 %copy-done = bf16[3,128,64,128]{3,2,1,0:T(8,128)(2,1)S(1)} copy-done((bf16[3,128,64,128]{3,2,1,0:T(8,128)(2,1)S(1)}, bf16[3,128,64,128]{3,2,1,0:T(8,128)(2,1)}, u32[]{:S(2)}) %copy-start) | copy-done | bytes 6291480
  3.4 0.7 copy-done.11
  4.1 0.8 own_rims.2.after_ref
  5.0 0.0 slice-start.1
  5.0 0.0 copy-start.4
  5.0 0.0 copy-start.5
  5.0 0.0 copy-start.6
  5.0 0.0 copy-start.10
  5.0 0.0 copy-start.12
  5.0 0.0 copy-start.13
  5.0 1.5 %collective-permute-start = (bf16[3,128,16,128]{3,2,1,0:T(8,128)(2,1)S(1)}, bf16[3,128,16,128]{3,2,1,0:T(8,128)(2,1)S(1)}, u32[]{:S(2)}, u32[]{:S(2)}) collective-permute-start(bf16[3,128,16,128]{3,2,1,0:T(8,128)(2,1)S(1)} %own_rims.2.after_ref), channel_id=1, source_target_pairs={{0,1},{1,0},{2,3},{3,2},{4,5},{5,4},{6,7},{7,6},{8,9},{9,8},{10,11... | collective-permute-start | bytes 4718600 | tf_op jit(solution)/shard_map/ppermute | solution.py:757
  6.5 2.7 %own_rims.3 = bf16[3,128,16,128]{3,2,1,0:T(8,128)(2,1)} custom-call(bf16[3,128,64,128]{3,2,1,0:T(8,128)(2,1)S(1)} %copy-done, bf16[3,128,64,128]{3,2,1,0:T(8,128)(2,1)S(1)} %copy-done, bf16[3,128,16,128]{3,2,1,0:T(8,128)(2,1)S(1)} %own_rims.2.after_ref), custom_call_target="tpu_custom_call" | custom-call | tf_op jit(solution)/shard_map/own_rims/pallas_call | solution.py:174
  9.2 0.0 collective-permute-start.1
  9.3 0.3 collective-permute-done.h_ref.near_ref
  9.6 0.0 slice-done
  9.6 0.0 slice-done.1
  9.6 0.0 copy-done.4
  9.6 0.0 copy-done.5
  9.6 0.0 copy-done.6
  9.6 0.0 copy-done.10
  9.6 0.0 copy-done.12
  9.6 0.0 copy-done.13
  9.6 0.0 copy-start.2
  9.7 15.7 %density.1 = (bf16[3,64,128,128]{3,2,1,0:T(8,128)(2,1)}, s16[64,144,128]{2,1,0:T(8,128)(2,1)}, f32[8,128]{1,0:T(8,128)S(1)}) custom-call(s32[192]{0:T(256)S(1)} %copy-done.12, s32[192]{0:T(256)S(1)} %copy-done.13, bf16[3,128,64,128]{3,2,1,0:T(8,128)(2,1)S(1)} %bitcast.4, bf16[3,128,16,128]{3,2,1,0:T(8,128)(2,1)S(1)} %collective-permute-done.h_ref.near_ref, ...), custom_call_target="tpu_custom_call" | custom-call | tf_op jit(solution)/shard_map/density/pallas_call | solution.py:318
  25.4 0.0 copy-done.2
  25.4 0.0 copy-start.16
  25.4 11.3 %all-to-all-start = ((s16[64,144,128]{2,1,0:T(8,128)(2,1)}), s16[64,144,128]{2,1,0:T(8,128)(2,1)S(1)}, u32[]{:S(2)}, u32[]{:S(2)}) async-start(s16[64,144,128]{2,1,0:T(8,128)(2,1)} %get-tuple-element.14), calls=%async_computation | async-start | bytes 4718592 | tf_op jit(solution)/shard_map/all_to_all | solution.py:765
  36.8 0.0 collective-permute-done.1.far_ref
  36.8 0.0 copy-done.15
  36.8 0.0 copy-done.16
  36.8 0.0 copy-start.3
  36.8 1.4 copy-done.3
  38.2 17.9 %kinetic.1 = (f32[3,128,64,128]{3,2,1,0:T(8,128)}, f32[3,16,128]{2,1,0:T(8,128)S(1)}) custom-call(bf16[3,128,64,128]{3,2,1,0:T(8,128)(2,1)} %c_ref.5, bf16[3,128,16,128]{3,2,1,0:T(8,128)(2,1)S(1)} %copy-done.3, bf16[3,128,16,128]{3,2,1,0:T(8,128)(2,1)} %collective-permute-done.1.far_ref, bf16[128,128]{1,0:T(8,128)(2,1)S(1)} %copy-done.15, ...), custom_call_target="tpu_custom_call" | custom-call | flops 9663676416 | bytes 22020096 | tf_op jit(solution)/shard_map/kinetic/pallas_call | solution.py:424
  56.1 12.5 %all-to-all-done.got_ref = s16[64,144,128]{2,1,0:T(8,128)(2,1)S(1)} async-done(((s16[64,144,128]{2,1,0:T(8,128)(2,1)}), s16[64,144,128]{2,1,0:T(8,128)(2,1)S(1)}, u32[]{:S(2)}, u32[]{:S(2)}) %all-to-all-start) | async-done | bytes 2359328 | tf_op jit(solution)/shard_map/all_to_all | solution.py:765
  68.6 0.9 slab_sum.1
  69.5 3.6 %all_gather.3.slab_ref = f32[2,128,128]{2,1,0:T(8,128)S(1)} all-gather(f32[2,64,128]{2,1,0:T(8,128)S(1)} %bitcast.5), channel_id=1, replica_groups=mesh['orb'=64,'grid'=2] {'grid'}, dimensions={1}, use_global_device_ids=true | all-gather | bytes 196608 | tf_op jit(solution)/shard_map/all_gather | solution.py:808
  73.1 0.0 copy-done.7
  73.1 2.2 %solve.1 = s16[64,144,128]{2,1,0:T(8,128)(2,1)S(1)} custom-call(f32[128]{0:T(128)S(1)} %copy-done.14, f32[2,128,128]{2,1,0:T(8,128)S(1)} %all_gather.3.slab_ref, f32[128,128]{1,0:T(8,128)S(1)} %copy-done.7, f32[128,128]{1,0:T(8,128)S(1)} %copy-done.8), custom_call_target="tpu_custom_call" | custom-call | tf_op jit(solution)/shard_map/solve/pallas_call | solution.py:535
  75.4 37.9 %all_to_all.10.got_ref = s16[64,144,128]{2,1,0:T(8,128)(2,1)S(1)} all-to-all(s16[64,144,128]{2,1,0:T(8,128)(2,1)S(1)} %solve.1), channel_id=1, replica_groups=mesh['orb'=64,'grid'=2] {'orb'}, dimensions={0} | all-to-all | bytes 4718592 | tf_op jit(solution)/shard_map/all_to_all | solution.py:765
  113.3 0.0 copy-done.1
  113.3 10.1 %field.1 = (bf16[3,128,64,128]{3,2,1,0:T(8,128)(2,1)}, bf16[3,128,16,128]{3,2,1,0:T(8,128)(2,1)}, f32[64,8,128]{2,1,0:T(8,128)S(1)}, f32[3,16,128]{2,1,0:T(8,128)S(1)}) custom-call(s16[64,144,128]{2,1,0:T(8,128)(2,1)S(1)} %all_to_all.10.got_ref, bf16[3,64,128,128]{3,2,1,0:T(8,128)(2,1)S(1)} %copy-done.1, ...), custom_call_target="tpu_custom_call" | custom-call | tf_op jit(solution)/shard_map/field/pallas_call | solution.py:653
  123.4 1.6 %collective-permute-start.3 = (bf16[3,128,16,128]{3,2,1,0:T(8,128)(2,1)}, bf16[3,128,16,128]{3,2,1,0:T(8,128)(2,1)S(1)}, u32[]{:S(2)}, u32[]{:S(2)}) collective-permute-start(bf16[3,128,16,128]{3,2,1,0:T(8,128)(2,1)} %get-tuple-element.20), channel_id=1, source_target_pairs={{0,1},{1,0},{2,3},{3,2},{4,5},{5,4},{6,7},{7,6},{8,9},{9,8},{10,11... | collective-permute-start | bytes 4718600 | tf_op jit(solution)/shard_map/ppermute | solution.py:757
  125.0 0.0 collective-permute-start.2
  125.0 0.6 copy.19
  125.6 2.3 %collective-permute-done.2.other_ref = f32[3,16,128]{2,1,0:T(8,128)S(1)} collective-permute-done((f32[3,16,128]{2,1,0:T(8,128)S(1)}, f32[3,16,128]{2,1,0:T(8,128)S(1)}, u32[]{:S(2)}, u32[]{:S(2)}) %collective-permute-start.2) | collective-permute-done | bytes 24608 | tf_op jit(solution)/shard_map/ppermute | solution.py:757
  127.9 0.3 collective-permute-done.3.rim_ref
  128.2 13.7 %update.1 = (bf16[3,128,64,128]{3,2,1,0:T(8,128)(2,1)}, f32[3]{0:T(128)}) custom-call(f32[3,16,128]{2,1,0:T(8,128)S(1)} %get-tuple-element.18.sums_ref, f32[3,16,128]{2,1,0:T(8,128)S(1)} %collective-permute-done.2.other_ref, bf16[3,128,64,128]{3,2,1,0:T(8,128)(2,1)} %get-tuple-element.19.back_ref, ...), custom_call_target="tpu_custom_call" | custom-call | tf_op jit(solution)/shard_map/update/pallas_call | solution.py:733
  (13 shorter events, 0.0 us)
Async XLA Ops:
  0.6 2.8 %copy-start = (bf16[3,128,64,128]{3,2,1,0:T(8,128)(2,1)S(1)}, bf16[3,128,64,128]{3,2,1,0:T(8,128)(2,1)}, u32[]{:S(2)}) copy-start(bf16[3,128,64,128]{3,2,1,0:T(8,128)(2,1)} %c_ref.5) | copy-start | bytes 18874372
  3.4 0.7 copy-start.11
  4.1 5.5 %slice-start = ((s8[6291456]{0:T(1024)(128)(4,1)}), s8[4194304]{0:T(1024)(128)(4,1)S(1)}, s32[]{:S(2)}) async-start(s8[6291456]{0:T(1024)(128)(4,1)} %bitcast.3), calls=%async_computation.2 | async-start | bytes 8388608
  5.0 4.6 %slice-start.1 = ((s8[6291456]{0:T(1024)(128)(4,1)}), s8[2097152]{0:T(1024)(128)(4,1)S(1)}, s32[]{:S(2)}) async-start(s8[6291456]{0:T(1024)(128)(4,1)} %bitcast.3), calls=%async_computation.3 | async-start | bytes 4194304
  5.0 4.6 %copy-start.4 = (bf16[128,256]{1,0:T(8,128)(2,1)S(1)}, bf16[128,256]{1,0:T(8,128)(2,1)}, u32[]{:S(2)}) copy-start(bf16[128,256]{1,0:T(8,128)(2,1)} %constant.35.clone.dht_ref) | copy-start | bytes 196612
  5.0 4.6 %copy-start.5 = (bf16[128,128]{1,0:T(8,128)(2,1)S(1)}, bf16[128,128]{1,0:T(8,128)(2,1)}, u32[]{:S(2)}) copy-start(bf16[128,128]{1,0:T(8,128)(2,1)} %constant.38.clone.mz_ref.ty_ref) | copy-start | bytes 98308
  5.0 4.6 %copy-start.6 = (bf16[128,128]{1,0:T(8,128)(2,1)S(1)}, bf16[128,128]{1,0:T(8,128)(2,1)}, u32[]{:S(2)}) copy-start(bf16[128,128]{1,0:T(8,128)(2,1)} %constant.36.clone.my_ref.tz_ref) | copy-start | bytes 98308
  5.0 4.6 %copy-start.10 = (bf16[64,80]{1,0:T(8,128)(2,1)S(1)}, bf16[64,80]{1,0:T(8,128)(2,1)}, u32[]{:S(2)}) copy-start(bf16[64,80]{1,0:T(8,128)(2,1)} %constant.37.clone.ax_ref) | copy-start | bytes 30724
  5.0 4.6 %copy-start.12 = (s32[192]{0:T(256)S(1)}, s32[192]{0:T(256)}, u32[]{:S(2)}) copy-start(s32[192]{0:T(256)} %occ_ref.1) | copy-start | bytes 2308
  5.0 4.6 %copy-start.13 = (s32[192]{0:T(256)S(1)}, s32[192]{0:T(256)}, u32[]{:S(2)}) copy-start(s32[192]{0:T(256)} %slot_ref.1) | copy-start | bytes 2308
  5.0 4.5 %collective-permute-start = (bf16[3,128,16,128]{3,2,1,0:T(8,128)(2,1)S(1)}, bf16[3,128,16,128]{3,2,1,0:T(8,128)(2,1)S(1)}, u32[]{:S(2)}, u32[]{:S(2)}) collective-permute-start(bf16[3,128,16,128]{3,2,1,0:T(8,128)(2,1)S(1)} %own_rims.2.after_ref), channel_id=1, source_target_pairs={{0,1},{1,0},{2,3},{3,2},{4,5},{5,4},{6,7},{7,6},{8,9},{9,8},{10,11... | collective-permute-start | bytes 4718600 | tf_op jit(solution)/shard_map/ppermute | solution.py:757
  9.2 27.5 %collective-permute-start.1 = (bf16[3,128,16,128]{3,2,1,0:T(8,128)(2,1)}, bf16[3,128,16,128]{3,2,1,0:T(8,128)(2,1)}, u32[]{:S(2)}, u32[]{:S(2)}) collective-permute-start(bf16[3,128,16,128]{3,2,1,0:T(8,128)(2,1)} %own_rims.3), channel_id=1, source_target_pairs={{0,1},{1,0},{2,3},{3,2},{4,5},{5,4},{6,7},{7,6},{8,9},{9,8},{10,11... | collective-permute-start | bytes 4718600 | tf_op jit(solution)/shard_map/ppermute | solution.py:757
  9.6 15.7 %copy-start.2 = (bf16[3,128,16,128]{3,2,1,0:T(8,128)(2,1)}, bf16[3,128,16,128]{3,2,1,0:T(8,128)(2,1)S(1)}, u32[]{:S(2)}) copy-start(bf16[3,128,16,128]{3,2,1,0:T(8,128)(2,1)S(1)} %collective-permute-done.h_ref.near_ref) | copy-start | bytes 4718596
  25.4 11.4 %copy-start.15 = (bf16[128,128]{1,0:T(8,128)(2,1)S(1)}, bf16[128,128]{1,0:T(8,128)(2,1)}, u32[]{:S(2)}) copy-start(bf16[128,128]{1,0:T(8,128)(2,1)} %constant.39.clone.dy_ref.dz_ref) | copy-start | bytes 98308
  25.4 11.4 %copy-start.16 = (bf16[64,96]{1,0:T(8,128)(2,1)S(1)}, bf16[64,96]{1,0:T(8,128)(2,1)}, u32[]{:S(2)}) copy-start(bf16[64,96]{1,0:T(8,128)(2,1)} %constant.40.clone.dx_ref) | copy-start | bytes 36868
  25.4 43.2 %all-to-all-start = ((s16[64,144,128]{2,1,0:T(8,128)(2,1)}), s16[64,144,128]{2,1,0:T(8,128)(2,1)S(1)}, u32[]{:S(2)}, u32[]{:S(2)}) async-start(s16[64,144,128]{2,1,0:T(8,128)(2,1)} %get-tuple-element.14), calls=%async_computation | async-start | bytes 4718592 | tf_op jit(solution)/shard_map/all_to_all | solution.py:765
  36.8 1.4 copy-start.3
  56.1 17.0 %copy-start.7 = (f32[128,128]{1,0:T(8,128)S(1)}, f32[128,128]{1,0:T(8,128)}, u32[]{:S(2)}) copy-start(f32[128,128]{1,0:T(8,128)} %constant.42.clone.dht_ref) | copy-start | bytes 196612
  56.1 17.0 %copy-start.8 = (f32[128,128]{1,0:T(8,128)S(1)}, f32[128,128]{1,0:T(8,128)}, u32[]{:S(2)}) copy-start(f32[128,128]{1,0:T(8,128)} %constant.43.clone.curve_ref) | copy-start | bytes 196612
  56.1 17.0 %copy-start.14 = (f32[128]{0:T(128)S(1)}, f32[128]{0:T(128)}, u32[]{:S(2)}) copy-start(f32[128]{0:T(128)} %constant.41.clone.curve_z_ref) | copy-start | bytes 1540
  73.1 40.2 %copy-start.1 = (bf16[3,64,128,128]{3,2,1,0:T(8,128)(2,1)S(1)}, bf16[3,64,128,128]{3,2,1,0:T(8,128)(2,1)}, u32[]{:S(2)}) copy-start(bf16[3,64,128,128]{3,2,1,0:T(8,128)(2,1)} %get-tuple-element.17.psi_ref) | copy-start | bytes 18874372
  113.3 14.9 %copy-start.9 = (bf16[64,80]{1,0:T(8,128)(2,1)S(1)}, bf16[64,80]{1,0:T(8,128)(2,1)}, u32[]{:S(2)}) copy-start(bf16[64,80]{1,0:T(8,128)(2,1)} %constant.44.clone.tx_ref) | copy-start | bytes 30724
  123.4 4.8 %collective-permute-start.3 = (bf16[3,128,16,128]{3,2,1,0:T(8,128)(2,1)}, bf16[3,128,16,128]{3,2,1,0:T(8,128)(2,1)S(1)}, u32[]{:S(2)}, u32[]{:S(2)}) collective-permute-start(bf16[3,128,16,128]{3,2,1,0:T(8,128)(2,1)} %get-tuple-element.20), channel_id=1, source_target_pairs={{0,1},{1,0},{2,3},{3,2},{4,5},{5,4},{6,7},{7,6},{8,9},{9,8},{10,11... | collective-permute-start | bytes 4718600 | tf_op jit(solution)/shard_map/ppermute | solution.py:757
  125.0 2.9 %collective-permute-start.2 = (f32[3,16,128]{2,1,0:T(8,128)S(1)}, f32[3,16,128]{2,1,0:T(8,128)S(1)}, u32[]{:S(2)}, u32[]{:S(2)}) collective-permute-start(f32[3,16,128]{2,1,0:T(8,128)S(1)} %get-tuple-element.18.sums_ref), channel_id=1, source_target_pairs={{0,1},{1,0},{2,3},{3,2},{4,5},{5,4},{6,7},{7,6},{8,9},{9,8},{10,11... | collective-permute-start | bytes 73736 | tf_op jit(solution)/shard_map/ppermute | solution.py:757

commit v4 on v3

--- a/solution.py
+++ b/solution.py
@@ -101,7 +101,7 @@
 def split_table(table):
     high = table.astype(ml_dtypes.bfloat16)
     low = (table - high.astype(np.float32)).astype(ml_dtypes.bfloat16)
-    return np.concatenate([high, low], axis=1)
+    return np.concatenate([high, low, high], axis=1)
 
 
 def curve(length):
@@ -119,6 +119,12 @@
 def params(count, mebibytes):
     return pltpu.CompilerParams(
         dimension_semantics=("arbitrary",) * count, vmem_limit_bytes=mebibytes * MIB
+    )
+
+
+def cost(cells, bytes_each):
+    return pl.CostEstimate(
+        flops=cells * 256, bytes_accessed=cells * bytes_each, transcendentals=0
     )
 
 
@@ -150,36 +156,38 @@
 def hartley_pair(table, pair):
     high = pair.astype(BF16)
     low = (pair - high.astype(F32)).astype(BF16)
-    return dot(table, jnp.concatenate([high, high], axis=0)) + dot(
-        table, jnp.concatenate([low, low], axis=0)
-    )
-
-
-def rims_kernel(inner, outer, low_ref, high_ref, after_ref, out_ref):
+    return dot(table, jnp.concatenate([high, high, low], axis=0))
+
+
+def rims_kernel(inner, outer, low_ref, high_ref, *rest):
+    out_ref, mark_ref = rest[-2:]
     tile = low_ref.shape[2]
-    low = low_ref[0].astype(F32)[:, tile - outer : tile - inner]
-    high = high_ref[0].astype(F32)[:, inner:outer]
-    out_ref[0] = jnp.concatenate([low, high], axis=1).astype(BF16)
-
-
-def own_rims(c, inner, outer, after):
+    low = low_ref[...].astype(F32)[:, :, tile - outer : tile - inner]
+    high = high_ref[...].astype(F32)[:, :, inner:outer]
+    out_ref[...] = jnp.concatenate([low, high], axis=2).astype(BF16)
+    mark_ref[...] = jnp.zeros_like(mark_ref)
+
+
+def own_rims(c, inner, outer, *after):
     orbitals, length, cells_x, cells_y = c.shape
     tile = 16
-    chunks = 2
-    part = length // chunks
 
     def at(k):
-        return pl.BlockSpec((1, part, tile, cells_y), lambda o, j: (o, j, k, 0))
+        return pl.BlockSpec((orbitals, length, tile, cells_y), lambda o: (0, 0, k, 0))
 
     return pl.pallas_call(
         functools.partial(rims_kernel, inner, outer),
-        grid=(orbitals, chunks),
-        in_specs=[at(cells_x // tile - 1), at(0), pl.BlockSpec(memory_space=pl.ANY)],
-        out_specs=at(0),
-        out_shape=jax.ShapeDtypeStruct((orbitals, length, 2 * (outer - inner), cells_y), BF16),
-        compiler_params=params(2, 8),
+        grid=(1,),
+        in_specs=[at(cells_x // tile - 1), at(0)]
+        + [pl.BlockSpec(memory_space=pl.ANY) for _ in after],
+        out_specs=[at(0), pl.BlockSpec((8, cells_y), lambda o: (0, 0))],
+        out_shape=[
+            jax.ShapeDtypeStruct((orbitals, length, 2 * (outer - inner), cells_y), BF16),
+            jax.ShapeDtypeStruct((8, cells_y), F32),
+        ],
+        compiler_params=params(1, 16),
         name="own_rims",
-    )(c, c, after)
+    )(c, c, *after)
 
 
 def density_kernel(
@@ -352,7 +360,7 @@
 
 
 def kinetic_kernel(
-    pitch, c_ref, near_ref, far_ref, dy_ref, dx_ref, dz_ref, after_ref, kin_ref, sums_ref, wide, acc
+    pitch, c_ref, near_ref, far_ref, dy_ref, dx_ref, dz_ref, after_ref, kin_ref, step_ref, sums_ref, wide, acc
 ):
     length, cells_x, cells_y = c_ref.shape[1], c_ref.shape[2], c_ref.shape[3]
     block = 8
@@ -382,6 +390,7 @@
         z0 = i * block
         own = c_ref[0, pl.ds(z0, block)]
         along_y = dot(own.reshape(block * cells_x, cells_y), dy_ref[...])
+        steps = []
         for p in range(0, block, 2):
             z = z0 + p
             pair = jnp.concatenate(
@@ -400,11 +409,16 @@
                     + along_x[:, k * cells_y : (k + 1) * cells_y]
                     + along_y[(p + k) * cells_x : (p + k + 1) * cells_x]
                 )
-                kin_ref[0, z + k] = value
+                tiles = (cells_x // 8, 8, cells_y)
+                largest = jnp.max(jnp.max(jnp.abs(value).reshape(tiles), axis=0), axis=0)
+                largest = jnp.maximum(largest, 1e-30).reshape(1, cells_y)
+                coded = jnp.round(value * (LEVELS / largest))
+                kin_ref[0, z + k] = coded.astype(jnp.int32).astype(jnp.int16)
+                steps.append(largest * (1.0 / LEVELS))
                 coeff = own[p + k].astype(F32)
-                tiles = (cells_x // 8, 8, cells_y)
                 energy = energy + jnp.sum((coeff * value).reshape(tiles), axis=0)
                 norm = norm + jnp.sum((coeff * coeff).reshape(tiles), axis=0)
+        step_ref[0, pl.ds(pl.multiple_of(z0, block), block), :] = jnp.concatenate(steps, axis=0)
         return energy, norm
 
     zeros = jnp.zeros((8, cells_y), F32)
@@ -433,9 +447,14 @@
             whole(dz),
             pl.BlockSpec(memory_space=pl.ANY),
         ],
-        out_specs=[block(c), pl.BlockSpec((1, 16, cells_y), lambda o: (o, 0, 0))],
+        out_specs=[
+            block(c),
+            pl.BlockSpec((1, length, cells_y), lambda o: (o, 0, 0)),
+            pl.BlockSpec((1, 16, cells_y), lambda o: (o, 0, 0)),
+        ],
         out_shape=[
-            pltpu.HBM(c.shape, F32),
+            pltpu.HBM(c.shape, jnp.int16),
+            jax.ShapeDtypeStruct((orbitals, length, cells_y), F32),
             jax.ShapeDtypeStruct((orbitals, 16, cells_y), F32),
         ],
         scratch_shapes=[
@@ -684,7 +703,17 @@
 
 
 def update_kernel(
-    sums_ref, other_ref, back_ref, rim_ref, c_ref, kin_ref, tx_ref, ty_ref, out_ref, energy_ref
+    sums_ref,
+    other_ref,
+    back_ref,
+    rim_ref,
+    c_ref,
+    kin_ref,
+    step_ref,
+    tx_ref,
+    ty_ref,
+    out_ref,
+    energy_ref,
 ):
     orbital = pl.program_id(0)
 
@@ -715,9 +744,11 @@
             both = dot(tx, flat).astype(BF16)
             crossed += [both[:, k * cells_y : (k + 1) * cells_y] for k in range(many)]
         potential = dot(jnp.concatenate(crossed, axis=0), ty)
+        steps = step_ref[0, pl.ds(pl.multiple_of(z0, block), block), :]
         for p in range(block):
             z = z0 + p
-            applied = potential[p * cells_x : (p + 1) * cells_x] + kin_ref[0, z]
+            kin = kin_ref[0, z].astype(jnp.int32).astype(F32) * steps[p : p + 1]
+            applied = potential[p * cells_x : (p + 1) * cells_x] + kin
             coeff = c_ref[0, z].astype(F32)
             out_ref[0, z] = (coeff - STEP_SIZE * (applied - energy * coeff)).astype(BF16)
         return carry
@@ -725,7 +756,7 @@
     lax.fori_loop(0, some_z // block, planes, 0, unroll=4)
 
 
-def update(sums, other_sums, back, rim, c, kin, tx, ty):
+def update(sums, other_sums, back, rim, c, kin, steps, tx, ty):
     orbitals, length, cells_x, cells_y = c.shape
     chunks = 2
     part = length // chunks
@@ -740,6 +771,7 @@
             pl.BlockSpec((1, part, rim.shape[2], cells_y), lambda o, j: (o, j, 0, 0)),
             block,
             block,
+            pl.BlockSpec((1, part, cells_y), lambda o, j: (o, j, 0)),
             whole(tx),
             whole(ty),
         ],
@@ -750,7 +782,7 @@
         ],
         compiler_params=params(2, 12),
         name="update",
-    )(sums, other_sums, back, rim, c, kin, tx, ty)
+    )(sums, other_sums, back, rim, c, kin, steps, tx, ty)
 
 
 def to_other(array):
@@ -780,9 +812,10 @@
     table = jnp.asarray(split_table(dht))
     waves = curve(length)
 
-    own_near = own_rims(coefficients, 0, 8, occupations)
+    c = in_hbm(coefficients)
+    own_near, mark = own_rims(c, 0, 8)
     near = to_other(own_near)
-    far = to_other(own_rims(coefficients, 8, 16, own_near))
+    far = to_other(own_rims(c, 8, 16, mark)[0])
     psi, coded, peak = density(
         occupations,
         slot_orbital,
@@ -795,8 +828,8 @@
         owners,
     )
     got = to_all(coded)
-    kin, kin_sums = kinetic(
-        in_hbm(coefficients),
+    kin, steps, kin_sums = kinetic(
+        c,
         near,
         far,
         jnp.asarray(kin_line.T),
@@ -821,8 +854,9 @@
         to_other(sums),
         in_hbm(back),
         to_other(back_rims),
-        in_hbm(coefficients),
+        c,
         in_hbm(kin),
+        steps,
         jnp.asarray(band_columns(cells_x, near_cells, trans)),
         jnp.asarray(trans_line.T),
     )

time: 142 us -> 140 us (0.986)
  local copies, waits for them, and re-layouts: 5.61 us -> 2.87 us
    unnamed x39 -> x35, local copies, waits for them, and re-layouts: 5.58 us -> 2.85 us
    pallas_call x2, Pallas kernels: 3.54 us -> 5.77 us  [own_rims(): pl.pallas_call(functools.partial(rims_kernel, inner, outer), grid=(1,), i...]
  transfers between devices with their start and end apart: 5 -> 5, of which waited for: 4 -> 3; matrix products, arithmetic and copies ran while one was open for 0% -> 0% of each run, Pallas kernels for 26% -> 27%
where the time goes in v4:
time: 140 us; the launch traced here: 139 us
  Pallas kernels  65.2 us (47%)
  blocking collectives  40.6 us (29%)
  waiting for transfers between devices  15.6 us (11%)
  starting transfers between devices  14.5 us (10%)
  local copies, waits for them, and re-layouts  2.87 us (2%)
    all_to_all x1, blocking collectives, to_all(): lax.all_to_all(blocks, 'orb', split_axis=0, concat_axis=0, tiled=True)  37.5 us
    pallas_call x1, Pallas kernels, kinetic(): pl.pallas_call(functools.partial(kinetic_kernel, pitch), grid=(orbitals,)...  18.2 us
    pallas_call x1, Pallas kernels, density(): pl.pallas_call(functools.partial(density_kernel, first_steps, pitch), gri...  15.4 us
    all_to_all x1, waiting for transfers between devices, to_all(): lax.all_to_all(blocks, 'orb', split_axis=0, concat_axis=0, tiled=True)  12.9 us
    pallas_call x1, Pallas kernels, update(): pl.pallas_call(update_kernel, grid=(orbitals, chunks), in_specs=[whole(su...  12.7 us
    all_to_all x1, starting transfers between devices, to_all(): lax.all_to_all(blocks, 'orb', split_axis=0, concat_axis=0, tiled=True)  11.4 us
    pallas_call x1, Pallas kernels, field(): pl.pallas_call(functools.partial(field_kernel, pitch, turn_pitch), grid=(...  9.99 us
    pallas_call x2, Pallas kernels, own_rims(): pl.pallas_call(functools.partial(rims_kernel, inner, outer), grid=(1,), i...  5.77 us
  transfers between devices with their start and end apart: 5, of which 3 were waited for; matrix products, arithmetic and copies ran while one was open for 0% of the time, Pallas kernels for 27%

profile of v4, /device:TPU:1, one launch (start us, length us, event | category | flops | bytes accessed | tf_op | source)
XLA Modules:
  0.0 139.5 jit_solution(10697306479416446202)
XLA Ops:
  0.6 2.2 %own_rims.2 = (bf16[3,128,16,128]{3,2,1,0:T(8,128)(2,1)S(1)}, f32[8,128]{1,0:T(8,128)S(1)}) custom-call(bf16[3,128,64,128]{3,2,1,0:T(8,128)(2,1)} %c_ref.5, bf16[3,128,64,128]{3,2,1,0:T(8,128)(2,1)} %c_ref.5), custom_call_target="tpu_custom_call" | custom-call | tf_op jit(solution)/shard_map/own_rims/pallas_call | solution.py:178
  2.8 1.5 %collective-permute-start = (bf16[3,128,16,128]{3,2,1,0:T(8,128)(2,1)S(1)}, bf16[3,128,16,128]{3,2,1,0:T(8,128)(2,1)S(1)}, u32[]{:S(2)}, u32[]{:S(2)}) collective-permute-start(bf16[3,128,16,128]{3,2,1,0:T(8,128)(2,1)S(1)} %get-tuple-element.18), channel_id=1, source_target_pairs={{0,1},{1,0},{2,3},{3,2},{4,5},{5,4},{6,7},{7,6},{8,9},{9,8},{10,11... | collective-permute-start | bytes 4718600 | tf_op jit(solution)/shard_map/ppermute | solution.py:789
  4.3 0.0 slice-start
  4.3 0.0 slice-start.1
  4.3 0.0 copy-start.3
  4.4 0.0 copy-start.5
  4.4 0.0 copy-start.9
  4.4 0.0 copy-start.10
  4.4 0.0 copy-start.11
  4.4 3.6 %own_rims.3 = (bf16[3,128,16,128]{3,2,1,0:T(8,128)(2,1)}, f32[8,128]{1,0:T(8,128)}) custom-call(bf16[3,128,64,128]{3,2,1,0:T(8,128)(2,1)} %c_ref.5, bf16[3,128,64,128]{3,2,1,0:T(8,128)(2,1)} %c_ref.5, f32[8,128]{1,0:T(8,128)S(1)} %get-tuple-element.20.rest_0_), custom_call_target="tpu_custom_call" | custom-call | tf_op jit(solution)/shard_map/own_rims/pallas_call | solution.py:178
  8.0 0.1 collective-permute-start.1
  8.0 0.0 collective-permute-done.h_ref.near_ref
  8.0 0.0 slice-done
  8.0 0.7 slice-done.1
  8.8 0.0 copy-done.3
  8.8 0.0 copy-done.4
  8.8 0.0 copy-done.5
  8.8 0.0 copy-done.9
  8.8 0.0 copy-done.10
  8.8 0.0 copy-done.11
  8.8 0.0 copy-start.1
  8.8 15.4 %density.1 = (bf16[3,64,128,128]{3,2,1,0:T(8,128)(2,1)}, s16[64,144,128]{2,1,0:T(8,128)(2,1)}, f32[8,128]{1,0:T(8,128)S(1)}) custom-call(s32[192]{0:T(256)S(1)} %copy-done.10, s32[192]{0:T(256)S(1)} %copy-done.11, bf16[3,128,64,128]{3,2,1,0:T(8,128)(2,1)S(1)} %bitcast.4, bf16[3,128,16,128]{3,2,1,0:T(8,128)(2,1)S(1)} %collective-permute-done.h_ref.near_ref, ...), custom_call_target="tpu_custom_call" | custom-call | tf_op jit(solution)/shard_map/density/pallas_call | solution.py:326
  24.3 0.0 copy-done.1
  24.3 0.0 copy-start.14
  24.3 11.4 %all-to-all-start = ((s16[64,144,128]{2,1,0:T(8,128)(2,1)}), s16[64,144,128]{2,1,0:T(8,128)(2,1)S(1)}, u32[]{:S(2)}, u32[]{:S(2)}) async-start(s16[64,144,128]{2,1,0:T(8,128)(2,1)} %get-tuple-element.19), calls=%async_computation | async-start | bytes 4718592 | tf_op jit(solution)/shard_map/all_to_all | solution.py:797
  35.6 0.0 collective-permute-done.1.far_ref
  35.7 0.0 copy-done.13
  35.7 0.0 copy-done.14
  35.7 0.0 copy-start.2
  35.7 1.4 %copy-done.2 = bf16[3,128,16,128]{3,2,1,0:T(8,128)(2,1)S(1)} copy-done((bf16[3,128,16,128]{3,2,1,0:T(8,128)(2,1)S(1)}, bf16[3,128,16,128]{3,2,1,0:T(8,128)(2,1)}, u32[]{:S(2)}) %copy-start.2) | copy-done | bytes 1572888
  37.1 18.2 %kinetic.1 = (s16[3,128,64,128]{3,2,1,0:T(8,128)(2,1)}, f32[3,128,128]{2,1,0:T(8,128)S(1)}, f32[3,16,128]{2,1,0:T(8,128)S(1)}) custom-call(bf16[3,128,64,128]{3,2,1,0:T(8,128)(2,1)} %c_ref.5, bf16[3,128,16,128]{3,2,1,0:T(8,128)(2,1)S(1)} %copy-done.2, bf16[3,128,16,128]{3,2,1,0:T(8,128)(2,1)} %collective-permute-done.1.far_ref, ...), custom_call_target="tpu_custom_call" | custom-call | flops 9663676416 | bytes 22020096 | tf_op jit(solution)/shard_map/kinetic/pallas_call | solution.py:438
  55.3 12.9 %all-to-all-done.got_ref = s16[64,144,128]{2,1,0:T(8,128)(2,1)S(1)} async-done(((s16[64,144,128]{2,1,0:T(8,128)(2,1)}), s16[64,144,128]{2,1,0:T(8,128)(2,1)S(1)}, u32[]{:S(2)}, u32[]{:S(2)}) %all-to-all-start) | async-done | bytes 2359328 | tf_op jit(solution)/shard_map/all_to_all | solution.py:797
  68.2 0.9 slab_sum.1
  69.1 3.1 %all_gather.3.slab_ref = f32[2,128,128]{2,1,0:T(8,128)S(1)} all-gather(f32[2,64,128]{2,1,0:T(8,128)S(1)} %bitcast.5), channel_id=1, replica_groups=mesh['orb'=64,'grid'=2] {'grid'}, dimensions={1}, use_global_device_ids=true | all-gather | bytes 196608 | tf_op jit(solution)/shard_map/all_gather | solution.py:841
  72.1 0.0 copy-done.6
  72.1 0.0 copy-done.7
  72.2 0.0 copy-done.12
  72.2 2.2 %solve.1 = s16[64,144,128]{2,1,0:T(8,128)(2,1)S(1)} custom-call(f32[128]{0:T(128)S(1)} %copy-done.12, f32[2,128,128]{2,1,0:T(8,128)S(1)} %all_gather.3.slab_ref, f32[128,128]{1,0:T(8,128)S(1)} %copy-done.6, f32[128,128]{1,0:T(8,128)S(1)} %copy-done.7), custom_call_target="tpu_custom_call" | custom-call | tf_op jit(solution)/shard_map/solve/pallas_call | solution.py:554
  74.4 37.5 %all_to_all.10.got_ref = s16[64,144,128]{2,1,0:T(8,128)(2,1)S(1)} all-to-all(s16[64,144,128]{2,1,0:T(8,128)(2,1)S(1)} %solve.1), channel_id=1, replica_groups=mesh['orb'=64,'grid'=2] {'orb'}, dimensions={0} | all-to-all | bytes 4718592 | tf_op jit(solution)/shard_map/all_to_all | solution.py:797
  111.9 0.0 copy-done
  111.9 10.0 %field.1 = (bf16[3,128,64,128]{3,2,1,0:T(8,128)(2,1)}, bf16[3,128,16,128]{3,2,1,0:T(8,128)(2,1)}, f32[64,8,128]{2,1,0:T(8,128)S(1)}, f32[3,16,128]{2,1,0:T(8,128)S(1)}) custom-call(s16[64,144,128]{2,1,0:T(8,128)(2,1)S(1)} %all_to_all.10.got_ref, bf16[3,64,128,128]{3,2,1,0:T(8,128)(2,1)S(1)} %copy-done, ...), custom_call_target="tpu_custom_call" | custom-call | tf_op jit(solution)/shard_map/field/pallas_call | solution.py:672
  121.9 1.6 %collective-permute-start.3 = (bf16[3,128,16,128]{3,2,1,0:T(8,128)(2,1)}, bf16[3,128,16,128]{3,2,1,0:T(8,128)(2,1)S(1)}, u32[]{:S(2)}, u32[]{:S(2)}) collective-permute-start(bf16[3,128,16,128]{3,2,1,0:T(8,128)(2,1)} %get-tuple-element.27), channel_id=1, source_target_pairs={{0,1},{1,0},{2,3},{3,2},{4,5},{5,4},{6,7},{7,6},{8,9},{9,8},{10,11... | collective-permute-start | bytes 4718600 | tf_op jit(solution)/shard_map/ppermute | solution.py:789
  123.5 0.0 collective-permute-start.2
  123.5 0.6 copy.19
  124.1 2.3 %collective-permute-done.2.other_ref = f32[3,16,128]{2,1,0:T(8,128)S(1)} collective-permute-done((f32[3,16,128]{2,1,0:T(8,128)S(1)}, f32[3,16,128]{2,1,0:T(8,128)S(1)}, u32[]{:S(2)}, u32[]{:S(2)}) %collective-permute-start.2) | collective-permute-done | bytes 24608 | tf_op jit(solution)/shard_map/ppermute | solution.py:789
  126.4 0.3 collective-permute-done.3.rim_ref
  126.8 0.0 copy-done.8
  126.8 12.7 %update.1 = (bf16[3,128,64,128]{3,2,1,0:T(8,128)(2,1)}, f32[3]{0:T(128)}) custom-call(f32[3,16,128]{2,1,0:T(8,128)S(1)} %get-tuple-element.25.sums_ref, f32[3,16,128]{2,1,0:T(8,128)S(1)} %collective-permute-done.2.other_ref, bf16[3,128,64,128]{3,2,1,0:T(8,128)(2,1)} %get-tuple-element.26.back_ref, ...), custom_call_target="tpu_custom_call" | custom-call | tf_op jit(solution)/shard_map/update/pallas_call | solution.py:764
  (9 shorter events, 0.0 us)
Async XLA Ops:
  2.8 5.2 %collective-permute-start = (bf16[3,128,16,128]{3,2,1,0:T(8,128)(2,1)S(1)}, bf16[3,128,16,128]{3,2,1,0:T(8,128)(2,1)S(1)}, u32[]{:S(2)}, u32[]{:S(2)}) collective-permute-start(bf16[3,128,16,128]{3,2,1,0:T(8,128)(2,1)S(1)} %get-tuple-element.18), channel_id=1, source_target_pairs={{0,1},{1,0},{2,3},{3,2},{4,5},{5,4},{6,7},{7,6},{8,9},{9,8},{10,11... | collective-permute-start | bytes 4718600 | tf_op jit(solution)/shard_map/ppermute | solution.py:789
  4.3 3.7 %slice-start = ((s8[6291456]{0:T(1024)(128)(4,1)}), s8[4194304]{0:T(1024)(128)(4,1)S(1)}, s32[]{:S(2)}) async-start(s8[6291456]{0:T(1024)(128)(4,1)} %bitcast.3), calls=%async_computation.2 | async-start | bytes 8388608
  4.3 4.4 %slice-start.1 = ((s8[6291456]{0:T(1024)(128)(4,1)}), s8[2097152]{0:T(1024)(128)(4,1)S(1)}, s32[]{:S(2)}) async-start(s8[6291456]{0:T(1024)(128)(4,1)} %bitcast.3), calls=%async_computation.3 | async-start | bytes 4194304
  4.3 4.4 %copy-start.3 = (bf16[128,384]{1,0:T(8,128)(2,1)S(1)}, bf16[128,384]{1,0:T(8,128)(2,1)}, u32[]{:S(2)}) copy-start(bf16[128,384]{1,0:T(8,128)(2,1)} %constant.35.clone.dht_ref) | copy-start | bytes 294916
  4.4 4.4 %copy-start.4 = (bf16[128,128]{1,0:T(8,128)(2,1)S(1)}, bf16[128,128]{1,0:T(8,128)(2,1)}, u32[]{:S(2)}) copy-start(bf16[128,128]{1,0:T(8,128)(2,1)} %constant.38.clone.mz_ref.ty_ref) | copy-start | bytes 98308
  4.4 4.4 %copy-start.5 = (bf16[128,128]{1,0:T(8,128)(2,1)S(1)}, bf16[128,128]{1,0:T(8,128)(2,1)}, u32[]{:S(2)}) copy-start(bf16[128,128]{1,0:T(8,128)(2,1)} %constant.36.clone.my_ref.tz_ref) | copy-start | bytes 98308
  4.4 4.4 %copy-start.9 = (bf16[64,80]{1,0:T(8,128)(2,1)S(1)}, bf16[64,80]{1,0:T(8,128)(2,1)}, u32[]{:S(2)}) copy-start(bf16[64,80]{1,0:T(8,128)(2,1)} %constant.37.clone.ax_ref) | copy-start | bytes 30724
  4.4 4.4 %copy-start.10 = (s32[192]{0:T(256)S(1)}, s32[192]{0:T(256)}, u32[]{:S(2)}) copy-start(s32[192]{0:T(256)} %occ_ref.1) | copy-start | bytes 2308
  4.4 4.4 %copy-start.11 = (s32[192]{0:T(256)S(1)}, s32[192]{0:T(256)}, u32[]{:S(2)}) copy-start(s32[192]{0:T(256)} %slot_ref.1) | copy-start | bytes 2308
  8.0 27.7 %collective-permute-start.1 = (bf16[3,128,16,128]{3,2,1,0:T(8,128)(2,1)}, bf16[3,128,16,128]{3,2,1,0:T(8,128)(2,1)}, u32[]{:S(2)}, u32[]{:S(2)}) collective-permute-start(bf16[3,128,16,128]{3,2,1,0:T(8,128)(2,1)} %get-tuple-element.21), channel_id=1, source_target_pairs={{0,1},{1,0},{2,3},{3,2},{4,5},{5,4},{6,7},{7,6},{8,9},{9,8},{10,11... | collective-permute-start | bytes 4718600 | tf_op jit(solution)/shard_map/ppermute | solution.py:789
  8.8 15.5 %copy-start.1 = (bf16[3,128,16,128]{3,2,1,0:T(8,128)(2,1)}, bf16[3,128,16,128]{3,2,1,0:T(8,128)(2,1)S(1)}, u32[]{:S(2)}) copy-start(bf16[3,128,16,128]{3,2,1,0:T(8,128)(2,1)S(1)} %collective-permute-done.h_ref.near_ref) | copy-start | bytes 4718596
  24.3 11.4 %copy-start.13 = (bf16[128,128]{1,0:T(8,128)(2,1)S(1)}, bf16[128,128]{1,0:T(8,128)(2,1)}, u32[]{:S(2)}) copy-start(bf16[128,128]{1,0:T(8,128)(2,1)} %constant.39.clone.dy_ref.dz_ref) | copy-start | bytes 98308
  24.3 11.4 %copy-start.14 = (bf16[64,96]{1,0:T(8,128)(2,1)S(1)}, bf16[64,96]{1,0:T(8,128)(2,1)}, u32[]{:S(2)}) copy-start(bf16[64,96]{1,0:T(8,128)(2,1)} %constant.40.clone.dx_ref) | copy-start | bytes 36868
  24.3 43.9 %all-to-all-start = ((s16[64,144,128]{2,1,0:T(8,128)(2,1)}), s16[64,144,128]{2,1,0:T(8,128)(2,1)S(1)}, u32[]{:S(2)}, u32[]{:S(2)}) async-start(s16[64,144,128]{2,1,0:T(8,128)(2,1)} %get-tuple-element.19), calls=%async_computation | async-start | bytes 4718592 | tf_op jit(solution)/shard_map/all_to_all | solution.py:797
  35.7 1.4 %copy-start.2 = (bf16[3,128,16,128]{3,2,1,0:T(8,128)(2,1)S(1)}, bf16[3,128,16,128]{3,2,1,0:T(8,128)(2,1)}, u32[]{:S(2)}) copy-start(bf16[3,128,16,128]{3,2,1,0:T(8,128)(2,1)} %copy-done.1) | copy-start | bytes 4718596
  55.3 16.9 %copy-start.6 = (f32[128,128]{1,0:T(8,128)S(1)}, f32[128,128]{1,0:T(8,128)}, u32[]{:S(2)}) copy-start(f32[128,128]{1,0:T(8,128)} %constant.42.clone.dht_ref) | copy-start | bytes 196612
  55.3 16.9 %copy-start.7 = (f32[128,128]{1,0:T(8,128)S(1)}, f32[128,128]{1,0:T(8,128)}, u32[]{:S(2)}) copy-start(f32[128,128]{1,0:T(8,128)} %constant.43.clone.curve_ref) | copy-start | bytes 196612
  55.3 16.9 %copy-start.12 = (f32[128]{0:T(128)S(1)}, f32[128]{0:T(128)}, u32[]{:S(2)}) copy-start(f32[128]{0:T(128)} %constant.41.clone.curve_z_ref) | copy-start | bytes 1540
  72.2 39.8 %copy-start = (bf16[3,64,128,128]{3,2,1,0:T(8,128)(2,1)S(1)}, bf16[3,64,128,128]{3,2,1,0:T(8,128)(2,1)}, u32[]{:S(2)}) copy-start(bf16[3,64,128,128]{3,2,1,0:T(8,128)(2,1)} %get-tuple-element.24.psi_ref) | copy-start | bytes 18874372
  111.9 14.8 %copy-start.8 = (bf16[64,80]{1,0:T(8,128)(2,1)S(1)}, bf16[64,80]{1,0:T(8,128)(2,1)}, u32[]{:S(2)}) copy-start(bf16[64,80]{1,0:T(8,128)(2,1)} %constant.44.clone.tx_ref) | copy-start | bytes 30724
  121.9 4.8 %collective-permute-start.3 = (bf16[3,128,16,128]{3,2,1,0:T(8,128)(2,1)}, bf16[3,128,16,128]{3,2,1,0:T(8,128)(2,1)S(1)}, u32[]{:S(2)}, u32[]{:S(2)}) collective-permute-start(bf16[3,128,16,128]{3,2,1,0:T(8,128)(2,1)} %get-tuple-element.27), channel_id=1, source_target_pairs={{0,1},{1,0},{2,3},{3,2},{4,5},{5,4},{6,7},{7,6},{8,9},{9,8},{10,11... | collective-permute-start | bytes 4718600 | tf_op jit(solution)/shard_map/ppermute | solution.py:789
  123.5 2.9 %collective-permute-start.2 = (f32[3,16,128]{2,1,0:T(8,128)S(1)}, f32[3,16,128]{2,1,0:T(8,128)S(1)}, u32[]{:S(2)}, u32[]{:S(2)}) collective-permute-start(f32[3,16,128]{2,1,0:T(8,128)S(1)} %get-tuple-element.25.sums_ref), channel_id=1, source_target_pairs={{0,1},{1,0},{2,3},{3,2},{4,5},{5,4},{6,7},{7,6},{8,9},{9,8},{10,11... | collective-permute-start | bytes 73736 | tf_op jit(solution)/shard_map/ppermute | solution.py:789

commit v5 on v4

--- a/solution.py
+++ b/solution.py
@@ -31,6 +31,7 @@
 STEP_SIZE = 0.1
 COULOMB = 4.0 * math.pi
 LEVELS = 32000.0
+CODE_ROWS = 8
 FINE = 16384.0
 F32 = jnp.float32
 BF16 = jnp.bfloat16
@@ -142,8 +143,8 @@
 
 
 def coded_rows(cells_y, codes):
-    row = lax.broadcasted_iota(jnp.int32, (16, cells_y), 0)
-    values = jnp.zeros((16, cells_y), F32)
+    row = lax.broadcasted_iota(jnp.int32, (CODE_ROWS, cells_y), 0)
+    values = jnp.zeros((CODE_ROWS, cells_y), F32)
     for k, code in enumerate(codes):
         values = jnp.where(row == k, code, values)
     return values.astype(jnp.int32).astype(jnp.int16)
@@ -303,7 +304,7 @@
                 values = jnp.round(waves[pl.ds(row, cells_x), :] * factor)
                 at = pl.ds(k * cells_x, cells_x)
                 q_ref[i, at, :] = values.astype(jnp.int32).astype(jnp.int16)
-            q_ref[i, rows : rows + 16, :] = code_rows
+            q_ref[i, rows : rows + CODE_ROWS, :] = code_rows
             return carry
 
         lax.fori_loop(0, q_ref.shape[0], quantise, 0, unroll=4)
@@ -317,7 +318,7 @@
     some_x = 8
     pitch = cells_x + 8
     smem = pl.BlockSpec(memory_space=pltpu.SMEM)
-    rows = (length // owners) * cells_x + 16
+    rows = (length // owners) * cells_x + CODE_ROWS
 
     def at_first(s):
         s = jnp.minimum(s, first_steps - 1)
@@ -470,7 +471,7 @@
 
 
 def unpacked(ref, source, rows):
-    codes = ref[source, rows : rows + 16, :].astype(jnp.int32).astype(F32)
+    codes = ref[source, rows : rows + CODE_ROWS, :].astype(jnp.int32).astype(F32)
     powers = jnp.exp2(codes) * (1.0 / (LEVELS * FINE))
     step = codes[1:2] * powers[0:1]
     mean = codes[4:5] * (codes[3:4] * powers[2:3])
@@ -542,7 +543,7 @@
 
     def spread(i, carry):
         q_ref[i, 0:rows, :] = coded
-        q_ref[i, rows : rows + 16, :] = code_rows
+        q_ref[i, rows : rows + CODE_ROWS, :] = code_rows
         return carry
 
     lax.fori_loop(0, q_ref.shape[0], spread, 0, unroll=4)
@@ -554,7 +555,7 @@
     return pl.pallas_call(
         solve_kernel,
         in_specs=[pl.BlockSpec(memory_space=pltpu.SMEM), vmem, vmem, vmem],
-        out_shape=jax.ShapeDtypeStruct((owners, per * (length // 2) + 16, cells_y), jnp.int16),
+        out_shape=jax.ShapeDtypeStruct((owners, per * (length // 2) + CODE_ROWS, cells_y), jnp.int16),
         compiler_params=params(0, 12),
         name="solve",
     )(curve_z, slab, dht, plane_curve)

time: 140 us -> 137 us (0.979)
  blocking collectives: 40.6 us -> 39 us
    all_to_all x1, blocking collectives: 37.5 us -> 35.9 us  [to_all(): lax.all_to_all(blocks, 'orb', split_axis=0, concat_axis=0, tiled=True)]
where the time goes in v5:
time: 137 us
  Pallas kernels  65.1 us (48%)
  blocking collectives  39 us (28%)
  starting transfers between devices  14.4 us (11%)
  waiting for transfers between devices  14.3 us (10%)
  local copies, waits for them, and re-layouts  2.87 us (2%)
    all_to_all x1, blocking collectives, to_all(): lax.all_to_all(blocks, 'orb', split_axis=0, concat_axis=0, tiled=True)  35.9 us
    pallas_call x1, Pallas kernels, kinetic(): pl.pallas_call(functools.partial(kinetic_kernel, pitch), grid=(orbitals,)...  18.2 us
    pallas_call x1, Pallas kernels, density(): pl.pallas_call(functools.partial(density_kernel, first_steps, pitch), gri...  15.4 us
    pallas_call x1, Pallas kernels, update(): pl.pallas_call(update_kernel, grid=(orbitals, chunks), in_specs=[whole(su...  12.7 us
    all_to_all x1, waiting for transfers between devices, to_all(): lax.all_to_all(blocks, 'orb', split_axis=0, concat_axis=0, tiled=True)  11.7 us
    all_to_all x1, starting transfers between devices, to_all(): lax.all_to_all(blocks, 'orb', split_axis=0, concat_axis=0, tiled=True)  11.4 us
    pallas_call x1, Pallas kernels, field(): pl.pallas_call(functools.partial(field_kernel, pitch, turn_pitch), grid=(...  9.99 us
    pallas_call x2, Pallas kernels, own_rims(): pl.pallas_call(functools.partial(rims_kernel, inner, outer), grid=(1,), i...  5.77 us
  transfers between devices with their start and end apart: 5, of which 3 were waited for; matrix products, arithmetic and copies ran while one was open for 0% of the time, Pallas kernels for 27%

profile of v5, /device:TPU:1, one launch (start us, length us, event | category | flops | bytes accessed | tf_op | source)
XLA Modules:
  0.0 136.6 jit_solution(16936343408169029292)
XLA Ops:
  0.6 2.2 %own_rims.2 = (bf16[3,128,16,128]{3,2,1,0:T(8,128)(2,1)S(1)}, f32[8,128]{1,0:T(8,128)S(1)}) custom-call(bf16[3,128,64,128]{3,2,1,0:T(8,128)(2,1)} %c_ref.5, bf16[3,128,64,128]{3,2,1,0:T(8,128)(2,1)} %c_ref.5), custom_call_target="tpu_custom_call" | custom-call | tf_op jit(solution)/shard_map/own_rims/pallas_call | solution.py:179
  2.8 1.5 %collective-permute-start = (bf16[3,128,16,128]{3,2,1,0:T(8,128)(2,1)S(1)}, bf16[3,128,16,128]{3,2,1,0:T(8,128)(2,1)S(1)}, u32[]{:S(2)}, u32[]{:S(2)}) collective-permute-start(bf16[3,128,16,128]{3,2,1,0:T(8,128)(2,1)S(1)} %get-tuple-element.18), channel_id=1, source_target_pairs={{0,1},{1,0},{2,3},{3,2},{4,5},{5,4},{6,7},{7,6},{8,9},{9,8},{10,11... | collective-permute-start | bytes 4718600 | tf_op jit(solution)/shard_map/ppermute | solution.py:790
  4.3 0.0 slice-start
  4.3 0.0 slice-start.1
  4.3 0.0 copy-start.3
  4.4 0.0 copy-start.5
  4.4 0.0 copy-start.9
  4.4 0.0 copy-start.10
  4.4 0.0 copy-start.11
  4.4 3.6 %own_rims.3 = (bf16[3,128,16,128]{3,2,1,0:T(8,128)(2,1)}, f32[8,128]{1,0:T(8,128)}) custom-call(bf16[3,128,64,128]{3,2,1,0:T(8,128)(2,1)} %c_ref.5, bf16[3,128,64,128]{3,2,1,0:T(8,128)(2,1)} %c_ref.5, f32[8,128]{1,0:T(8,128)S(1)} %get-tuple-element.20.rest_0_), custom_call_target="tpu_custom_call" | custom-call | tf_op jit(solution)/shard_map/own_rims/pallas_call | solution.py:179
  8.0 0.1 collective-permute-start.1
  8.0 0.0 collective-permute-done.h_ref.near_ref
  8.0 0.0 slice-done
  8.0 0.7 slice-done.1
  8.8 0.0 copy-done.3
  8.8 0.0 copy-done.4
  8.8 0.0 copy-done.5
  8.8 0.0 copy-done.9
  8.8 0.0 copy-done.10
  8.8 0.0 copy-done.11
  8.8 0.0 copy-start.1
  8.8 15.4 %density.1 = (bf16[3,64,128,128]{3,2,1,0:T(8,128)(2,1)}, s16[64,136,128]{2,1,0:T(8,128)(2,1)}, f32[8,128]{1,0:T(8,128)S(1)}) custom-call(s32[192]{0:T(256)S(1)} %copy-done.10, s32[192]{0:T(256)S(1)} %copy-done.11, bf16[3,128,64,128]{3,2,1,0:T(8,128)(2,1)S(1)} %bitcast.4, bf16[3,128,16,128]{3,2,1,0:T(8,128)(2,1)S(1)} %collective-permute-done.h_ref.near_ref, ...), custom_call_target="tpu_custom_call" | custom-call | tf_op jit(solution)/shard_map/density/pallas_call | solution.py:327
  24.2 0.0 copy-done.1
  24.2 0.0 copy-start.14
  24.2 11.4 %all-to-all-start = ((s16[64,136,128]{2,1,0:T(8,128)(2,1)}), s16[64,136,128]{2,1,0:T(8,128)(2,1)S(1)}, u32[]{:S(2)}, u32[]{:S(2)}) async-start(s16[64,136,128]{2,1,0:T(8,128)(2,1)} %get-tuple-element.19), calls=%async_computation | async-start | bytes 4456448 | tf_op jit(solution)/shard_map/all_to_all | solution.py:798
  35.6 0.0 collective-permute-done.1.far_ref
  35.6 0.0 copy-done.13
  35.6 0.0 copy-done.14
  35.6 0.0 copy-start.2
  35.6 1.4 %copy-done.2 = bf16[3,128,16,128]{3,2,1,0:T(8,128)(2,1)S(1)} copy-done((bf16[3,128,16,128]{3,2,1,0:T(8,128)(2,1)S(1)}, bf16[3,128,16,128]{3,2,1,0:T(8,128)(2,1)}, u32[]{:S(2)}) %copy-start.2) | copy-done | bytes 1572888
  37.0 18.2 %kinetic.1 = (s16[3,128,64,128]{3,2,1,0:T(8,128)(2,1)}, f32[3,128,128]{2,1,0:T(8,128)S(1)}, f32[3,16,128]{2,1,0:T(8,128)S(1)}) custom-call(bf16[3,128,64,128]{3,2,1,0:T(8,128)(2,1)} %c_ref.5, bf16[3,128,16,128]{3,2,1,0:T(8,128)(2,1)S(1)} %copy-done.2, bf16[3,128,16,128]{3,2,1,0:T(8,128)(2,1)} %collective-permute-done.1.far_ref, ...), custom_call_target="tpu_custom_call" | custom-call | flops 9663676416 | bytes 22020096 | tf_op jit(solution)/shard_map/kinetic/pallas_call | solution.py:439
  55.2 11.7 %all-to-all-done.got_ref = s16[64,136,128]{2,1,0:T(8,128)(2,1)S(1)} async-done(((s16[64,136,128]{2,1,0:T(8,128)(2,1)}), s16[64,136,128]{2,1,0:T(8,128)(2,1)S(1)}, u32[]{:S(2)}, u32[]{:S(2)}) %all-to-all-start) | async-done | bytes 2228256 | tf_op jit(solution)/shard_map/all_to_all | solution.py:798
  66.9 0.9 slab_sum.1
  67.8 3.0 %all_gather.3.slab_ref = f32[2,128,128]{2,1,0:T(8,128)S(1)} all-gather(f32[2,64,128]{2,1,0:T(8,128)S(1)} %bitcast.5), channel_id=1, replica_groups=mesh['orb'=64,'grid'=2] {'grid'}, dimensions={1}, use_global_device_ids=true | all-gather | bytes 196608 | tf_op jit(solution)/shard_map/all_gather | solution.py:842
  70.8 0.0 copy-done.6
  70.8 0.0 copy-done.7
  70.8 0.0 copy-done.12
  70.8 2.2 %solve.1 = s16[64,136,128]{2,1,0:T(8,128)(2,1)S(1)} custom-call(f32[128]{0:T(128)S(1)} %copy-done.12, f32[2,128,128]{2,1,0:T(8,128)S(1)} %all_gather.3.slab_ref, f32[128,128]{1,0:T(8,128)S(1)} %copy-done.6, f32[128,128]{1,0:T(8,128)S(1)} %copy-done.7), custom_call_target="tpu_custom_call" | custom-call | tf_op jit(solution)/shard_map/solve/pallas_call | solution.py:555
  73.1 35.9 %all_to_all.10.got_ref = s16[64,136,128]{2,1,0:T(8,128)(2,1)S(1)} all-to-all(s16[64,136,128]{2,1,0:T(8,128)(2,1)S(1)} %solve.1), channel_id=1, replica_groups=mesh['orb'=64,'grid'=2] {'orb'}, dimensions={0} | all-to-all | bytes 4456448 | tf_op jit(solution)/shard_map/all_to_all | solution.py:798
  109.0 0.0 copy-done
  109.0 10.0 %field.1 = (bf16[3,128,64,128]{3,2,1,0:T(8,128)(2,1)}, bf16[3,128,16,128]{3,2,1,0:T(8,128)(2,1)}, f32[64,8,128]{2,1,0:T(8,128)S(1)}, f32[3,16,128]{2,1,0:T(8,128)S(1)}) custom-call(s16[64,136,128]{2,1,0:T(8,128)(2,1)S(1)} %all_to_all.10.got_ref, bf16[3,64,128,128]{3,2,1,0:T(8,128)(2,1)S(1)} %copy-done, ...), custom_call_target="tpu_custom_call" | custom-call | tf_op jit(solution)/shard_map/field/pallas_call | solution.py:673
  119.0 1.5 %collective-permute-start.3 = (bf16[3,128,16,128]{3,2,1,0:T(8,128)(2,1)}, bf16[3,128,16,128]{3,2,1,0:T(8,128)(2,1)S(1)}, u32[]{:S(2)}, u32[]{:S(2)}) collective-permute-start(bf16[3,128,16,128]{3,2,1,0:T(8,128)(2,1)} %get-tuple-element.27), channel_id=1, source_target_pairs={{0,1},{1,0},{2,3},{3,2},{4,5},{5,4},{6,7},{7,6},{8,9},{9,8},{10,11... | collective-permute-start | bytes 4718600 | tf_op jit(solution)/shard_map/ppermute | solution.py:790
  120.5 0.0 collective-permute-start.2
  120.6 0.6 copy.19
  121.2 2.3 %collective-permute-done.2.other_ref = f32[3,16,128]{2,1,0:T(8,128)S(1)} collective-permute-done((f32[3,16,128]{2,1,0:T(8,128)S(1)}, f32[3,16,128]{2,1,0:T(8,128)S(1)}, u32[]{:S(2)}, u32[]{:S(2)}) %collective-permute-start.2) | collective-permute-done | bytes 24608 | tf_op jit(solution)/shard_map/ppermute | solution.py:790
  123.5 0.3 collective-permute-done.3.rim_ref
  123.8 0.0 copy-done.8
  123.8 12.7 %update.1 = (bf16[3,128,64,128]{3,2,1,0:T(8,128)(2,1)}, f32[3]{0:T(128)}) custom-call(f32[3,16,128]{2,1,0:T(8,128)S(1)} %get-tuple-element.25.sums_ref, f32[3,16,128]{2,1,0:T(8,128)S(1)} %collective-permute-done.2.other_ref, bf16[3,128,64,128]{3,2,1,0:T(8,128)(2,1)} %get-tuple-element.26.back_ref, ...), custom_call_target="tpu_custom_call" | custom-call | tf_op jit(solution)/shard_map/update/pallas_call | solution.py:765
  (9 shorter events, 0.0 us)
Async XLA Ops:
  2.8 5.2 %collective-permute-start = (bf16[3,128,16,128]{3,2,1,0:T(8,128)(2,1)S(1)}, bf16[3,128,16,128]{3,2,1,0:T(8,128)(2,1)S(1)}, u32[]{:S(2)}, u32[]{:S(2)}) collective-permute-start(bf16[3,128,16,128]{3,2,1,0:T(8,128)(2,1)S(1)} %get-tuple-element.18), channel_id=1, source_target_pairs={{0,1},{1,0},{2,3},{3,2},{4,5},{5,4},{6,7},{7,6},{8,9},{9,8},{10,11... | collective-permute-start | bytes 4718600 | tf_op jit(solution)/shard_map/ppermute | solution.py:790
  4.3 3.7 %slice-start = ((s8[6291456]{0:T(1024)(128)(4,1)}), s8[4194304]{0:T(1024)(128)(4,1)S(1)}, s32[]{:S(2)}) async-start(s8[6291456]{0:T(1024)(128)(4,1)} %bitcast.3), calls=%async_computation.2 | async-start | bytes 8388608
  4.3 4.4 %slice-start.1 = ((s8[6291456]{0:T(1024)(128)(4,1)}), s8[2097152]{0:T(1024)(128)(4,1)S(1)}, s32[]{:S(2)}) async-start(s8[6291456]{0:T(1024)(128)(4,1)} %bitcast.3), calls=%async_computation.3 | async-start | bytes 4194304
  4.3 4.4 %copy-start.3 = (bf16[128,384]{1,0:T(8,128)(2,1)S(1)}, bf16[128,384]{1,0:T(8,128)(2,1)}, u32[]{:S(2)}) copy-start(bf16[128,384]{1,0:T(8,128)(2,1)} %constant.35.clone.dht_ref) | copy-start | bytes 294916
  4.4 4.4 %copy-start.4 = (bf16[128,128]{1,0:T(8,128)(2,1)S(1)}, bf16[128,128]{1,0:T(8,128)(2,1)}, u32[]{:S(2)}) copy-start(bf16[128,128]{1,0:T(8,128)(2,1)} %constant.38.clone.mz_ref.ty_ref) | copy-start | bytes 98308
  4.4 4.4 %copy-start.5 = (bf16[128,128]{1,0:T(8,128)(2,1)S(1)}, bf16[128,128]{1,0:T(8,128)(2,1)}, u32[]{:S(2)}) copy-start(bf16[128,128]{1,0:T(8,128)(2,1)} %constant.36.clone.my_ref.tz_ref) | copy-start | bytes 98308
  4.4 4.4 %copy-start.9 = (bf16[64,80]{1,0:T(8,128)(2,1)S(1)}, bf16[64,80]{1,0:T(8,128)(2,1)}, u32[]{:S(2)}) copy-start(bf16[64,80]{1,0:T(8,128)(2,1)} %constant.37.clone.ax_ref) | copy-start | bytes 30724
  4.4 4.4 %copy-start.10 = (s32[192]{0:T(256)S(1)}, s32[192]{0:T(256)}, u32[]{:S(2)}) copy-start(s32[192]{0:T(256)} %occ_ref.1) | copy-start | bytes 2308
  4.4 4.4 %copy-start.11 = (s32[192]{0:T(256)S(1)}, s32[192]{0:T(256)}, u32[]{:S(2)}) copy-start(s32[192]{0:T(256)} %slot_ref.1) | copy-start | bytes 2308
  8.0 27.6 %collective-permute-start.1 = (bf16[3,128,16,128]{3,2,1,0:T(8,128)(2,1)}, bf16[3,128,16,128]{3,2,1,0:T(8,128)(2,1)}, u32[]{:S(2)}, u32[]{:S(2)}) collective-permute-start(bf16[3,128,16,128]{3,2,1,0:T(8,128)(2,1)} %get-tuple-element.21), channel_id=1, source_target_pairs={{0,1},{1,0},{2,3},{3,2},{4,5},{5,4},{6,7},{7,6},{8,9},{9,8},{10,11... | collective-permute-start | bytes 4718600 | tf_op jit(solution)/shard_map/ppermute | solution.py:790
  8.8 15.4 %copy-start.1 = (bf16[3,128,16,128]{3,2,1,0:T(8,128)(2,1)}, bf16[3,128,16,128]{3,2,1,0:T(8,128)(2,1)S(1)}, u32[]{:S(2)}) copy-start(bf16[3,128,16,128]{3,2,1,0:T(8,128)(2,1)S(1)} %collective-permute-done.h_ref.near_ref) | copy-start | bytes 4718596
  24.2 11.4 %copy-start.13 = (bf16[128,128]{1,0:T(8,128)(2,1)S(1)}, bf16[128,128]{1,0:T(8,128)(2,1)}, u32[]{:S(2)}) copy-start(bf16[128,128]{1,0:T(8,128)(2,1)} %constant.39.clone.dy_ref.dz_ref) | copy-start | bytes 98308
  24.2 11.4 %copy-start.14 = (bf16[64,96]{1,0:T(8,128)(2,1)S(1)}, bf16[64,96]{1,0:T(8,128)(2,1)}, u32[]{:S(2)}) copy-start(bf16[64,96]{1,0:T(8,128)(2,1)} %constant.40.clone.dx_ref) | copy-start | bytes 36868
  24.2 42.7 %all-to-all-start = ((s16[64,136,128]{2,1,0:T(8,128)(2,1)}), s16[64,136,128]{2,1,0:T(8,128)(2,1)S(1)}, u32[]{:S(2)}, u32[]{:S(2)}) async-start(s16[64,136,128]{2,1,0:T(8,128)(2,1)} %get-tuple-element.19), calls=%async_computation | async-start | bytes 4456448 | tf_op jit(solution)/shard_map/all_to_all | solution.py:798
  35.6 1.4 %copy-start.2 = (bf16[3,128,16,128]{3,2,1,0:T(8,128)(2,1)S(1)}, bf16[3,128,16,128]{3,2,1,0:T(8,128)(2,1)}, u32[]{:S(2)}) copy-start(bf16[3,128,16,128]{3,2,1,0:T(8,128)(2,1)} %copy-done.1) | copy-start | bytes 4718596
  55.2 15.6 %copy-start.6 = (f32[128,128]{1,0:T(8,128)S(1)}, f32[128,128]{1,0:T(8,128)}, u32[]{:S(2)}) copy-start(f32[128,128]{1,0:T(8,128)} %constant.42.clone.dht_ref) | copy-start | bytes 196612
  55.2 15.6 %copy-start.7 = (f32[128,128]{1,0:T(8,128)S(1)}, f32[128,128]{1,0:T(8,128)}, u32[]{:S(2)}) copy-start(f32[128,128]{1,0:T(8,128)} %constant.43.clone.curve_ref) | copy-start | bytes 196612
  55.2 15.6 %copy-start.12 = (f32[128]{0:T(128)S(1)}, f32[128]{0:T(128)}, u32[]{:S(2)}) copy-start(f32[128]{0:T(128)} %constant.41.clone.curve_z_ref) | copy-start | bytes 1540
  70.8 38.2 %copy-start = (bf16[3,64,128,128]{3,2,1,0:T(8,128)(2,1)S(1)}, bf16[3,64,128,128]{3,2,1,0:T(8,128)(2,1)}, u32[]{:S(2)}) copy-start(bf16[3,64,128,128]{3,2,1,0:T(8,128)(2,1)} %get-tuple-element.24.psi_ref) | copy-start | bytes 18874372
  109.0 14.8 %copy-start.8 = (bf16[64,80]{1,0:T(8,128)(2,1)S(1)}, bf16[64,80]{1,0:T(8,128)(2,1)}, u32[]{:S(2)}) copy-start(bf16[64,80]{1,0:T(8,128)(2,1)} %constant.44.clone.tx_ref) | copy-start | bytes 30724
  119.0 4.8 %collective-permute-start.3 = (bf16[3,128,16,128]{3,2,1,0:T(8,128)(2,1)}, bf16[3,128,16,128]{3,2,1,0:T(8,128)(2,1)S(1)}, u32[]{:S(2)}, u32[]{:S(2)}) collective-permute-start(bf16[3,128,16,128]{3,2,1,0:T(8,128)(2,1)} %get-tuple-element.27), channel_id=1, source_target_pairs={{0,1},{1,0},{2,3},{3,2},{4,5},{5,4},{6,7},{7,6},{8,9},{9,8},{10,11... | collective-permute-start | bytes 4718600 | tf_op jit(solution)/shard_map/ppermute | solution.py:790
  120.5 2.9 %collective-permute-start.2 = (f32[3,16,128]{2,1,0:T(8,128)S(1)}, f32[3,16,128]{2,1,0:T(8,128)S(1)}, u32[]{:S(2)}, u32[]{:S(2)}) collective-permute-start(f32[3,16,128]{2,1,0:T(8,128)S(1)} %get-tuple-element.25.sums_ref), channel_id=1, source_target_pairs={{0,1},{1,0},{2,3},{3,2},{4,5},{5,4},{6,7},{7,6},{8,9},{9,8},{10,11... | collective-permute-start | bytes 73736 | tf_op jit(solution)/shard_map/ppermute | solution.py:790

commit v6 on v5

--- a/solution.py
+++ b/solution.py
@@ -210,12 +210,13 @@
     level,
 ):
     step = pl.program_id(0)
-    cells_z, cells_x, cells_y = c_ref.shape[1], c_ref.shape[2], c_ref.shape[3]
+    cells_x, cells_y = c_ref.shape[2], c_ref.shape[3]
+    cells_z = c_ref.shape[0] * c_ref.shape[1] // first_steps
     rim = h_ref.shape[2]
     orbitals, some_x, length = psi_ref.shape[0], psi_ref.shape[1], psi_ref.shape[2]
-    block = 64
+    block = 128
     many = 8
-    group = 8
+    group = 16
 
     @pl.when(step < first_steps)
     def _():
@@ -224,9 +225,9 @@
 
         def planes(i, carry):
             z0 = i * block
-            own = dot(c_ref[0, pl.ds(z0, block)].reshape(block * cells_x, cells_y), my)
+            own = dot(c_ref[step, pl.ds(z0, block)].reshape(block * cells_x, cells_y), my)
             own = own.astype(BF16).reshape(block, cells_x, cells_y)
-            far = dot(h_ref[0, pl.ds(z0, block)].reshape(block * rim, cells_y), my)
+            far = dot(h_ref[step, pl.ds(z0, block)].reshape(block * rim, cells_y), my)
             far = far.astype(BF16).reshape(block, rim, cells_y)
             for p in range(0, block, many):
                 some = range(p, p + many)
@@ -307,22 +308,16 @@
             q_ref[i, rows : rows + CODE_ROWS, :] = code_rows
             return carry
 
-        lax.fori_loop(0, q_ref.shape[0], quantise, 0, unroll=4)
+        lax.fori_loop(0, q_ref.shape[0], quantise, 0, unroll=16)
 
 
 def density(occupations, slot_orbital, c, halo, my, ax, mz, dht, owners):
     orbitals, length, cells_x, cells_y = c.shape
-    chunks = 2
-    part = length // chunks
-    first_steps = orbitals * chunks
-    some_x = 8
+    first_steps = orbitals
+    some_x = 16
     pitch = cells_x + 8
     smem = pl.BlockSpec(memory_space=pltpu.SMEM)
     rows = (length // owners) * cells_x + CODE_ROWS
-
-    def at_first(s):
-        s = jnp.minimum(s, first_steps - 1)
-        return (s // chunks, s % chunks, 0, 0)
 
     return pl.pallas_call(
         functools.partial(density_kernel, first_steps, pitch),
@@ -330,8 +325,8 @@
         in_specs=[
             smem,
             smem,
-            pl.BlockSpec((1, part, cells_x, cells_y), at_first),
-            pl.BlockSpec((1, part, halo.shape[2], cells_y), at_first),
+            pl.BlockSpec(memory_space=pltpu.VMEM),
+            pl.BlockSpec(memory_space=pltpu.VMEM),
             whole(my),
             whole(ax),
             whole(mz),
@@ -351,11 +346,11 @@
             jax.ShapeDtypeStruct((8, cells_y), F32),
         ],
         scratch_shapes=[
-            pltpu.VMEM((orbitals * length * pitch, cells_y), F32),
-            pltpu.VMEM((length * pitch, cells_y), F32),
+            pltpu.VMEM(((orbitals * length + 1) * pitch, cells_y), F32),
+            pltpu.VMEM(((length + 1) * pitch, cells_y), F32),
             pltpu.SMEM((3,), F32),
         ],
-        compiler_params=params(1, 30),
+        compiler_params=params(1, 36),
         name="density",
     )(occupations, slot_orbital, c, halo, my, ax, mz, dht)
 
@@ -459,8 +454,8 @@
             jax.ShapeDtypeStruct((orbitals, 16, cells_y), F32),
         ],
         scratch_shapes=[
-            pltpu.VMEM((length * pitch, cells_y), F32),
-            pltpu.VMEM((length * pitch, cells_y), F32),
+            pltpu.VMEM(((length + 1) * pitch, cells_y), F32),
+            pltpu.VMEM(((length + 1) * pitch, cells_y), F32),
         ],
         compiler_params=params(1, 26),
         cost_estimate=pl.CostEstimate(
@@ -579,10 +574,10 @@
     values,
 ):
     step = pl.program_id(0)
-    orbitals, some_x, length, cells_y = psi_ref.shape
+    orbitals, cells_x, length, cells_y = psi_ref.shape
+    some_x = cells_x // pl.num_programs(0)
     owners = got_ref.shape[0]
     per = length // owners
-    cells_x = some_x * pl.num_programs(0)
     rim = rim_ref.shape[2] // 2
     first = pl.multiple_of((lax.axis_index("orb") * per) // 8 * 8, 8)
 
@@ -595,10 +590,10 @@
                 waves[at, :] = found[k * cells_x : (k + 1) * cells_x]
             return carry
 
-        lax.fori_loop(0, owners, unpack, 0, unroll=4)
+        lax.fori_loop(0, owners, unpack, 0, unroll=16)
         sums_ref[...] = kin_ref[...]
 
-    group = 8
+    group = 16
     energy = [jnp.zeros((8, cells_y), F32) for _ in range(orbitals)]
     for local in range(0, some_x, group):
         x = step * some_x + local
@@ -614,7 +609,7 @@
             slab_ref[local + k] = own[:, k * cells_y : (k + 1) * cells_y]
         products = []
         for o in range(orbitals):
-            psi = jnp.concatenate([psi_ref[o, local + k] for k in range(group)], axis=1)
+            psi = jnp.concatenate([psi_ref[o, x + k] for k in range(group)], axis=1)
             psi = psi.astype(F32)
             product = field * psi
             products.append(product.astype(BF16))
@@ -642,7 +637,7 @@
             back_ref[o, z] = turned(o, z, 0, some_x).astype(BF16)
         return carry
 
-    lax.fori_loop(0, length, rows, 0, unroll=8)
+    lax.fori_loop(0, length, rows, 0, unroll=16)
 
     @pl.when(step == 0)
     def _():
@@ -651,7 +646,7 @@
                 head[o, z] = turned(o, z, 0, rim)
             return carry
 
-        lax.fori_loop(0, length, keep, 0, unroll=8)
+        lax.fori_loop(0, length, keep, 0, unroll=16)
 
     @pl.when(step == pl.num_programs(0) - 1)
     def _():
@@ -661,7 +656,7 @@
                 rim_ref[o, z] = both.astype(BF16)
             return carry
 
-        lax.fori_loop(0, length, send, 0, unroll=8)
+        lax.fori_loop(0, length, send, 0, unroll=16)
 
 
 def field(got, psi, kin_sums, dht, tz):
@@ -675,7 +670,7 @@
         grid=(cells_x // some_x,),
         in_specs=[
             pl.BlockSpec(memory_space=pltpu.VMEM),
-            pl.BlockSpec((orbitals, some_x, length, cells_y), lambda i: (0, i, 0, 0)),
+            pl.BlockSpec(memory_space=pltpu.VMEM),
             whole(kin_sums),
             whole(dht),
             whole(tz),
@@ -693,12 +688,12 @@
             jax.ShapeDtypeStruct(kin_sums.shape, F32),
         ],
         scratch_shapes=[
-            pltpu.VMEM((length * pitch, cells_y), F32),
-            pltpu.VMEM((orbitals * length * turn_pitch, cells_y), F32),
+            pltpu.VMEM(((length + 1) * pitch, cells_y), F32),
+            pltpu.VMEM(((orbitals * length + 1) * turn_pitch, cells_y), F32),
             pltpu.VMEM((orbitals, length, rim, cells_y), F32),
-            pltpu.VMEM((2, length, 8 * cells_y), F32),
-        ],
-        compiler_params=params(1, 26),
+            pltpu.VMEM((1, length, 16 * cells_y), F32),
+        ],
+        compiler_params=params(1, 30),
         name="field",
     )(got, psi, kin_sums, dht, tz)
 

time: 137 us -> 134 us (0.978)
  Pallas kernels: 65.1 us -> 62.2 us
    pallas_call x1, Pallas kernels: 15.4 us -> 13.5 us  [density(): pl.pallas_call(functools.partial(density_kernel, first_steps, pitch), gri...]
    pallas_call x1, Pallas kernels: 9.99 us -> 8.62 us  [field(): pl.pallas_call(functools.partial(field_kernel, pitch, turn_pitch), grid=(...]
where the time goes in v6:
time: 134 us; the launch traced here: 133 us
  Pallas kernels  62.2 us (46%)
  blocking collectives  39 us (29%)
  starting transfers between devices  14.4 us (11%)
  waiting for transfers between devices  14 us (10%)
  local copies, waits for them, and re-layouts  2.87 us (2%)
    all_to_all x1, blocking collectives, to_all(): lax.all_to_all(blocks, 'orb', split_axis=0, concat_axis=0, tiled=True)  36 us
    pallas_call x1, Pallas kernels, kinetic(): pl.pallas_call(functools.partial(kinetic_kernel, pitch), grid=(orbitals,)...  18.5 us
    pallas_call x1, Pallas kernels, density(): pl.pallas_call(functools.partial(density_kernel, first_steps, pitch), gri...  13.5 us
    pallas_call x1, Pallas kernels, update(): pl.pallas_call(update_kernel, grid=(orbitals, chunks), in_specs=[whole(su...  12.7 us
    all_to_all x1, waiting for transfers between devices, to_all(): lax.all_to_all(blocks, 'orb', split_axis=0, concat_axis=0, tiled=True)  11.4 us
    all_to_all x1, starting transfers between devices, to_all(): lax.all_to_all(blocks, 'orb', split_axis=0, concat_axis=0, tiled=True)  11.3 us
    pallas_call x1, Pallas kernels, field(): pl.pallas_call(functools.partial(field_kernel, pitch, turn_pitch), grid=(...  8.62 us
    pallas_call x2, Pallas kernels, own_rims(): pl.pallas_call(functools.partial(rims_kernel, inner, outer), grid=(1,), i...  5.77 us
  transfers between devices with their start and end apart: 5, of which 3 were waited for; matrix products, arithmetic and copies ran while one was open for 0% of the time, Pallas kernels for 27%

profile of v6, /device:TPU:1, one launch (start us, length us, event | category | flops | bytes accessed | tf_op | source)
XLA Modules:
  0.0 133.2 jit_solution(4268640206321771327)
XLA Ops:
  0.6 2.2 %own_rims.2 = (bf16[3,128,16,128]{3,2,1,0:T(8,128)(2,1)S(1)}, f32[8,128]{1,0:T(8,128)S(1)}) custom-call(bf16[3,128,64,128]{3,2,1,0:T(8,128)(2,1)} %c_ref.5, bf16[3,128,64,128]{3,2,1,0:T(8,128)(2,1)} %c_ref.5), custom_call_target="tpu_custom_call" | custom-call | tf_op jit(solution)/shard_map/own_rims/pallas_call | solution.py:179
  2.8 1.5 %collective-permute-start = (bf16[3,128,16,128]{3,2,1,0:T(8,128)(2,1)S(1)}, bf16[3,128,16,128]{3,2,1,0:T(8,128)(2,1)S(1)}, u32[]{:S(2)}, u32[]{:S(2)}) collective-permute-start(bf16[3,128,16,128]{3,2,1,0:T(8,128)(2,1)S(1)} %get-tuple-element.18), channel_id=1, source_target_pairs={{0,1},{1,0},{2,3},{3,2},{4,5},{5,4},{6,7},{7,6},{8,9},{9,8},{10,11... | collective-permute-start | bytes 4718600 | tf_op jit(solution)/shard_map/ppermute | solution.py:785
  4.3 0.0 slice-start
  4.3 0.0 slice-start.1
  4.3 0.0 copy-start.3
  4.4 0.0 copy-start.5
  4.4 0.0 copy-start.9
  4.4 0.0 copy-start.10
  4.4 0.0 copy-start.11
  4.4 3.6 %own_rims.3 = (bf16[3,128,16,128]{3,2,1,0:T(8,128)(2,1)}, f32[8,128]{1,0:T(8,128)}) custom-call(bf16[3,128,64,128]{3,2,1,0:T(8,128)(2,1)} %c_ref.5, bf16[3,128,64,128]{3,2,1,0:T(8,128)(2,1)} %c_ref.5, f32[8,128]{1,0:T(8,128)S(1)} %get-tuple-element.20.rest_0_), custom_call_target="tpu_custom_call" | custom-call | tf_op jit(solution)/shard_map/own_rims/pallas_call | solution.py:179
  8.0 0.1 collective-permute-start.1
  8.0 0.0 collective-permute-done.h_ref.near_ref
  8.0 0.0 slice-done
  8.0 0.7 slice-done.1
  8.8 0.0 copy-done.3
  8.8 0.0 copy-done.4
  8.8 0.0 copy-done.5
  8.8 0.0 copy-done.9
  8.8 0.0 copy-done.10
  8.8 0.0 copy-done.11
  8.8 0.0 copy-start.1
  8.8 13.5 %density.1 = (bf16[3,64,128,128]{3,2,1,0:T(8,128)(2,1)}, s16[64,136,128]{2,1,0:T(8,128)(2,1)}, f32[8,128]{1,0:T(8,128)S(1)}) custom-call(s32[192]{0:T(256)S(1)} %copy-done.10, s32[192]{0:T(256)S(1)} %copy-done.11, bf16[3,128,64,128]{3,2,1,0:T(8,128)(2,1)S(1)} %bitcast.4, bf16[3,128,16,128]{3,2,1,0:T(8,128)(2,1)S(1)} %collective-permute-done.h_ref.near_ref, ...), custom_call_target="tpu_custom_call" | custom-call | tf_op jit(solution)/shard_map/density/pallas_call | solution.py:322
  22.3 0.0 copy-done.1
  22.3 0.0 copy-start.14
  22.3 11.3 %all-to-all-start = ((s16[64,136,128]{2,1,0:T(8,128)(2,1)}), s16[64,136,128]{2,1,0:T(8,128)(2,1)S(1)}, u32[]{:S(2)}, u32[]{:S(2)}) async-start(s16[64,136,128]{2,1,0:T(8,128)(2,1)} %get-tuple-element.19), calls=%async_computation | async-start | bytes 4456448 | tf_op jit(solution)/shard_map/all_to_all | solution.py:793
  33.7 0.0 collective-permute-done.1.far_ref
  33.7 0.0 copy-done.13
  33.7 0.0 copy-done.14
  33.7 0.0 copy-start.2
  33.7 1.4 %copy-done.2 = bf16[3,128,16,128]{3,2,1,0:T(8,128)(2,1)S(1)} copy-done((bf16[3,128,16,128]{3,2,1,0:T(8,128)(2,1)S(1)}, bf16[3,128,16,128]{3,2,1,0:T(8,128)(2,1)}, u32[]{:S(2)}) %copy-start.2) | copy-done | bytes 1572888
  35.1 18.5 %kinetic.1 = (s16[3,128,64,128]{3,2,1,0:T(8,128)(2,1)}, f32[3,128,128]{2,1,0:T(8,128)S(1)}, f32[3,16,128]{2,1,0:T(8,128)S(1)}) custom-call(bf16[3,128,64,128]{3,2,1,0:T(8,128)(2,1)} %c_ref.5, bf16[3,128,16,128]{3,2,1,0:T(8,128)(2,1)S(1)} %copy-done.2, bf16[3,128,16,128]{3,2,1,0:T(8,128)(2,1)} %collective-permute-done.1.far_ref, ...), custom_call_target="tpu_custom_call" | custom-call | flops 9663676416 | bytes 22020096 | tf_op jit(solution)/shard_map/kinetic/pallas_call | solution.py:434
  53.6 11.4 %all-to-all-done.got_ref = s16[64,136,128]{2,1,0:T(8,128)(2,1)S(1)} async-done(((s16[64,136,128]{2,1,0:T(8,128)(2,1)}), s16[64,136,128]{2,1,0:T(8,128)(2,1)S(1)}, u32[]{:S(2)}, u32[]{:S(2)}) %all-to-all-start) | async-done | bytes 2228256 | tf_op jit(solution)/shard_map/all_to_all | solution.py:793
  65.0 0.9 slab_sum.1
  65.9 3.0 %all_gather.3.slab_ref = f32[2,128,128]{2,1,0:T(8,128)S(1)} all-gather(f32[2,64,128]{2,1,0:T(8,128)S(1)} %bitcast.5), channel_id=1, replica_groups=mesh['orb'=64,'grid'=2] {'grid'}, dimensions={1}, use_global_device_ids=true | all-gather | bytes 196608 | tf_op jit(solution)/shard_map/all_gather | solution.py:837
  68.9 0.0 copy-done.6
  68.9 0.0 copy-done.7
  68.9 0.0 copy-done.12
  68.9 2.2 %solve.1 = s16[64,136,128]{2,1,0:T(8,128)(2,1)S(1)} custom-call(f32[128]{0:T(128)S(1)} %copy-done.12, f32[2,128,128]{2,1,0:T(8,128)S(1)} %all_gather.3.slab_ref, f32[128,128]{1,0:T(8,128)S(1)} %copy-done.6, f32[128,128]{1,0:T(8,128)S(1)} %copy-done.7), custom_call_target="tpu_custom_call" | custom-call | tf_op jit(solution)/shard_map/solve/pallas_call | solution.py:550
  71.1 36.0 %all_to_all.10.got_ref = s16[64,136,128]{2,1,0:T(8,128)(2,1)S(1)} all-to-all(s16[64,136,128]{2,1,0:T(8,128)(2,1)S(1)} %solve.1), channel_id=1, replica_groups=mesh['orb'=64,'grid'=2] {'orb'}, dimensions={0} | all-to-all | bytes 4456448 | tf_op jit(solution)/shard_map/all_to_all | solution.py:793
  107.1 0.0 copy-done
  107.1 8.6 %field.1 = (bf16[3,128,64,128]{3,2,1,0:T(8,128)(2,1)}, bf16[3,128,16,128]{3,2,1,0:T(8,128)(2,1)}, f32[64,8,128]{2,1,0:T(8,128)S(1)}, f32[3,16,128]{2,1,0:T(8,128)S(1)}) custom-call(s16[64,136,128]{2,1,0:T(8,128)(2,1)S(1)} %all_to_all.10.got_ref, bf16[3,64,128,128]{3,2,1,0:T(8,128)(2,1)S(1)} %copy-done, ...), custom_call_target="tpu_custom_call" | custom-call | tf_op jit(solution)/shard_map/field/pallas_call | solution.py:668
  115.7 1.5 %collective-permute-start.3 = (bf16[3,128,16,128]{3,2,1,0:T(8,128)(2,1)}, bf16[3,128,16,128]{3,2,1,0:T(8,128)(2,1)S(1)}, u32[]{:S(2)}, u32[]{:S(2)}) collective-permute-start(bf16[3,128,16,128]{3,2,1,0:T(8,128)(2,1)} %get-tuple-element.27), channel_id=1, source_target_pairs={{0,1},{1,0},{2,3},{3,2},{4,5},{5,4},{6,7},{7,6},{8,9},{9,8},{10,11... | collective-permute-start | bytes 4718600 | tf_op jit(solution)/shard_map/ppermute | solution.py:785
  117.2 0.0 collective-permute-start.2
  117.3 0.6 copy.19
  117.9 2.3 %collective-permute-done.2.other_ref = f32[3,16,128]{2,1,0:T(8,128)S(1)} collective-permute-done((f32[3,16,128]{2,1,0:T(8,128)S(1)}, f32[3,16,128]{2,1,0:T(8,128)S(1)}, u32[]{:S(2)}, u32[]{:S(2)}) %collective-permute-start.2) | collective-permute-done | bytes 24608 | tf_op jit(solution)/shard_map/ppermute | solution.py:785
  120.2 0.3 collective-permute-done.3.rim_ref
  120.5 0.0 copy-done.8
  120.5 12.7 %update.1 = (bf16[3,128,64,128]{3,2,1,0:T(8,128)(2,1)}, f32[3]{0:T(128)}) custom-call(f32[3,16,128]{2,1,0:T(8,128)S(1)} %get-tuple-element.25.sums_ref, f32[3,16,128]{2,1,0:T(8,128)S(1)} %collective-permute-done.2.other_ref, bf16[3,128,64,128]{3,2,1,0:T(8,128)(2,1)} %get-tuple-element.26.back_ref, ...), custom_call_target="tpu_custom_call" | custom-call | tf_op jit(solution)/shard_map/update/pallas_call | solution.py:760
  (9 shorter events, 0.0 us)
Async XLA Ops:
  2.8 5.2 %collective-permute-start = (bf16[3,128,16,128]{3,2,1,0:T(8,128)(2,1)S(1)}, bf16[3,128,16,128]{3,2,1,0:T(8,128)(2,1)S(1)}, u32[]{:S(2)}, u32[]{:S(2)}) collective-permute-start(bf16[3,128,16,128]{3,2,1,0:T(8,128)(2,1)S(1)} %get-tuple-element.18), channel_id=1, source_target_pairs={{0,1},{1,0},{2,3},{3,2},{4,5},{5,4},{6,7},{7,6},{8,9},{9,8},{10,11... | collective-permute-start | bytes 4718600 | tf_op jit(solution)/shard_map/ppermute | solution.py:785
  4.3 3.7 %slice-start = ((s8[6291456]{0:T(1024)(128)(4,1)}), s8[4194304]{0:T(1024)(128)(4,1)S(1)}, s32[]{:S(2)}) async-start(s8[6291456]{0:T(1024)(128)(4,1)} %bitcast.3), calls=%async_computation.2 | async-start | bytes 8388608
  4.3 4.4 %slice-start.1 = ((s8[6291456]{0:T(1024)(128)(4,1)}), s8[2097152]{0:T(1024)(128)(4,1)S(1)}, s32[]{:S(2)}) async-start(s8[6291456]{0:T(1024)(128)(4,1)} %bitcast.3), calls=%async_computation.3 | async-start | bytes 4194304
  4.3 4.4 %copy-start.3 = (bf16[128,384]{1,0:T(8,128)(2,1)S(1)}, bf16[128,384]{1,0:T(8,128)(2,1)}, u32[]{:S(2)}) copy-start(bf16[128,384]{1,0:T(8,128)(2,1)} %constant.35.clone.dht_ref) | copy-start | bytes 294916
  4.4 4.4 %copy-start.4 = (bf16[128,128]{1,0:T(8,128)(2,1)S(1)}, bf16[128,128]{1,0:T(8,128)(2,1)}, u32[]{:S(2)}) copy-start(bf16[128,128]{1,0:T(8,128)(2,1)} %constant.38.clone.mz_ref.ty_ref) | copy-start | bytes 98308
  4.4 4.4 %copy-start.5 = (bf16[128,128]{1,0:T(8,128)(2,1)S(1)}, bf16[128,128]{1,0:T(8,128)(2,1)}, u32[]{:S(2)}) copy-start(bf16[128,128]{1,0:T(8,128)(2,1)} %constant.36.clone.my_ref.tz_ref) | copy-start | bytes 98308
  4.4 4.4 %copy-start.9 = (bf16[64,80]{1,0:T(8,128)(2,1)S(1)}, bf16[64,80]{1,0:T(8,128)(2,1)}, u32[]{:S(2)}) copy-start(bf16[64,80]{1,0:T(8,128)(2,1)} %constant.37.clone.ax_ref) | copy-start | bytes 30724
  4.4 4.4 %copy-start.10 = (s32[192]{0:T(256)S(1)}, s32[192]{0:T(256)}, u32[]{:S(2)}) copy-start(s32[192]{0:T(256)} %occ_ref.1) | copy-start | bytes 2308
  4.4 4.4 %copy-start.11 = (s32[192]{0:T(256)S(1)}, s32[192]{0:T(256)}, u32[]{:S(2)}) copy-start(s32[192]{0:T(256)} %slot_ref.1) | copy-start | bytes 2308
  8.0 25.7 %collective-permute-start.1 = (bf16[3,128,16,128]{3,2,1,0:T(8,128)(2,1)}, bf16[3,128,16,128]{3,2,1,0:T(8,128)(2,1)}, u32[]{:S(2)}, u32[]{:S(2)}) collective-permute-start(bf16[3,128,16,128]{3,2,1,0:T(8,128)(2,1)} %get-tuple-element.21), channel_id=1, source_target_pairs={{0,1},{1,0},{2,3},{3,2},{4,5},{5,4},{6,7},{7,6},{8,9},{9,8},{10,11... | collective-permute-start | bytes 4718600 | tf_op jit(solution)/shard_map/ppermute | solution.py:785
  8.8 13.5 %copy-start.1 = (bf16[3,128,16,128]{3,2,1,0:T(8,128)(2,1)}, bf16[3,128,16,128]{3,2,1,0:T(8,128)(2,1)S(1)}, u32[]{:S(2)}) copy-start(bf16[3,128,16,128]{3,2,1,0:T(8,128)(2,1)S(1)} %collective-permute-done.h_ref.near_ref) | copy-start | bytes 4718596
  22.3 11.4 %copy-start.13 = (bf16[128,128]{1,0:T(8,128)(2,1)S(1)}, bf16[128,128]{1,0:T(8,128)(2,1)}, u32[]{:S(2)}) copy-start(bf16[128,128]{1,0:T(8,128)(2,1)} %constant.39.clone.dy_ref.dz_ref) | copy-start | bytes 98308
  22.3 11.4 %copy-start.14 = (bf16[64,96]{1,0:T(8,128)(2,1)S(1)}, bf16[64,96]{1,0:T(8,128)(2,1)}, u32[]{:S(2)}) copy-start(bf16[64,96]{1,0:T(8,128)(2,1)} %constant.40.clone.dx_ref) | copy-start | bytes 36868
  22.3 42.7 %all-to-all-start = ((s16[64,136,128]{2,1,0:T(8,128)(2,1)}), s16[64,136,128]{2,1,0:T(8,128)(2,1)S(1)}, u32[]{:S(2)}, u32[]{:S(2)}) async-start(s16[64,136,128]{2,1,0:T(8,128)(2,1)} %get-tuple-element.19), calls=%async_computation | async-start | bytes 4456448 | tf_op jit(solution)/shard_map/all_to_all | solution.py:793
  33.7 1.4 %copy-start.2 = (bf16[3,128,16,128]{3,2,1,0:T(8,128)(2,1)S(1)}, bf16[3,128,16,128]{3,2,1,0:T(8,128)(2,1)}, u32[]{:S(2)}) copy-start(bf16[3,128,16,128]{3,2,1,0:T(8,128)(2,1)} %copy-done.1) | copy-start | bytes 4718596
  53.6 15.3 %copy-start.6 = (f32[128,128]{1,0:T(8,128)S(1)}, f32[128,128]{1,0:T(8,128)}, u32[]{:S(2)}) copy-start(f32[128,128]{1,0:T(8,128)} %constant.42.clone.dht_ref) | copy-start | bytes 196612
  53.6 15.3 %copy-start.7 = (f32[128,128]{1,0:T(8,128)S(1)}, f32[128,128]{1,0:T(8,128)}, u32[]{:S(2)}) copy-start(f32[128,128]{1,0:T(8,128)} %constant.43.clone.curve_ref) | copy-start | bytes 196612
  53.6 15.3 %copy-start.12 = (f32[128]{0:T(128)S(1)}, f32[128]{0:T(128)}, u32[]{:S(2)}) copy-start(f32[128]{0:T(128)} %constant.41.clone.curve_z_ref) | copy-start | bytes 1540
  68.9 38.2 %copy-start = (bf16[3,64,128,128]{3,2,1,0:T(8,128)(2,1)S(1)}, bf16[3,64,128,128]{3,2,1,0:T(8,128)(2,1)}, u32[]{:S(2)}) copy-start(bf16[3,64,128,128]{3,2,1,0:T(8,128)(2,1)} %get-tuple-element.24.psi_ref) | copy-start | bytes 18874372
  107.1 13.4 %copy-start.8 = (bf16[64,80]{1,0:T(8,128)(2,1)S(1)}, bf16[64,80]{1,0:T(8,128)(2,1)}, u32[]{:S(2)}) copy-start(bf16[64,80]{1,0:T(8,128)(2,1)} %constant.44.clone.tx_ref) | copy-start | bytes 30724
  115.7 4.8 %collective-permute-start.3 = (bf16[3,128,16,128]{3,2,1,0:T(8,128)(2,1)}, bf16[3,128,16,128]{3,2,1,0:T(8,128)(2,1)S(1)}, u32[]{:S(2)}, u32[]{:S(2)}) collective-permute-start(bf16[3,128,16,128]{3,2,1,0:T(8,128)(2,1)} %get-tuple-element.27), channel_id=1, source_target_pairs={{0,1},{1,0},{2,3},{3,2},{4,5},{5,4},{6,7},{7,6},{8,9},{9,8},{10,11... | collective-permute-start | bytes 4718600 | tf_op jit(solution)/shard_map/ppermute | solution.py:785
  117.2 2.9 %collective-permute-start.2 = (f32[3,16,128]{2,1,0:T(8,128)S(1)}, f32[3,16,128]{2,1,0:T(8,128)S(1)}, u32[]{:S(2)}, u32[]{:S(2)}) collective-permute-start(f32[3,16,128]{2,1,0:T(8,128)S(1)} %get-tuple-element.25.sums_ref), channel_id=1, source_target_pairs={{0,1},{1,0},{2,3},{3,2},{4,5},{5,4},{6,7},{7,6},{8,9},{9,8},{10,11... | collective-permute-start | bytes 73736 | tf_op jit(solution)/shard_map/ppermute | solution.py:785

commit v7 on v6

--- a/solution.py
+++ b/solution.py
@@ -204,6 +204,7 @@
     dht_ref,
     psi_ref,
     q_ref,
+    rims_ref,
     peak,
     mid,
     waves,
@@ -222,6 +223,9 @@
     def _():
         my = my_ref[...]
         ax = ax_ref[...]
+        low = c_ref[step, :, cells_x - 16 : cells_x].astype(F32)[:, 0:8]
+        high = c_ref[step, :, 0:16].astype(F32)[:, 8:16]
+        rims_ref[0] = jnp.concatenate([low, high], axis=1).astype(BF16)
 
         def planes(i, carry):
             z0 = i * block
@@ -338,11 +342,15 @@
                 lambda s: (0, jnp.maximum(s - first_steps, 0), 0, 0),
             ),
             pl.BlockSpec((owners, rows, cells_y), lambda s: (0, 0, 0)),
+            pl.BlockSpec(
+                (1, *halo.shape[1:]), lambda s: (jnp.minimum(s, first_steps - 1), 0, 0, 0)
+            ),
             pl.BlockSpec((8, cells_y), lambda s: (0, 0)),
         ],
         out_shape=[
             pltpu.HBM((orbitals, cells_x, length, cells_y), BF16),
             pltpu.HBM((owners, rows, cells_y), jnp.int16),
+            pltpu.HBM(halo.shape, BF16),
             jax.ShapeDtypeStruct((8, cells_y), F32),
         ],
         scratch_shapes=[
@@ -350,7 +358,7 @@
             pltpu.VMEM(((length + 1) * pitch, cells_y), F32),
             pltpu.SMEM((3,), F32),
         ],
-        compiler_params=params(1, 36),
+        compiler_params=params(1, 38),
         name="density",
     )(occupations, slot_orbital, c, halo, my, ax, mz, dht)
 
@@ -809,10 +817,9 @@
     waves = curve(length)
 
     c = in_hbm(coefficients)
-    own_near, mark = own_rims(c, 0, 8)
+    own_near, _ = own_rims(c, 0, 8)
     near = to_other(own_near)
-    far = to_other(own_rims(c, 8, 16, mark)[0])
-    psi, coded, peak = density(
+    psi, coded, own_far, peak = density(
         occupations,
         slot_orbital,
         coefficients,
@@ -824,6 +831,7 @@
         owners,
     )
     got = to_all(coded)
+    far = to_other(own_far)
     kin, steps, kin_sums = kinetic(
         c,
         near,

time: 134 us -> 134 us (level)
  waiting for transfers between devices: 14 us -> 16.7 us
  Pallas kernels: 62.2 us -> 59.6 us
    ppermute x4, waiting for transfers between devices: 2.62 us -> 5.65 us  [to_other(): return lax.ppermute(array, 'grid', [(0, 1), (1, 0)])]
    pallas_call x2 -> x1, Pallas kernels: 5.77 us -> 2.95 us  [own_rims(): pl.pallas_call(functools.partial(rims_kernel, inner, outer), grid=(1,), i...]
    unnamed x35 -> x33, local copies, waits for them, and re-layouts: 2.85 us -> 2.11 us
  transfers between devices with their start and end apart: 5 -> 5, of which waited for: 3 -> 4; matrix products, arithmetic and copies ran while one was open for 0% -> 0% of each run, Pallas kernels for 27% -> 14%
where the time goes in v7:
time: 134 us; the launch traced here: 133 us
  Pallas kernels  59.6 us (44%)
  blocking collectives  39.4 us (29%)
  waiting for transfers between devices  16.7 us (12%)
  starting transfers between devices  14.7 us (11%)
  local copies, waits for them, and re-layouts  2.13 us (2%)
    all_to_all x1, blocking collectives, to_all(): lax.all_to_all(blocks, 'orb', split_axis=0, concat_axis=0, tiled=True)  36.1 us
    pallas_call x1, Pallas kernels, kinetic(): pl.pallas_call(functools.partial(kinetic_kernel, pitch), grid=(orbitals,)...  18.4 us
    pallas_call x1, Pallas kernels, density(): pl.pallas_call(functools.partial(density_kernel, first_steps, pitch), gri...  13.9 us
    pallas_call x1, Pallas kernels, update(): pl.pallas_call(update_kernel, grid=(orbitals, chunks), in_specs=[whole(su...  12.7 us
    all_to_all x1, starting transfers between devices, to_all(): lax.all_to_all(blocks, 'orb', split_axis=0, concat_axis=0, tiled=True)  11.3 us
    all_to_all x1, waiting for transfers between devices, to_all(): lax.all_to_all(blocks, 'orb', split_axis=0, concat_axis=0, tiled=True)  11 us
    pallas_call x1, Pallas kernels, field(): pl.pallas_call(functools.partial(field_kernel, pitch, turn_pitch), grid=(...  8.56 us
    ppermute x4, waiting for transfers between devices, to_other(): return lax.ppermute(array, 'grid', [(0, 1), (1, 0)])  5.65 us
  transfers between devices with their start and end apart: 5, of which 4 were waited for; matrix products, arithmetic and copies ran while one was open for 0% of the time, Pallas kernels for 14%

profile of v7, /device:TPU:1, one launch (start us, length us, event | category | flops | bytes accessed | tf_op | source)
XLA Modules:
  0.0 133.3 jit_solution(12721501590228187001)
XLA Ops:
  0.6 0.0 copy-start.4
  0.6 0.0 copy-start.5
  0.7 0.0 copy-start.6
  0.7 0.0 copy-start.10
  0.7 0.0 copy-start.11
  0.7 0.0 copy-start
  0.7 0.0 copy-start.12
  0.7 2.9 %own_rims.1 = (bf16[3,128,16,128]{3,2,1,0:T(8,128)(2,1)S(1)}, f32[8,128]{1,0:T(8,128)}) custom-call(bf16[3,128,64,128]{3,2,1,0:T(8,128)(2,1)} %c_ref.5, bf16[3,128,64,128]{3,2,1,0:T(8,128)(2,1)} %c_ref.5), custom_call_target="tpu_custom_call" | custom-call | tf_op jit(solution)/shard_map/own_rims/pallas_call | solution.py:179
  3.7 1.4 %collective-permute-start = (bf16[3,128,16,128]{3,2,1,0:T(8,128)(2,1)S(1)}, bf16[3,128,16,128]{3,2,1,0:T(8,128)(2,1)S(1)}, u32[]{:S(2)}, u32[]{:S(2)}) collective-permute-start(bf16[3,128,16,128]{3,2,1,0:T(8,128)(2,1)S(1)} %get-tuple-element.17), channel_id=1, source_target_pairs={{0,1},{1,0},{2,3},{3,2},{4,5},{5,4},{6,7},{7,6},{8,9},{9,8},{10,11... | collective-permute-start | bytes 4718600 | tf_op jit(solution)/shard_map/ppermute | solution.py:793
  5.1 3.0 %collective-permute-done.h_ref.near_ref = bf16[3,128,16,128]{3,2,1,0:T(8,128)(2,1)S(1)} collective-permute-done((bf16[3,128,16,128]{3,2,1,0:T(8,128)(2,1)S(1)}, bf16[3,128,16,128]{3,2,1,0:T(8,128)(2,1)S(1)}, u32[]{:S(2)}, u32[]{:S(2)}) %collective-permute-start) | collective-permute-done | bytes 1572896 | tf_op jit(solution)/shard_map/ppermute | solution.py:793
  8.1 0.0 copy-done.4
  8.1 0.0 copy-done.5
  8.1 0.0 copy-done.6
  8.1 0.0 copy-done.10
  8.1 0.0 copy-done.11
  8.1 0.0 copy-done
  8.2 0.0 copy-done.12
  8.2 0.0 copy-start.2
  8.2 13.9 %density.1 = (bf16[3,64,128,128]{3,2,1,0:T(8,128)(2,1)}, s16[64,136,128]{2,1,0:T(8,128)(2,1)}, bf16[3,128,16,128]{3,2,1,0:T(8,128)(2,1)}, f32[8,128]{1,0:T(8,128)S(1)}) custom-call(s32[192]{0:T(256)S(1)} %copy-done.11, s32[192]{0:T(256)S(1)} %copy-done.12, bf16[3,128,64,128]{3,2,1,0:T(8,128)(2,1)S(1)} %copy-done, ...), custom_call_target="tpu_custom_call" | custom-call | tf_op jit(solution)/shard_map/density/pallas_call | solution.py:326
  22.1 0.0 copy-done.2
  22.1 0.4 collective-permute-start.1
  22.5 0.0 copy-start.14
  22.5 0.0 copy-start.15
  22.5 11.3 %all-to-all-start = ((s16[64,136,128]{2,1,0:T(8,128)(2,1)}), s16[64,136,128]{2,1,0:T(8,128)(2,1)S(1)}, u32[]{:S(2)}, u32[]{:S(2)}) async-start(s16[64,136,128]{2,1,0:T(8,128)(2,1)} %get-tuple-element.18), calls=%async_computation | async-start | bytes 4456448 | tf_op jit(solution)/shard_map/all_to_all | solution.py:801
  33.8 0.0 collective-permute-done.1.far_ref
  33.8 0.0 copy-done.14
  33.8 0.0 copy-done.15
  33.8 0.0 copy-start.3
  33.8 1.4 %copy-done.3 = bf16[3,128,16,128]{3,2,1,0:T(8,128)(2,1)S(1)} copy-done((bf16[3,128,16,128]{3,2,1,0:T(8,128)(2,1)S(1)}, bf16[3,128,16,128]{3,2,1,0:T(8,128)(2,1)}, u32[]{:S(2)}) %copy-start.3) | copy-done | bytes 1572888
  35.2 18.4 %kinetic.1 = (s16[3,128,64,128]{3,2,1,0:T(8,128)(2,1)}, f32[3,128,128]{2,1,0:T(8,128)S(1)}, f32[3,16,128]{2,1,0:T(8,128)S(1)}) custom-call(bf16[3,128,64,128]{3,2,1,0:T(8,128)(2,1)} %c_ref.5, bf16[3,128,16,128]{3,2,1,0:T(8,128)(2,1)S(1)} %copy-done.3, bf16[3,128,16,128]{3,2,1,0:T(8,128)(2,1)} %collective-permute-done.1.far_ref, ...), custom_call_target="tpu_custom_call" | custom-call | flops 9663676416 | bytes 22020096 | tf_op jit(solution)/shard_map/kinetic/pallas_call | solution.py:442
  53.7 0.0 copy-start.7
  53.7 11.0 %all-to-all-done.got_ref = s16[64,136,128]{2,1,0:T(8,128)(2,1)S(1)} async-done(((s16[64,136,128]{2,1,0:T(8,128)(2,1)}), s16[64,136,128]{2,1,0:T(8,128)(2,1)S(1)}, u32[]{:S(2)}, u32[]{:S(2)}) %all-to-all-start) | async-done | bytes 2228256 | tf_op jit(solution)/shard_map/all_to_all | solution.py:801
  64.7 0.9 slab_sum.1
  65.6 3.3 %all_gather.3.slab_ref = f32[2,128,128]{2,1,0:T(8,128)S(1)} all-gather(f32[2,64,128]{2,1,0:T(8,128)S(1)} %bitcast.3), channel_id=1, replica_groups=mesh['orb'=64,'grid'=2] {'grid'}, dimensions={1}, use_global_device_ids=true | all-gather | bytes 196608 | tf_op jit(solution)/shard_map/all_gather | solution.py:845
  68.9 0.0 copy-done.7
  68.9 0.0 copy-done.8
  68.9 0.0 copy-done.13
  68.9 2.2 %solve.1 = s16[64,136,128]{2,1,0:T(8,128)(2,1)S(1)} custom-call(f32[128]{0:T(128)S(1)} %copy-done.13, f32[2,128,128]{2,1,0:T(8,128)S(1)} %all_gather.3.slab_ref, f32[128,128]{1,0:T(8,128)S(1)} %copy-done.7, f32[128,128]{1,0:T(8,128)S(1)} %copy-done.8), custom_call_target="tpu_custom_call" | custom-call | tf_op jit(solution)/shard_map/solve/pallas_call | solution.py:558
  71.1 36.1 %all_to_all.10.got_ref = s16[64,136,128]{2,1,0:T(8,128)(2,1)S(1)} all-to-all(s16[64,136,128]{2,1,0:T(8,128)(2,1)S(1)} %solve.1), channel_id=1, replica_groups=mesh['orb'=64,'grid'=2] {'orb'}, dimensions={0} | all-to-all | bytes 4456448 | tf_op jit(solution)/shard_map/all_to_all | solution.py:801
  107.2 0.0 copy-done.1
  107.2 8.6 %field.1 = (bf16[3,128,64,128]{3,2,1,0:T(8,128)(2,1)}, bf16[3,128,16,128]{3,2,1,0:T(8,128)(2,1)}, f32[64,8,128]{2,1,0:T(8,128)S(1)}, f32[3,16,128]{2,1,0:T(8,128)S(1)}) custom-call(s16[64,136,128]{2,1,0:T(8,128)(2,1)S(1)} %all_to_all.10.got_ref, bf16[3,64,128,128]{3,2,1,0:T(8,128)(2,1)S(1)} %copy-done.1, ...), custom_call_target="tpu_custom_call" | custom-call | tf_op jit(solution)/shard_map/field/pallas_call | solution.py:676
  115.8 1.5 %collective-permute-start.3 = (bf16[3,128,16,128]{3,2,1,0:T(8,128)(2,1)}, bf16[3,128,16,128]{3,2,1,0:T(8,128)(2,1)S(1)}, u32[]{:S(2)}, u32[]{:S(2)}) collective-permute-start(bf16[3,128,16,128]{3,2,1,0:T(8,128)(2,1)} %get-tuple-element.25), channel_id=1, source_target_pairs={{0,1},{1,0},{2,3},{3,2},{4,5},{5,4},{6,7},{7,6},{8,9},{9,8},{10,11... | collective-permute-start | bytes 4718600 | tf_op jit(solution)/shard_map/ppermute | solution.py:793
  117.3 0.0 collective-permute-start.2
  117.4 0.6 copy.19
  118.0 2.3 %collective-permute-done.2.other_ref = f32[3,16,128]{2,1,0:T(8,128)S(1)} collective-permute-done((f32[3,16,128]{2,1,0:T(8,128)S(1)}, f32[3,16,128]{2,1,0:T(8,128)S(1)}, u32[]{:S(2)}, u32[]{:S(2)}) %collective-permute-start.2) | collective-permute-done | bytes 24608 | tf_op jit(solution)/shard_map/ppermute | solution.py:793
  120.3 0.3 collective-permute-done.3.rim_ref
  120.6 0.0 copy-done.9
  120.6 12.7 %update.1 = (bf16[3,128,64,128]{3,2,1,0:T(8,128)(2,1)}, f32[3]{0:T(128)}) custom-call(f32[3,16,128]{2,1,0:T(8,128)S(1)} %get-tuple-element.23.sums_ref, f32[3,16,128]{2,1,0:T(8,128)S(1)} %collective-permute-done.2.other_ref, bf16[3,128,64,128]{3,2,1,0:T(8,128)(2,1)} %get-tuple-element.24.back_ref, ...), custom_call_target="tpu_custom_call" | custom-call | tf_op jit(solution)/shard_map/update/pallas_call | solution.py:768
  (5 shorter events, 0.0 us)
Async XLA Ops:
  0.6 7.5 %copy-start.4 = (bf16[128,384]{1,0:T(8,128)(2,1)S(1)}, bf16[128,384]{1,0:T(8,128)(2,1)}, u32[]{:S(2)}) copy-start(bf16[128,384]{1,0:T(8,128)(2,1)} %constant.35.clone.dht_ref) | copy-start | bytes 294916
  0.6 7.5 %copy-start.5 = (bf16[128,128]{1,0:T(8,128)(2,1)S(1)}, bf16[128,128]{1,0:T(8,128)(2,1)}, u32[]{:S(2)}) copy-start(bf16[128,128]{1,0:T(8,128)(2,1)} %constant.38.clone.mz_ref.ty_ref) | copy-start | bytes 98308
  0.7 7.5 %copy-start.6 = (bf16[128,128]{1,0:T(8,128)(2,1)S(1)}, bf16[128,128]{1,0:T(8,128)(2,1)}, u32[]{:S(2)}) copy-start(bf16[128,128]{1,0:T(8,128)(2,1)} %constant.36.clone.my_ref.tz_ref) | copy-start | bytes 98308
  0.7 7.5 %copy-start.10 = (bf16[64,80]{1,0:T(8,128)(2,1)S(1)}, bf16[64,80]{1,0:T(8,128)(2,1)}, u32[]{:S(2)}) copy-start(bf16[64,80]{1,0:T(8,128)(2,1)} %constant.37.clone.ax_ref) | copy-start | bytes 30724
  0.7 7.5 %copy-start.11 = (s32[192]{0:T(256)S(1)}, s32[192]{0:T(256)}, u32[]{:S(2)}) copy-start(s32[192]{0:T(256)} %occ_ref.1) | copy-start | bytes 2308
  0.7 7.5 %copy-start = (bf16[3,128,64,128]{3,2,1,0:T(8,128)(2,1)S(1)}, bf16[3,128,64,128]{3,2,1,0:T(8,128)(2,1)}, u32[]{:S(2)}) copy-start(bf16[3,128,64,128]{3,2,1,0:T(8,128)(2,1)} %c_ref.5) | copy-start | bytes 18874372
  0.7 7.5 %copy-start.12 = (s32[192]{0:T(256)S(1)}, s32[192]{0:T(256)}, u32[]{:S(2)}) copy-start(s32[192]{0:T(256)} %slot_ref.1) | copy-start | bytes 2308
  3.7 4.5 %collective-permute-start = (bf16[3,128,16,128]{3,2,1,0:T(8,128)(2,1)S(1)}, bf16[3,128,16,128]{3,2,1,0:T(8,128)(2,1)S(1)}, u32[]{:S(2)}, u32[]{:S(2)}) collective-permute-start(bf16[3,128,16,128]{3,2,1,0:T(8,128)(2,1)S(1)} %get-tuple-element.17), channel_id=1, source_target_pairs={{0,1},{1,0},{2,3},{3,2},{4,5},{5,4},{6,7},{7,6},{8,9},{9,8},{10,11... | collective-permute-start | bytes 4718600 | tf_op jit(solution)/shard_map/ppermute | solution.py:793
  8.2 13.9 %copy-start.2 = (bf16[3,128,16,128]{3,2,1,0:T(8,128)(2,1)}, bf16[3,128,16,128]{3,2,1,0:T(8,128)(2,1)S(1)}, u32[]{:S(2)}) copy-start(bf16[3,128,16,128]{3,2,1,0:T(8,128)(2,1)S(1)} %collective-permute-done.h_ref.near_ref) | copy-start | bytes 4718596
  22.1 11.7 %collective-permute-start.1 = (bf16[3,128,16,128]{3,2,1,0:T(8,128)(2,1)}, bf16[3,128,16,128]{3,2,1,0:T(8,128)(2,1)}, u32[]{:S(2)}, u32[]{:S(2)}) collective-permute-start(bf16[3,128,16,128]{3,2,1,0:T(8,128)(2,1)} %get-tuple-element.19), channel_id=1, source_target_pairs={{0,1},{1,0},{2,3},{3,2},{4,5},{5,4},{6,7},{7,6},{8,9},{9,8},{10,11... | collective-permute-start | bytes 4718600 | tf_op jit(solution)/shard_map/ppermute | solution.py:793
  22.5 11.4 %copy-start.14 = (bf16[128,128]{1,0:T(8,128)(2,1)S(1)}, bf16[128,128]{1,0:T(8,128)(2,1)}, u32[]{:S(2)}) copy-start(bf16[128,128]{1,0:T(8,128)(2,1)} %constant.39.clone.dy_ref.dz_ref) | copy-start | bytes 98308
  22.5 11.4 %copy-start.15 = (bf16[64,96]{1,0:T(8,128)(2,1)S(1)}, bf16[64,96]{1,0:T(8,128)(2,1)}, u32[]{:S(2)}) copy-start(bf16[64,96]{1,0:T(8,128)(2,1)} %constant.40.clone.dx_ref) | copy-start | bytes 36868
  22.5 42.2 %all-to-all-start = ((s16[64,136,128]{2,1,0:T(8,128)(2,1)}), s16[64,136,128]{2,1,0:T(8,128)(2,1)S(1)}, u32[]{:S(2)}, u32[]{:S(2)}) async-start(s16[64,136,128]{2,1,0:T(8,128)(2,1)} %get-tuple-element.18), calls=%async_computation | async-start | bytes 4456448 | tf_op jit(solution)/shard_map/all_to_all | solution.py:801
  33.8 1.4 %copy-start.3 = (bf16[3,128,16,128]{3,2,1,0:T(8,128)(2,1)S(1)}, bf16[3,128,16,128]{3,2,1,0:T(8,128)(2,1)}, u32[]{:S(2)}) copy-start(bf16[3,128,16,128]{3,2,1,0:T(8,128)(2,1)} %copy-done.2) | copy-start | bytes 4718596
  53.7 15.2 %copy-start.7 = (f32[128,128]{1,0:T(8,128)S(1)}, f32[128,128]{1,0:T(8,128)}, u32[]{:S(2)}) copy-start(f32[128,128]{1,0:T(8,128)} %constant.42.clone.dht_ref) | copy-start | bytes 196612
  53.7 15.2 %copy-start.8 = (f32[128,128]{1,0:T(8,128)S(1)}, f32[128,128]{1,0:T(8,128)}, u32[]{:S(2)}) copy-start(f32[128,128]{1,0:T(8,128)} %constant.43.clone.curve_ref) | copy-start | bytes 196612
  53.7 15.2 %copy-start.13 = (f32[128]{0:T(128)S(1)}, f32[128]{0:T(128)}, u32[]{:S(2)}) copy-start(f32[128]{0:T(128)} %constant.41.clone.curve_z_ref) | copy-start | bytes 1540
  68.9 38.4 %copy-start.1 = (bf16[3,64,128,128]{3,2,1,0:T(8,128)(2,1)S(1)}, bf16[3,64,128,128]{3,2,1,0:T(8,128)(2,1)}, u32[]{:S(2)}) copy-start(bf16[3,64,128,128]{3,2,1,0:T(8,128)(2,1)} %get-tuple-element.22.psi_ref) | copy-start | bytes 18874372
  107.2 13.4 %copy-start.9 = (bf16[64,80]{1,0:T(8,128)(2,1)S(1)}, bf16[64,80]{1,0:T(8,128)(2,1)}, u32[]{:S(2)}) copy-start(bf16[64,80]{1,0:T(8,128)(2,1)} %constant.44.clone.tx_ref) | copy-start | bytes 30724
  115.8 4.8 %collective-permute-start.3 = (bf16[3,128,16,128]{3,2,1,0:T(8,128)(2,1)}, bf16[3,128,16,128]{3,2,1,0:T(8,128)(2,1)S(1)}, u32[]{:S(2)}, u32[]{:S(2)}) collective-permute-start(bf16[3,128,16,128]{3,2,1,0:T(8,128)(2,1)} %get-tuple-element.25), channel_id=1, source_target_pairs={{0,1},{1,0},{2,3},{3,2},{4,5},{5,4},{6,7},{7,6},{8,9},{9,8},{10,11... | collective-permute-start | bytes 4718600 | tf_op jit(solution)/shard_map/ppermute | solution.py:793
  117.3 2.9 %collective-permute-start.2 = (f32[3,16,128]{2,1,0:T(8,128)S(1)}, f32[3,16,128]{2,1,0:T(8,128)S(1)}, u32[]{:S(2)}, u32[]{:S(2)}) collective-permute-start(f32[3,16,128]{2,1,0:T(8,128)S(1)} %get-tuple-element.23.sums_ref), channel_id=1, source_target_pairs={{0,1},{1,0},{2,3},{3,2},{4,5},{5,4},{6,7},{7,6},{8,9},{9,8},{10,11... | collective-permute-start | bytes 73736 | tf_op jit(solution)/shard_map/ppermute | solution.py:793

commit v8 on v7

--- a/solution.py
+++ b/solution.py
@@ -160,35 +160,29 @@
     return dot(table, jnp.concatenate([high, high, low], axis=0))
 
 
-def rims_kernel(inner, outer, low_ref, high_ref, *rest):
-    out_ref, mark_ref = rest[-2:]
-    tile = low_ref.shape[2]
-    low = low_ref[...].astype(F32)[:, :, tile - outer : tile - inner]
-    high = high_ref[...].astype(F32)[:, :, inner:outer]
+def rims_kernel(low_ref, high_ref, out_ref):
+    half = low_ref.shape[2] // 2
+    low = low_ref[...].astype(F32)[:, :, half:]
+    high = high_ref[...].astype(F32)[:, :, :half]
     out_ref[...] = jnp.concatenate([low, high], axis=2).astype(BF16)
-    mark_ref[...] = jnp.zeros_like(mark_ref)
-
-
-def own_rims(c, inner, outer, *after):
+
+
+def own_rims(c):
     orbitals, length, cells_x, cells_y = c.shape
     tile = 16
 
     def at(k):
-        return pl.BlockSpec((orbitals, length, tile, cells_y), lambda o: (0, 0, k, 0))
+        return pl.BlockSpec((1, length, tile, cells_y), lambda o: (o, 0, k, 0))
 
     return pl.pallas_call(
-        functools.partial(rims_kernel, inner, outer),
-        grid=(1,),
-        in_specs=[at(cells_x // tile - 1), at(0)]
-        + [pl.BlockSpec(memory_space=pl.ANY) for _ in after],
-        out_specs=[at(0), pl.BlockSpec((8, cells_y), lambda o: (0, 0))],
-        out_shape=[
-            jax.ShapeDtypeStruct((orbitals, length, 2 * (outer - inner), cells_y), BF16),
-            jax.ShapeDtypeStruct((8, cells_y), F32),
-        ],
-        compiler_params=params(1, 16),
+        rims_kernel,
+        grid=(orbitals,),
+        in_specs=[at(cells_x // tile - 1), at(0)],
+        out_specs=at(0),
+        out_shape=jax.ShapeDtypeStruct((orbitals, length, tile, cells_y), BF16),
+        compiler_params=params(1, 8),
         name="own_rims",
-    )(c, c, *after)
+    )(c, c)
 
 
 def density_kernel(
@@ -495,7 +489,7 @@
         got_ref.shape[0],
         body,
         (jnp.zeros((rows, cells_y), F32), jnp.zeros((1, cells_y), F32)),
-        unroll=2,
+        unroll=8,
     )
     length = got_ref.shape[0] * per
     row = lax.broadcasted_iota(jnp.int32, (rows, cells_y), 0)
@@ -817,8 +811,7 @@
     waves = curve(length)
 
     c = in_hbm(coefficients)
-    own_near, _ = own_rims(c, 0, 8)
-    near = to_other(own_near)
+    near = to_other(own_rims(c))
     psi, coded, own_far, peak = density(
         occupations,
         slot_orbital,

time: 134 us -> 134 us (level)
  no operation moved by 1% of the time
where the time goes in v8:
time: 134 us
  Pallas kernels  60.1 us (45%)
  blocking collectives  39.4 us (29%)
  waiting for transfers between devices  16.7 us (12%)
  starting transfers between devices  14.8 us (11%)
  local copies, waits for them, and re-layouts  2.13 us (2%)
    all_to_all x1, blocking collectives, to_all(): lax.all_to_all(blocks, 'orb', split_axis=0, concat_axis=0, tiled=True)  36.1 us
    pallas_call x1, Pallas kernels, kinetic(): pl.pallas_call(functools.partial(kinetic_kernel, pitch), grid=(orbitals,)...  18.4 us
    pallas_call x1, Pallas kernels, density(): pl.pallas_call(functools.partial(density_kernel, first_steps, pitch), gri...  13.9 us
    pallas_call x1, Pallas kernels, update(): pl.pallas_call(update_kernel, grid=(orbitals, chunks), in_specs=[whole(su...  12.7 us
    all_to_all x1, starting transfers between devices, to_all(): lax.all_to_all(blocks, 'orb', split_axis=0, concat_axis=0, tiled=True)  11.3 us
    all_to_all x1, waiting for transfers between devices, to_all(): lax.all_to_all(blocks, 'orb', split_axis=0, concat_axis=0, tiled=True)  11.1 us
    pallas_call x1, Pallas kernels, field(): pl.pallas_call(functools.partial(field_kernel, pitch, turn_pitch), grid=(...  8.55 us
    ppermute x4, waiting for transfers between devices, to_other(): return lax.ppermute(array, 'grid', [(0, 1), (1, 0)])  5.65 us
  transfers between devices with their start and end apart: 5, of which 4 were waited for; matrix products, arithmetic and copies ran while one was open for 0% of the time, Pallas kernels for 14%

profile of v8, /device:TPU:1, one launch (start us, length us, event | category | flops | bytes accessed | tf_op | source)
XLA Modules:
  0.0 133.9 jit_solution(2495265030842067350)
XLA Ops:
  0.6 0.0 copy-start.4
  0.6 0.0 copy-start.5
  0.7 0.0 copy-start.6
  0.7 0.0 copy-start.10
  0.7 0.0 copy-start.11
  0.7 0.0 copy-start
  0.7 0.0 copy-start.12
  0.7 3.6 %own_rims.1 = bf16[3,128,16,128]{3,2,1,0:T(8,128)(2,1)S(1)} custom-call(bf16[3,128,64,128]{3,2,1,0:T(8,128)(2,1)} %c_ref.5, bf16[3,128,64,128]{3,2,1,0:T(8,128)(2,1)} %c_ref.5), custom_call_target="tpu_custom_call" | custom-call | tf_op jit(solution)/shard_map/own_rims/pallas_call | solution.py:177
  4.3 1.5 %collective-permute-start = (bf16[3,128,16,128]{3,2,1,0:T(8,128)(2,1)S(1)}, bf16[3,128,16,128]{3,2,1,0:T(8,128)(2,1)S(1)}, u32[]{:S(2)}, u32[]{:S(2)}) collective-permute-start(bf16[3,128,16,128]{3,2,1,0:T(8,128)(2,1)S(1)} %own_rims.1), channel_id=1, source_target_pairs={{0,1},{1,0},{2,3},{3,2},{4,5},{5,4},{6,7},{7,6},{8,9},{9,8},{10,11... | collective-permute-start | bytes 4718600 | tf_op jit(solution)/shard_map/ppermute | solution.py:787
  5.8 3.0 %collective-permute-done.h_ref.near_ref = bf16[3,128,16,128]{3,2,1,0:T(8,128)(2,1)S(1)} collective-permute-done((bf16[3,128,16,128]{3,2,1,0:T(8,128)(2,1)S(1)}, bf16[3,128,16,128]{3,2,1,0:T(8,128)(2,1)S(1)}, u32[]{:S(2)}, u32[]{:S(2)}) %collective-permute-start) | collective-permute-done | bytes 1572896 | tf_op jit(solution)/shard_map/ppermute | solution.py:787
  8.9 0.0 copy-done.4
  8.9 0.0 copy-done.5
  8.9 0.0 copy-done.6
  8.9 0.0 copy-done.10
  8.9 0.0 copy-done.11
  8.9 0.0 copy-done
  8.9 0.0 copy-done.12
  8.9 0.0 copy-start.2
  8.9 13.9 %density.1 = (bf16[3,64,128,128]{3,2,1,0:T(8,128)(2,1)}, s16[64,136,128]{2,1,0:T(8,128)(2,1)}, bf16[3,128,16,128]{3,2,1,0:T(8,128)(2,1)}, f32[8,128]{1,0:T(8,128)S(1)}) custom-call(s32[192]{0:T(256)S(1)} %copy-done.11, s32[192]{0:T(256)S(1)} %copy-done.12, bf16[3,128,64,128]{3,2,1,0:T(8,128)(2,1)S(1)} %copy-done, ...), custom_call_target="tpu_custom_call" | custom-call | tf_op jit(solution)/shard_map/density/pallas_call | solution.py:320
  22.8 0.0 copy-done.2
  22.8 0.4 collective-permute-start.1
  23.2 0.0 copy-start.15
  23.2 11.3 %all-to-all-start = ((s16[64,136,128]{2,1,0:T(8,128)(2,1)}), s16[64,136,128]{2,1,0:T(8,128)(2,1)S(1)}, u32[]{:S(2)}, u32[]{:S(2)}) async-start(s16[64,136,128]{2,1,0:T(8,128)(2,1)} %get-tuple-element.16), calls=%async_computation | async-start | bytes 4456448 | tf_op jit(solution)/shard_map/all_to_all | solution.py:795
  34.6 0.0 collective-permute-done.1.far_ref
  34.6 0.0 copy-done.14
  34.6 0.0 copy-done.15
  34.6 0.0 copy-start.3
  34.6 1.4 %copy-done.3 = bf16[3,128,16,128]{3,2,1,0:T(8,128)(2,1)S(1)} copy-done((bf16[3,128,16,128]{3,2,1,0:T(8,128)(2,1)S(1)}, bf16[3,128,16,128]{3,2,1,0:T(8,128)(2,1)}, u32[]{:S(2)}) %copy-start.3) | copy-done | bytes 1572888
  36.0 18.4 %kinetic.1 = (s16[3,128,64,128]{3,2,1,0:T(8,128)(2,1)}, f32[3,128,128]{2,1,0:T(8,128)S(1)}, f32[3,16,128]{2,1,0:T(8,128)S(1)}) custom-call(bf16[3,128,64,128]{3,2,1,0:T(8,128)(2,1)} %c_ref.5, bf16[3,128,16,128]{3,2,1,0:T(8,128)(2,1)S(1)} %copy-done.3, bf16[3,128,16,128]{3,2,1,0:T(8,128)(2,1)} %collective-permute-done.1.far_ref, ...), custom_call_target="tpu_custom_call" | custom-call | flops 9663676416 | bytes 22020096 | tf_op jit(solution)/shard_map/kinetic/pallas_call | solution.py:436
  54.4 0.0 copy-start.7
  54.4 0.0 copy-start.8
  54.4 11.1 %all-to-all-done.got_ref = s16[64,136,128]{2,1,0:T(8,128)(2,1)S(1)} async-done(((s16[64,136,128]{2,1,0:T(8,128)(2,1)}), s16[64,136,128]{2,1,0:T(8,128)(2,1)S(1)}, u32[]{:S(2)}, u32[]{:S(2)}) %all-to-all-start) | async-done | bytes 2228256 | tf_op jit(solution)/shard_map/all_to_all | solution.py:795
  65.5 0.7 slab_sum.1
  66.2 3.3 %all_gather.3.slab_ref = f32[2,128,128]{2,1,0:T(8,128)S(1)} all-gather(f32[2,64,128]{2,1,0:T(8,128)S(1)} %bitcast.3), channel_id=1, replica_groups=mesh['orb'=64,'grid'=2] {'grid'}, dimensions={1}, use_global_device_ids=true | all-gather | bytes 196608 | tf_op jit(solution)/shard_map/all_gather | solution.py:838
  69.4 0.0 copy-done.7
  69.4 0.0 copy-done.8
  69.4 0.0 copy-done.13
  69.5 2.2 %solve.1 = s16[64,136,128]{2,1,0:T(8,128)(2,1)S(1)} custom-call(f32[128]{0:T(128)S(1)} %copy-done.13, f32[2,128,128]{2,1,0:T(8,128)S(1)} %all_gather.3.slab_ref, f32[128,128]{1,0:T(8,128)S(1)} %copy-done.7, f32[128,128]{1,0:T(8,128)S(1)} %copy-done.8), custom_call_target="tpu_custom_call" | custom-call | tf_op jit(solution)/shard_map/solve/pallas_call | solution.py:552
  71.7 36.1 %all_to_all.10.got_ref = s16[64,136,128]{2,1,0:T(8,128)(2,1)S(1)} all-to-all(s16[64,136,128]{2,1,0:T(8,128)(2,1)S(1)} %solve.1), channel_id=1, replica_groups=mesh['orb'=64,'grid'=2] {'orb'}, dimensions={0} | all-to-all | bytes 4456448 | tf_op jit(solution)/shard_map/all_to_all | solution.py:795
  107.8 0.0 copy-done.1
  107.8 8.6 %field.1 = (bf16[3,128,64,128]{3,2,1,0:T(8,128)(2,1)}, bf16[3,128,16,128]{3,2,1,0:T(8,128)(2,1)}, f32[64,8,128]{2,1,0:T(8,128)S(1)}, f32[3,16,128]{2,1,0:T(8,128)S(1)}) custom-call(s16[64,136,128]{2,1,0:T(8,128)(2,1)S(1)} %all_to_all.10.got_ref, bf16[3,64,128,128]{3,2,1,0:T(8,128)(2,1)S(1)} %copy-done.1, ...), custom_call_target="tpu_custom_call" | custom-call | tf_op jit(solution)/shard_map/field/pallas_call | solution.py:670
  116.4 1.5 %collective-permute-start.3 = (bf16[3,128,16,128]{3,2,1,0:T(8,128)(2,1)}, bf16[3,128,16,128]{3,2,1,0:T(8,128)(2,1)S(1)}, u32[]{:S(2)}, u32[]{:S(2)}) collective-permute-start(bf16[3,128,16,128]{3,2,1,0:T(8,128)(2,1)} %get-tuple-element.23), channel_id=1, source_target_pairs={{0,1},{1,0},{2,3},{3,2},{4,5},{5,4},{6,7},{7,6},{8,9},{9,8},{10,11... | collective-permute-start | bytes 4718600 | tf_op jit(solution)/shard_map/ppermute | solution.py:787
  117.9 0.0 collective-permute-start.2
  117.9 0.6 copy.19
  118.6 2.3 %collective-permute-done.2.other_ref = f32[3,16,128]{2,1,0:T(8,128)S(1)} collective-permute-done((f32[3,16,128]{2,1,0:T(8,128)S(1)}, f32[3,16,128]{2,1,0:T(8,128)S(1)}, u32[]{:S(2)}, u32[]{:S(2)}) %collective-permute-start.2) | collective-permute-done | bytes 24608 | tf_op jit(solution)/shard_map/ppermute | solution.py:787
  120.8 0.3 collective-permute-done.3.rim_ref
  121.2 0.0 copy-done.9
  121.2 12.7 %update.1 = (bf16[3,128,64,128]{3,2,1,0:T(8,128)(2,1)}, f32[3]{0:T(128)}) custom-call(f32[3,16,128]{2,1,0:T(8,128)S(1)} %get-tuple-element.21.sums_ref, f32[3,16,128]{2,1,0:T(8,128)S(1)} %collective-permute-done.2.other_ref, bf16[3,128,64,128]{3,2,1,0:T(8,128)(2,1)} %get-tuple-element.22.back_ref, ...), custom_call_target="tpu_custom_call" | custom-call | tf_op jit(solution)/shard_map/update/pallas_call | solution.py:762
  (5 shorter events, 0.0 us)
Async XLA Ops:
  0.6 8.3 %copy-start.4 = (bf16[128,384]{1,0:T(8,128)(2,1)S(1)}, bf16[128,384]{1,0:T(8,128)(2,1)}, u32[]{:S(2)}) copy-start(bf16[128,384]{1,0:T(8,128)(2,1)} %constant.35.clone.dht_ref) | copy-start | bytes 294916
  0.6 8.2 %copy-start.5 = (bf16[128,128]{1,0:T(8,128)(2,1)S(1)}, bf16[128,128]{1,0:T(8,128)(2,1)}, u32[]{:S(2)}) copy-start(bf16[128,128]{1,0:T(8,128)(2,1)} %constant.38.clone.mz_ref.ty_ref) | copy-start | bytes 98308
  0.7 8.2 %copy-start.6 = (bf16[128,128]{1,0:T(8,128)(2,1)S(1)}, bf16[128,128]{1,0:T(8,128)(2,1)}, u32[]{:S(2)}) copy-start(bf16[128,128]{1,0:T(8,128)(2,1)} %constant.36.clone.my_ref.tz_ref) | copy-start | bytes 98308
  0.7 8.2 %copy-start.10 = (bf16[64,80]{1,0:T(8,128)(2,1)S(1)}, bf16[64,80]{1,0:T(8,128)(2,1)}, u32[]{:S(2)}) copy-start(bf16[64,80]{1,0:T(8,128)(2,1)} %constant.37.clone.ax_ref) | copy-start | bytes 30724
  0.7 8.2 %copy-start.11 = (s32[192]{0:T(256)S(1)}, s32[192]{0:T(256)}, u32[]{:S(2)}) copy-start(s32[192]{0:T(256)} %occ_ref.1) | copy-start | bytes 2308
  0.7 8.2 %copy-start = (bf16[3,128,64,128]{3,2,1,0:T(8,128)(2,1)S(1)}, bf16[3,128,64,128]{3,2,1,0:T(8,128)(2,1)}, u32[]{:S(2)}) copy-start(bf16[3,128,64,128]{3,2,1,0:T(8,128)(2,1)} %c_ref.5) | copy-start | bytes 18874372
  0.7 8.2 %copy-start.12 = (s32[192]{0:T(256)S(1)}, s32[192]{0:T(256)}, u32[]{:S(2)}) copy-start(s32[192]{0:T(256)} %slot_ref.1) | copy-start | bytes 2308
  4.3 4.5 %collective-permute-start = (bf16[3,128,16,128]{3,2,1,0:T(8,128)(2,1)S(1)}, bf16[3,128,16,128]{3,2,1,0:T(8,128)(2,1)S(1)}, u32[]{:S(2)}, u32[]{:S(2)}) collective-permute-start(bf16[3,128,16,128]{3,2,1,0:T(8,128)(2,1)S(1)} %own_rims.1), channel_id=1, source_target_pairs={{0,1},{1,0},{2,3},{3,2},{4,5},{5,4},{6,7},{7,6},{8,9},{9,8},{10,11... | collective-permute-start | bytes 4718600 | tf_op jit(solution)/shard_map/ppermute | solution.py:787
  8.9 13.9 %copy-start.2 = (bf16[3,128,16,128]{3,2,1,0:T(8,128)(2,1)}, bf16[3,128,16,128]{3,2,1,0:T(8,128)(2,1)S(1)}, u32[]{:S(2)}) copy-start(bf16[3,128,16,128]{3,2,1,0:T(8,128)(2,1)S(1)} %collective-permute-done.h_ref.near_ref) | copy-start | bytes 4718596
  22.8 11.7 %collective-permute-start.1 = (bf16[3,128,16,128]{3,2,1,0:T(8,128)(2,1)}, bf16[3,128,16,128]{3,2,1,0:T(8,128)(2,1)}, u32[]{:S(2)}, u32[]{:S(2)}) collective-permute-start(bf16[3,128,16,128]{3,2,1,0:T(8,128)(2,1)} %get-tuple-element.17), channel_id=1, source_target_pairs={{0,1},{1,0},{2,3},{3,2},{4,5},{5,4},{6,7},{7,6},{8,9},{9,8},{10,11... | collective-permute-start | bytes 4718600 | tf_op jit(solution)/shard_map/ppermute | solution.py:787
  23.2 11.4 %copy-start.14 = (bf16[128,128]{1,0:T(8,128)(2,1)S(1)}, bf16[128,128]{1,0:T(8,128)(2,1)}, u32[]{:S(2)}) copy-start(bf16[128,128]{1,0:T(8,128)(2,1)} %constant.39.clone.dy_ref.dz_ref) | copy-start | bytes 98308
  23.2 11.4 %copy-start.15 = (bf16[64,96]{1,0:T(8,128)(2,1)S(1)}, bf16[64,96]{1,0:T(8,128)(2,1)}, u32[]{:S(2)}) copy-start(bf16[64,96]{1,0:T(8,128)(2,1)} %constant.40.clone.dx_ref) | copy-start | bytes 36868
  23.2 42.2 %all-to-all-start = ((s16[64,136,128]{2,1,0:T(8,128)(2,1)}), s16[64,136,128]{2,1,0:T(8,128)(2,1)S(1)}, u32[]{:S(2)}, u32[]{:S(2)}) async-start(s16[64,136,128]{2,1,0:T(8,128)(2,1)} %get-tuple-element.16), calls=%async_computation | async-start | bytes 4456448 | tf_op jit(solution)/shard_map/all_to_all | solution.py:795
  34.6 1.4 %copy-start.3 = (bf16[3,128,16,128]{3,2,1,0:T(8,128)(2,1)S(1)}, bf16[3,128,16,128]{3,2,1,0:T(8,128)(2,1)}, u32[]{:S(2)}) copy-start(bf16[3,128,16,128]{3,2,1,0:T(8,128)(2,1)} %copy-done.2) | copy-start | bytes 4718596
  54.4 15.0 %copy-start.7 = (f32[128,128]{1,0:T(8,128)S(1)}, f32[128,128]{1,0:T(8,128)}, u32[]{:S(2)}) copy-start(f32[128,128]{1,0:T(8,128)} %constant.42.clone.dht_ref) | copy-start | bytes 196612
  54.4 15.0 %copy-start.8 = (f32[128,128]{1,0:T(8,128)S(1)}, f32[128,128]{1,0:T(8,128)}, u32[]{:S(2)}) copy-start(f32[128,128]{1,0:T(8,128)} %constant.43.clone.curve_ref) | copy-start | bytes 196612
  54.4 15.0 %copy-start.13 = (f32[128]{0:T(128)S(1)}, f32[128]{0:T(128)}, u32[]{:S(2)}) copy-start(f32[128]{0:T(128)} %constant.41.clone.curve_z_ref) | copy-start | bytes 1540
  69.4 38.4 %copy-start.1 = (bf16[3,64,128,128]{3,2,1,0:T(8,128)(2,1)S(1)}, bf16[3,64,128,128]{3,2,1,0:T(8,128)(2,1)}, u32[]{:S(2)}) copy-start(bf16[3,64,128,128]{3,2,1,0:T(8,128)(2,1)} %get-tuple-element.20.psi_ref) | copy-start | bytes 18874372
  107.8 13.4 %copy-start.9 = (bf16[64,80]{1,0:T(8,128)(2,1)S(1)}, bf16[64,80]{1,0:T(8,128)(2,1)}, u32[]{:S(2)}) copy-start(bf16[64,80]{1,0:T(8,128)(2,1)} %constant.44.clone.tx_ref) | copy-start | bytes 30724
  116.4 4.8 %collective-permute-start.3 = (bf16[3,128,16,128]{3,2,1,0:T(8,128)(2,1)}, bf16[3,128,16,128]{3,2,1,0:T(8,128)(2,1)S(1)}, u32[]{:S(2)}, u32[]{:S(2)}) collective-permute-start(bf16[3,128,16,128]{3,2,1,0:T(8,128)(2,1)} %get-tuple-element.23), channel_id=1, source_target_pairs={{0,1},{1,0},{2,3},{3,2},{4,5},{5,4},{6,7},{7,6},{8,9},{9,8},{10,11... | collective-permute-start | bytes 4718600 | tf_op jit(solution)/shard_map/ppermute | solution.py:787
  117.9 2.9 %collective-permute-start.2 = (f32[3,16,128]{2,1,0:T(8,128)S(1)}, f32[3,16,128]{2,1,0:T(8,128)S(1)}, u32[]{:S(2)}, u32[]{:S(2)}) collective-permute-start(f32[3,16,128]{2,1,0:T(8,128)S(1)} %get-tuple-element.21.sums_ref), channel_id=1, source_target_pairs={{0,1},{1,0},{2,3},{3,2},{4,5},{5,4},{6,7},{7,6},{8,9},{9,8},{10,11... | collective-permute-start | bytes 73736 | tf_op jit(solution)/shard_map/ppermute | solution.py:787
